TPU v7x, 256 devices: a whole 4x4x8 slice. The times are simulated.
256 devices in a mesh: grp: 32 (over z, x), sub: 8 (over y, core).
Axes of the slice: x: 4, y: 4, z: 8, core: 2. Of those that a mesh axis runs over, the one named last changes fastest.
Arguments:
- resid3: float32 [6, 32, 32768], P(None, None, ('grp', 'sub')), may hold values from -6 to 6
- diag3: float32 [6, 6, 32768], P(None, None, ('grp', 'sub')), may hold values from -0.25 to 4.25
- smooth3: float32 [6, 6, 32768], P(None, None, ('grp', 'sub')), may hold values from -0.09 to 0.79
- off3: float32 [26, 6, 6, 32768], P(None, None, None, ('grp', 'sub')), may hold values from -0.18 to 0.18
- cols3: int32 [26, 32768], P(None, ('grp', 'sub')), may hold values from 0 to 159
- send3: int32 [2, 4096], P(None, ('grp', 'sub')), may hold values from 0 to 127
- prolong3: float32 [6, 6, 32768], P(None, None, ('grp', 'sub')), may hold values from -0.4375 to 0.4375
- agg3: int32 [32768], P(('grp', 'sub')), may hold values from 0 to 31
- diag4: float32 [6, 6, 1024], P(None, None, 'grp'), may hold values from -0.25 to 4.25
- smooth4: float32 [6, 6, 1024], P(None, None, 'grp'), may hold values from -0.09 to 0.79
- off4: float32 [26, 6, 6, 1024], P(None, None, None, 'grp'), may hold values from -0.18 to 0.18
- cols4: int32 [26, 1024], P(None, 'grp'), may hold values from 0 to 47
- send4: int32 [2, 256], P(None, 'grp'), may hold values from 0 to 31
- prolong4: float32 [6, 6, 1024], P(None, None, 'grp'), may hold values from -2.5 to 2.5
- agg4: int32 [1024], P('grp'), may hold values from 0 to 1279, as said below
- coarse_factor: float32 [7680, 7680], P(('grp', 'sub')), may hold values from -1 to 4, as said below
Outputs:
- result: float32 [6, 32, 32768], P(None, None, ('grp', 'sub'))
- correction: float32 [6, 32, 1024], P(None, None, 'grp')
Inputs may be any that keep to these rules, and one draw needn't show every extreme that they name: `cols3`: column indices below 128 name the device's own block rows, the next 16 the rows received from the lower neighbour, the last 16 those from the upper one. `send3`: row 0 lists own block rows for the lower neighbour, row 1 for the upper one. `cols4`: as cols3, per group, with 32 own rows and 8 rows from each neighbouring group. `send4`: row 0 for the lower group, row 1 for the upper one. `agg4`: A level-4 row of group g names a coarsest row of its own group, g * 40 to g * 40 + 39; in every group the first and the last of these are named. `coarse_factor`: G is lower triangular.
All inputs are finite; a program needn't handle non-finite values.
Results may differ from a plain program's by a relative error of at most 0.000076.
Values sent between devices are 32-bit elements; how exact they have to be, the bound alone decides.
No kernel may reach another device: no remote copies, remote signals or barrier semaphores. Data moves between devices by JAX's collectives and lax.ppermute only.
A program may use at most 64 MiB of HBM per device.

v0:
```python
import jax
import jax.numpy as jnp
from jax import lax
from jax.sharding import PartitionSpec as P


def with_halo(shard, sides, width):
    for axis, dim in sides:
        devices, length = (lax.axis_size(axis), shard.shape[dim])
        up = [(i, (i + 1) % devices) for i in range(devices - 1)]
        down = [(j, i) for i, j in up]
        last = lax.slice_in_dim(shard, length - width, length, axis=dim)
        initial = lax.slice_in_dim(shard, 0, width, axis=dim)
        before = lax.ppermute(last, axis, up)
        after = lax.ppermute(initial, axis, down)
        shard = jnp.concatenate([before, shard, after], axis=dim)
    return shard


def blockmul(blocks, vector):
    return jnp.sum(blocks[:, :, None, :] * vector[None], axis=1)


def transposed(blocks):
    return jnp.transpose(blocks, (1, 0, 2))


def row_blocks(offdiag):
    count = offdiag.shape[0]
    return jnp.transpose(offdiag, (3, 1, 0, 2)).reshape(offdiag.shape[3], 6, count * 6)


def stencil(extended, own_rows, diagonal, offdiagonal_rows, column_list):
    sides = extended.shape[1]
    own_count = own_rows.shape[2]
    count = column_list.shape[0]
    rows_first = jnp.transpose(extended.reshape(6 * sides, extended.shape[2]))
    selected_entries = jnp.take(rows_first, jnp.transpose(column_list).reshape(-1), axis=0)
    selected_entries = selected_entries.reshape(own_count, count * 6, sides)
    accumulated_sum = jnp.einsum(
        "oae,oeb->oab", offdiagonal_rows, selected_entries, precision=lax.Precision.HIGHEST
    )
    return blockmul(diagonal, own_rows) + jnp.transpose(accumulated_sum, (1, 2, 0))


def fine_apply(vector, diagonal, offdiagonal_rows, column_list, sends):
    packed = jnp.stack([jnp.take(vector, sends[0], axis=2), jnp.take(vector, sends[1], axis=2)])
    padded = with_halo(packed, ((("grp", "sub"), 0),), 1)
    extended = jnp.concatenate([vector, padded[0], padded[3]], axis=2)
    return stencil(extended, vector, diagonal, offdiagonal_rows, column_list)


def coarse_apply(whole_field, own_rows, diagonal, offdiagonal_rows, column_list, sends):
    packed = jnp.stack(
        [jnp.take(whole_field, sends[0], axis=2), jnp.take(whole_field, sends[1], axis=2)]
    )
    padded = with_halo(packed, (("grp", 0),), 1)
    extended = jnp.concatenate([whole_field, padded[0], padded[3]], axis=2)
    return stencil(extended, own_rows, diagonal, offdiagonal_rows, column_list)


def summed_rows(vector, blocks, aggregates, segments):
    restricted = blockmul(transposed(blocks), vector)
    picker = (aggregates[:, None] == jnp.arange(segments, dtype=jnp.int32)[None, :]).astype(
        jnp.float32
    )
    flat = restricted.reshape(-1, restricted.shape[2])
    return jnp.dot(flat, picker, precision=lax.Precision.HIGHEST).reshape(
        6, vector.shape[1], segments
    )


def on_device(
    resid3,
    diag3,
    smooth3,
    off3,
    cols3,
    send3,
    prolong3,
    agg3,
    diag4,
    smooth4,
    off4,
    cols4,
    send4,
    prolong4,
    agg4,
    coarse_factor,
):
    level_rows = diag4.shape[2]
    coarse_rows = coarse_factor.shape[1] // 6
    factor = coarse_factor.reshape(coarse_factor.shape[0], 6, coarse_rows)
    fine_blocks = row_blocks(off3)
    smoothed_once = blockmul(smooth3, resid3)
    smoothed_twice = smoothed_once + blockmul(
        smooth3, resid3 - fine_apply(smoothed_once, diag3, fine_blocks, cols3, send3)
    )
    fine_left = resid3 - fine_apply(smoothed_twice, diag3, fine_blocks, cols3, send3)
    partial_four = summed_rows(fine_left, prolong3, agg3, level_rows)
    four_blocks = row_blocks(off4)
    rhs_four = lax.psum(partial_four, "sub")
    start_four = blockmul(smooth4, rhs_four)
    left_four_blocks = rhs_four - coarse_apply(
        start_four, start_four, diag4, four_blocks, cols4, send4
    )
    coarse_rhs = lax.psum(summed_rows(left_four_blocks, prolong4, agg4, coarse_rows), "grp")
    projected = jnp.einsum("mic,irc->mr", factor, coarse_rhs, precision=lax.Precision.HIGHEST)
    partial_sum = jnp.einsum("mic,mr->irc", factor, projected, precision=lax.Precision.HIGHEST)
    solved = lax.psum(partial_sum, ("grp", "sub"))
    mid_four = start_four + blockmul(prolong4, jnp.take(solved, agg4 - 0, axis=2))
    correction = mid_four + blockmul(
        smooth4, rhs_four - coarse_apply(mid_four, mid_four, diag4, four_blocks, cols4, send4)
    )
    fine_correction = smoothed_twice + blockmul(prolong3, jnp.take(correction, agg3, axis=2))
    result = fine_correction + blockmul(
        smooth3, resid3 - fine_apply(fine_correction, diag3, fine_blocks, cols3, send3)
    )
    return (result, correction)


def solution(mesh):
    return jax.shard_map(
        on_device,
        mesh=mesh,
        in_specs=(
            P(None, None, ("grp", "sub")),
            P(None, None, ("grp", "sub")),
            P(None, None, ("grp", "sub")),
            P(None, None, None, ("grp", "sub")),
            P(None, ("grp", "sub")),
            P(None, ("grp", "sub")),
            P(None, None, ("grp", "sub")),
            P(("grp", "sub")),
            P(None, None, "grp"),
            P(None, None, "grp"),
            P(None, None, None, "grp"),
            P(None, "grp"),
            P(None, "grp"),
            P(None, None, "grp"),
            P("grp"),
            P(("grp", "sub"), None),
        ),
        out_specs=(P(None, None, ("grp", "sub")), P(None, None, "grp")),
        check_vma=False,
    )
```

profile of v0, /device:TPU:32, one launch (start us, length us, event | category | flops | bytes accessed | tf_op | source)
XLA Modules:
  0.0 664.0 jit_solution(9216924733061063575)
XLA Ops:
  7.2 1.0 multiply_reduce_fusion.13
  10.6 1.9 collective-permute-start
  13.8 7.8 %collective-permute-start.1 = (f32[1,6,32,16]{2,1,3,0:T(8,128)}, f32[1,6,32,16]{2,1,3,0:T(8,128)S(1)}, u32[]{:S(2)}, u32[]{:S(2)}) collective-permute-start(f32[1,6,32,16]{2,1,3,0:T(8,128)} %select_bitcast_fusion.6), channel_id=1, source_target_pairs={{1,0},{2,1},{3,2},{4,3},{5,4},{6,5},{7,6},{8,7},{9,8},{10,9},{11,1... | collective-permute-start | bytes 36872 | tf_op jit(solution)/shard_map/ppermute | solution.py:15
  24.4 1.4 compare_and_fusion.3
  27.0 1.4 copy.137
  30.7 1.4 copy.158
  32.8 8.9 %gather_fusion.4 = f32[3328,192]{1,0:T(8,128)} fusion(f32[160,192]{1,0:T(8,128)S(1)} %maximum_bitcast_fusion.2, s32[4096]{0:T(1024)S(1)} %pad_clamp_fusion), kind=kCustom, calls=%fused_computation.1.clone | custom fusion | bytes 5125120 | tf_op jit(solution)/shard_map/jit(_take)/gather | solution.py:38
  41.7 4.4 broadcast_select_fusion.2
  46.1 8.3 %reshape.155 = f32[128,156,32]{2,1,0:T(8,128)} reshape(f32[3328,192]{1,0:T(8,128)} %broadcast_select_fusion.2) | data formatting | bytes 5111808 | tf_op jit(solution)/shard_map/reshape | solution.py:39
  54.5 11.4 %fusion.16 = f32[128,32,6]{1,2,0:T(8,128)S(1)} fusion(f32[128,156,32]{2,1,0:T(8,128)} %reshape.155, f32[128,6,156]{2,1,0:T(8,128)S(1)} %copy.139), kind=kOutput, calls=%fused_computation.101 | convolution fusion | flops 46006272 | bytes 3133440 | tf_op jit(solution)/shard_map/oae,oeb->oab/dot_general | solution.py:40
  68.1 1.9 collective-permute-start.2
  70.1 8.2 %collective-permute-start.3 = (f32[1,6,32,16]{2,1,3,0:T(8,128)S(1)}, f32[1,6,32,16]{2,1,3,0:T(8,128)S(1)}, u32[]{:S(2)}, u32[]{:S(2)}) collective-permute-start(f32[1,6,32,16]{2,1,3,0:T(8,128)S(1)} %select_bitcast_fusion.4), channel_id=1, source_target_pairs={{1,0},{2,1},{3,2},{4,3},{5,4},{6,5},{7,6},{8,7},{9,8},{10,9},{11,1... | collective-permute-start | bytes 36872 | tf_op jit(solution)/shard_map/ppermute | solution.py:15
  78.4 1.4 collective-permute-done.3
  80.1 8.9 %gather_fusion.7 = f32[3328,192]{1,0:T(8,128)} fusion(f32[160,192]{1,0:T(8,128)S(1)} %copy.147, s32[4096]{0:T(1024)S(1)} %pad_clamp_fusion), kind=kCustom, calls=%fused_computation.9.clone | custom fusion | bytes 5125120 | tf_op jit(solution)/shard_map/jit(_take)/gather | solution.py:38
  89.0 4.4 broadcast_select_fusion.1
  93.4 8.3 %reshape.157 = f32[128,156,32]{2,1,0:T(8,128)} reshape(f32[3328,192]{1,0:T(8,128)} %broadcast_select_fusion.1) | data formatting | bytes 5111808 | tf_op jit(solution)/shard_map/reshape | solution.py:39
  101.8 11.4 %fusion.17 = f32[128,32,6]{1,2,0:T(8,128)S(1)} fusion(f32[128,156,32]{2,1,0:T(8,128)} %reshape.157, f32[128,6,156]{2,1,0:T(8,128)S(1)} %copy.139), kind=kOutput, calls=%fused_computation.102 | convolution fusion | flops 46006272 | bytes 3133440 | tf_op jit(solution)/shard_map/oae,oeb->oab/dot_general | solution.py:40
  113.7 24.4 %psum.21 = f32[6,32,32]{2,1,0:T(8,128)S(1)} all-reduce(f32[6,32,32]{2,1,0:T(8,128)S(1)} %fusion.13), channel_id=1, replica_groups=mesh['grp'=32,'sub'=8] {'sub'}, use_global_device_ids=true, to_apply=%region_5.8 | all-reduce | flops 6144 | bytes 49152 | tf_op jit(solution)/shard_map/psum | solution.py:102
  139.0 3.0 collective-permute-start.4
  142.8 7.8 %collective-permute-start.5 = (f32[1,6,32,8]{2,1,3,0:T(8,128)S(1)}, f32[1,6,32,8]{2,1,3,0:T(8,128)S(1)}, u32[]{:S(2)}, u32[]{:S(2)}) collective-permute-start(f32[1,6,32,8]{2,1,3,0:T(8,128)S(1)} %select_bitcast_fusion.10), channel_id=1, source_target_pairs={{8,0},{16,8},{24,16},{32,24},{40,32},{48,40},{56,48},{64,56},{72,6... | collective-permute-start | bytes 18440 | tf_op jit(solution)/shard_map/ppermute | solution.py:15
  151.8 2.7 gather_fusion.10
  154.5 1.1 broadcast_select_fusion.4
  155.6 3.2 reshape.159
  158.7 4.0 fusion.18
  163.0 1.6 fusion.4
  164.7 1.5 reshape.161
  167.4 1.2 compare_select_fusion.7
  168.6 148.4 %all-reduce.3.cloned.1.call-done = f32[6,32,1280]{2,1,0:T(8,128)} async-done(((f32[6,32,1280]{2,1,0:T(8,128)}), f32[6,32,1280]{2,1,0:T(8,128)}) %all-reduce.3.cloned.1.call-update) | async-done | bytes 983056 | tf_op jit(solution)/shard_map/psum | solution.py:107
  317.0 2.3 fusion.1
  319.3 2.1 convolution_bitcast_fusion
  321.5 1.2 pad_clamp_fusion.1
  323.3 1.2 compare_and_fusion.7
  324.5 249.9 %all-reduce.5.cloned.1.call-done = f32[6,32,1280]{2,1,0:T(8,128)} async-done(((f32[6,32,1280]{2,1,0:T(8,128)}), f32[6,32,1280]{2,1,0:T(8,128)}) %all-reduce.5.cloned.1.call-update) | async-done | bytes 983056 | tf_op jit(solution)/shard_map/psum | solution.py:110
  574.4 4.1 copy.162
  578.5 3.2 gather_fusion
  583.7 3.3 collective-permute-start.6
  587.1 5.8 collective-permute-start.7
  593.2 1.2 collective-permute-done.7
  594.4 2.7 gather_fusion.13
  597.1 1.1 broadcast_select_fusion.3
  598.2 3.2 reshape.162
  601.4 4.0 fusion.19
  610.5 1.9 collective-permute-start.8
  612.5 8.1 %collective-permute-start.9 = (f32[1,6,32,16]{2,1,3,0:T(8,128)S(1)}, f32[1,6,32,16]{2,1,3,0:T(8,128)S(1)}, u32[]{:S(2)}, u32[]{:S(2)}) collective-permute-start(f32[1,6,32,16]{2,1,3,0:T(8,128)S(1)} %select_bitcast_fusion.2), channel_id=1, source_target_pairs={{1,0},{2,1},{3,2},{4,3},{5,4},{6,5},{7,6},{8,7},{9,8},{10,9},{11,1... | collective-permute-start | bytes 36872 | tf_op jit(solution)/shard_map/ppermute | solution.py:15
  622.6 8.9 %gather_fusion.16 = f32[3328,192]{1,0:T(8,128)} fusion(f32[160,192]{1,0:T(8,128)S(1)} %copy.177, s32[4096]{0:T(1024)S(1)} %pad_clamp_fusion), kind=kCustom, calls=%fused_computation.10.clone | custom fusion | bytes 5125120 | tf_op jit(solution)/shard_map/jit(_take)/gather | solution.py:38
  631.4 4.4 broadcast_select_fusion
  635.8 8.3 %reshape.163 = f32[128,156,32]{2,1,0:T(8,128)} reshape(f32[3328,192]{1,0:T(8,128)} %broadcast_select_fusion) | data formatting | bytes 5111808 | tf_op jit(solution)/shard_map/reshape | solution.py:39
  644.2 11.4 %fusion.20 = f32[128,32,6]{1,2,0:T(8,128)S(1)} fusion(f32[128,156,32]{2,1,0:T(8,128)} %reshape.163, f32[128,6,156]{2,1,0:T(8,128)S(1)} %copy.139), kind=kOutput, calls=%fused_computation.105 | convolution fusion | flops 46006272 | bytes 3133440 | tf_op jit(solution)/shard_map/oae,oeb->oab/dot_general | solution.py:40
  (179 shorter events, 29.2 us)
Async XLA Ops:
  7.2 21.8 %copy-start.13 = (f32[6,6,128]{2,1,0:T(8,128)S(1)}, f32[6,6,128]{2,1,0:T(8,128)}, u32[]{:S(2)}) copy-start(f32[6,6,128]{2,1,0:T(8,128)} %param.30) | copy-start | bytes 55300
  7.2 22.4 %copy-start.1 = (f32[26,6,6,32]{3,0,2,1:T(8,128)S(1)}, f32[26,6,6,32]{3,0,2,1:T(8,128)}, u32[]{:S(2)}) copy-start(f32[26,6,6,32]{3,0,2,1:T(8,128)} %param.34) | copy-start | bytes 359428
  7.2 309.8 %all-reduce.3.cloned.1.call-start = ((), (), s32[]{:S(2)}) async-start(), calls=%async_computation | async-start | bytes 1966080 | tf_op jit(solution)/shard_map/psum | solution.py:107
  9.2 58.7 %copy-start.16 = (pred[16]{0:T(512)(128)(4,1)}, pred[16]{0:T(512)(128)(4,1)S(1)}, u32[]{:S(2)}) copy-start(pred[16]{0:T(512)(128)(4,1)S(1)} %get-tuple-element.16) | copy-start | bytes 52
  9.3 57.2 %copy-start.18 = (s32[1024]{0:T(1024)}, s32[1024]{0:T(1024)S(1)}, u32[]{:S(2)}) copy-start(s32[1024]{0:T(1024)S(1)} %pad_clamp_fusion.7) | copy-start | bytes 12292
  10.6 22.1 %collective-permute-start = (f32[1,6,32,16]{2,1,3,0:T(8,128)}, f32[1,6,32,16]{2,1,3,0:T(8,128)S(1)}, u32[]{:S(2)}, u32[]{:S(2)}) collective-permute-start(f32[1,6,32,16]{2,1,3,0:T(8,128)} %select_bitcast_fusion.7), channel_id=1, source_target_pairs={{0,1},{1,2},{2,3},{3,4},{4,5},{5,6},{6,7},{7,8},{8,9},{9,10},{10,1... | collective-permute-start | bytes 36872 | tf_op jit(solution)/shard_map/ppermute | solution.py:14
  12.5 9.2 %copy-start.19 = (s32[1024]{0:T(1024)}, s32[1024]{0:T(1024)S(1)}, u32[]{:S(2)}) copy-start(s32[1024]{0:T(1024)S(1)} %pad_clamp_fusion.6) | copy-start | bytes 12292
  13.8 19.0 %collective-permute-start.1 = (f32[1,6,32,16]{2,1,3,0:T(8,128)}, f32[1,6,32,16]{2,1,3,0:T(8,128)S(1)}, u32[]{:S(2)}, u32[]{:S(2)}) collective-permute-start(f32[1,6,32,16]{2,1,3,0:T(8,128)} %select_bitcast_fusion.6), channel_id=1, source_target_pairs={{1,0},{2,1},{3,2},{4,3},{5,4},{6,5},{7,6},{8,7},{9,8},{10,9},{11,1... | collective-permute-start | bytes 36872 | tf_op jit(solution)/shard_map/ppermute | solution.py:15
  27.0 5.0 copy-start.11
  54.5 11.6 %copy-start = (f32[6,32,128]{2,1,0:T(8,128)S(1)}, f32[6,32,128]{2,1,0:T(8,128)}, u32[]{:S(2)}) copy-start(f32[6,32,128]{2,1,0:T(8,128)} %param.24) | copy-start | bytes 294916
  54.5 11.6 %copy-start.5 = (f32[6,6,128]{2,1,0:T(8,128)S(1)}, f32[6,6,128]{2,1,0:T(8,128)}, u32[]{:S(2)}) copy-start(f32[6,6,128]{2,1,0:T(8,128)} %param.26) | copy-start | bytes 55300
  65.9 12.3 %copy-start.3 = (f32[6,6,128]{2,1,0:T(8,128)S(1)}, f32[6,6,128]{2,1,0:T(8,128)}, u32[]{:S(2)}) copy-start(f32[6,6,128]{2,1,0:T(8,128)} %param.25) | copy-start | bytes 55300
  68.1 10.2 %collective-permute-start.2 = (f32[1,6,32,16]{2,1,3,0:T(8,128)S(1)}, f32[1,6,32,16]{2,1,3,0:T(8,128)S(1)}, u32[]{:S(2)}, u32[]{:S(2)}) collective-permute-start(f32[1,6,32,16]{2,1,3,0:T(8,128)S(1)} %select_bitcast_fusion.5), channel_id=1, source_target_pairs={{0,1},{1,2},{2,3},{3,4},{4,5},{5,6},{6,7},{7,8},{8,9},{9,10},{10,1... | collective-permute-start | bytes 36872 | tf_op jit(solution)/shard_map/ppermute | solution.py:14
  70.1 9.8 %collective-permute-start.3 = (f32[1,6,32,16]{2,1,3,0:T(8,128)S(1)}, f32[1,6,32,16]{2,1,3,0:T(8,128)S(1)}, u32[]{:S(2)}, u32[]{:S(2)}) collective-permute-start(f32[1,6,32,16]{2,1,3,0:T(8,128)S(1)} %select_bitcast_fusion.4), channel_id=1, source_target_pairs={{1,0},{2,1},{3,2},{4,3},{5,4},{6,5},{7,6},{8,7},{9,8},{10,9},{11,1... | collective-permute-start | bytes 36872 | tf_op jit(solution)/shard_map/ppermute | solution.py:15
  101.8 11.7 %copy-start.15 = (f32[6,6,128]{2,1,0:T(8,128)S(1)}, f32[6,6,128]{2,1,0:T(8,128)}, u32[]{:S(2)}) copy-start(f32[6,6,128]{2,1,0:T(8,128)} %copy.143) | copy-start | bytes 55300
  101.8 11.7 %copy-start.25 = (s32[128]{0:T(128)S(1)}, s32[128]{0:T(128)}, u32[]{:S(2)}) copy-start(s32[128]{0:T(128)} %param.31) | copy-start | bytes 1540
  101.8 36.3 %copy-start.9 = (f32[6,6,32]{2,1,0:T(8,128)S(1)}, f32[6,6,32]{2,1,0:T(8,128)}, u32[]{:S(2)}) copy-start(f32[6,6,32]{2,1,0:T(8,128)} %param.33) | copy-start | bytes 13828
  101.8 37.2 %copy-start.22 = (pred[8]{0:T(512)(128)(4,1)S(1)}, pred[8]{0:T(512)(128)(4,1)}, u32[]{:S(2)}) copy-start(pred[8]{0:T(512)(128)(4,1)} %get-tuple-element.12) | copy-start | bytes 28
  101.8 41.0 %copy-start.20 = (pred[8]{0:T(512)(128)(4,1)S(1)}, pred[8]{0:T(512)(128)(4,1)}, u32[]{:S(2)}) copy-start(pred[8]{0:T(512)(128)(4,1)} %get-tuple-element.20) | copy-start | bytes 28
  101.8 48.9 %copy-start.7 = (f32[6,6,32]{2,1,0:T(8,128)S(1)}, f32[6,6,32]{2,1,0:T(8,128)}, u32[]{:S(2)}) copy-start(f32[6,6,32]{2,1,0:T(8,128)} %param.32) | copy-start | bytes 13828
  139.0 11.8 %collective-permute-start.4 = (f32[1,6,32,8]{2,1,3,0:T(8,128)S(1)}, f32[1,6,32,8]{2,1,3,0:T(8,128)S(1)}, u32[]{:S(2)}, u32[]{:S(2)}) collective-permute-start(f32[1,6,32,8]{2,1,3,0:T(8,128)S(1)} %select_bitcast_fusion.11), channel_id=1, source_target_pairs={{0,8},{8,16},{16,24},{24,32},{32,40},{40,48},{48,56},{56,64},{64,7... | collective-permute-start | bytes 18440 | tf_op jit(solution)/shard_map/ppermute | solution.py:14
  142.8 8.9 %collective-permute-start.5 = (f32[1,6,32,8]{2,1,3,0:T(8,128)S(1)}, f32[1,6,32,8]{2,1,3,0:T(8,128)S(1)}, u32[]{:S(2)}, u32[]{:S(2)}) collective-permute-start(f32[1,6,32,8]{2,1,3,0:T(8,128)S(1)} %select_bitcast_fusion.10), channel_id=1, source_target_pairs={{8,0},{16,8},{24,16},{32,24},{40,32},{48,40},{56,48},{64,56},{72,6... | collective-permute-start | bytes 18440 | tf_op jit(solution)/shard_map/ppermute | solution.py:15
  155.6 7.3 %copy-start.14 = (f32[6,6,32]{2,1,0:T(8,128)S(1)}, f32[6,6,32]{2,1,0:T(8,128)}, u32[]{:S(2)}) copy-start(f32[6,6,32]{2,1,0:T(8,128)} %copy.151) | copy-start | bytes 13828
  155.6 7.4 %copy-start.24 = (s32[32]{0:T(128)S(1)}, s32[32]{0:T(128)}, u32[]{:S(2)}) copy-start(s32[32]{0:T(128)} %param.38) | copy-start | bytes 388
  164.6 409.8 %all-reduce.5.cloned.1.call-start = ((), (), s32[]{:S(2)}) async-start(), calls=%async_computation.1 | async-start | bytes 1966080 | tf_op jit(solution)/shard_map/psum | solution.py:110
  324.5 257.4 %copy-start.12 = (f32[6,6,32]{2,1,0:T(8,128)S(1)}, f32[6,6,32]{2,1,0:T(8,128)}, u32[]{:S(2)}) copy-start(f32[6,6,32]{2,1,0:T(8,128)} %param.37) | copy-start | bytes 13828
  324.5 259.1 %copy-start.23 = (pred[8]{0:T(512)(128)(4,1)S(1)}, pred[8]{0:T(512)(128)(4,1)}, u32[]{:S(2)}) copy-start(pred[8]{0:T(512)(128)(4,1)} %get-tuple-element.12) | copy-start | bytes 28
  324.5 262.5 %copy-start.21 = (pred[8]{0:T(512)(128)(4,1)S(1)}, pred[8]{0:T(512)(128)(4,1)}, u32[]{:S(2)}) copy-start(pred[8]{0:T(512)(128)(4,1)} %get-tuple-element.20) | copy-start | bytes 28
  324.5 268.4 %copy-start.8 = (f32[6,6,32]{2,1,0:T(8,128)S(1)}, f32[6,6,32]{2,1,0:T(8,128)}, u32[]{:S(2)}) copy-start(f32[6,6,32]{2,1,0:T(8,128)} %param.32) | copy-start | bytes 13828
  583.7 9.4 %collective-permute-start.6 = (f32[1,6,32,8]{2,1,3,0:T(8,128)S(1)}, f32[1,6,32,8]{2,1,3,0:T(8,128)S(1)}, u32[]{:S(2)}, u32[]{:S(2)}) collective-permute-start(f32[1,6,32,8]{2,1,3,0:T(8,128)S(1)} %select_bitcast_fusion.9), channel_id=1, source_target_pairs={{0,8},{8,16},{16,24},{24,32},{32,40},{40,48},{48,56},{56,64},{64,7... | collective-permute-start | bytes 18440 | tf_op jit(solution)/shard_map/ppermute | solution.py:14
  587.1 7.2 %collective-permute-start.7 = (f32[1,6,32,8]{2,1,3,0:T(8,128)S(1)}, f32[1,6,32,8]{2,1,3,0:T(8,128)S(1)}, u32[]{:S(2)}, u32[]{:S(2)}) collective-permute-start(f32[1,6,32,8]{2,1,3,0:T(8,128)S(1)} %select_bitcast_fusion.8), channel_id=1, source_target_pairs={{8,0},{16,8},{24,16},{32,24},{40,32},{48,40},{56,48},{64,56},{72,6... | collective-permute-start | bytes 18440 | tf_op jit(solution)/shard_map/ppermute | solution.py:15
  598.2 7.3 %copy-start.10 = (f32[6,6,32]{2,1,0:T(8,128)S(1)}, f32[6,6,32]{2,1,0:T(8,128)}, u32[]{:S(2)}) copy-start(f32[6,6,32]{2,1,0:T(8,128)} %param.33) | copy-start | bytes 13828
  598.2 8.4 %copy-start.26 = (pred[128]{0:T(512)(128)(4,1)S(1)}, pred[128]{0:T(512)(128)(4,1)}, u32[]{:S(2)}) copy-start(pred[128]{0:T(512)(128)(4,1)} %compare_and_fusion.7) | copy-start | bytes 388
  605.5 4.9 copy-start.17
  605.5 15.0 %copy-start.4 = (f32[6,6,128]{2,1,0:T(8,128)S(1)}, f32[6,6,128]{2,1,0:T(8,128)}, u32[]{:S(2)}) copy-start(f32[6,6,128]{2,1,0:T(8,128)} %param.25) | copy-start | bytes 55300
  608.5 13.8 %copy-start.2 = (f32[192,128]{1,0:T(8,128)S(1)}, f32[192,128]{1,0:T(8,128)}, u32[]{:S(2)}) copy-start(f32[192,128]{1,0:T(8,128)} %bitcast_add_fusion.1) | copy-start | bytes 294916
  610.5 10.9 %collective-permute-start.8 = (f32[1,6,32,16]{2,1,3,0:T(8,128)S(1)}, f32[1,6,32,16]{2,1,3,0:T(8,128)S(1)}, u32[]{:S(2)}, u32[]{:S(2)}) collective-permute-start(f32[1,6,32,16]{2,1,3,0:T(8,128)S(1)} %select_bitcast_fusion.3), channel_id=1, source_target_pairs={{0,1},{1,2},{2,3},{3,4},{4,5},{5,6},{6,7},{7,8},{8,9},{9,10},{10,1... | collective-permute-start | bytes 36872 | tf_op jit(solution)/shard_map/ppermute | solution.py:14
  612.5 9.8 %collective-permute-start.9 = (f32[1,6,32,16]{2,1,3,0:T(8,128)S(1)}, f32[1,6,32,16]{2,1,3,0:T(8,128)S(1)}, u32[]{:S(2)}, u32[]{:S(2)}) collective-permute-start(f32[1,6,32,16]{2,1,3,0:T(8,128)S(1)} %select_bitcast_fusion.2), channel_id=1, source_target_pairs={{1,0},{2,1},{3,2},{4,3},{5,4},{6,5},{7,6},{8,7},{9,8},{10,9},{11,1... | collective-permute-start | bytes 36872 | tf_op jit(solution)/shard_map/ppermute | solution.py:15
  644.2 11.6 %copy-start.6 = (f32[6,6,128]{2,1,0:T(8,128)S(1)}, f32[6,6,128]{2,1,0:T(8,128)}, u32[]{:S(2)}) copy-start(f32[6,6,128]{2,1,0:T(8,128)} %param.26) | copy-start | bytes 55300
Sparse Core Ops, SparseCore 0:
  164.7 152.2 all-reduce.2
  322.5 251.8 all-reduce.4
where the time goes:
time: 676 us; the launch traced here: 664 us
  waiting for transfers between devices  403 us (60%)
  local copies, waits for them, and re-layouts  92.4 us (14%)
  starting transfers between devices  49.9 us (7%)
  matrix products  48.5 us (7%)
  other arithmetic  31.1 us (5%)
  blocking collectives  24.4 us (4%)
  between operations  15.3 us (2%)
    psum x1, waiting for transfers between devices, on_device(): solved = lax.psum(partial_sum, ('grp', 'sub'))  250 us
    psum x1, waiting for transfers between devices, on_device(): lax.psum(summed_rows(left_four_blocks, prolong4, agg4, coarse_rows), 'grp')  148 us
    dot_general x5, matrix products, stencil(): jnp.einsum('oae,oeb->oab', offdiagonal_rows, selected_entries, precision=...  42.3 us
    ppermute x5, starting transfers between devices, with_halo(): after = lax.ppermute(initial, axis, down)  37.7 us
    gather x5, local copies, waits for them, and re-layouts, stencil(): jnp.take(rows_first, jnp.transpose(column_list).reshape(-1), axis=0)  32 us
    reshape x5, local copies, waits for them, and re-layouts, stencil(): selected_entries = selected_entries.reshape(own_count, count * 6, sides)  31.3 us
    psum x1, blocking collectives, on_device(): rhs_four = lax.psum(partial_four, 'sub')  24.4 us
    select_n x7, other arithmetic, stencil(): jnp.take(rows_first, jnp.transpose(column_list).reshape(-1), axis=0)  15.4 us
  transfers between devices with their start and end apart: 12, of which 6 were waited for; matrix products, arithmetic and copies ran while one was open for 3% of the time, Pallas kernels for 0%

commit v1 on v0

v1 whole, which is shorter than its diff:
```python
import jax
import jax.numpy as jnp
from jax import lax
from jax.experimental import pallas as pl
from jax.experimental.pallas import tpu as pltpu
from jax.sharding import PartitionSpec as P

F32 = jnp.float32
BF16 = jnp.bfloat16
LIMIT = 40 * 1024 * 1024
NT = (((1,), (1,)), ((), ()))
HIGHEST = lax.Precision.HIGHEST

ROWS = 128
R = 32
NOFF = 26
PAIRS = NOFF // 2
HALO = 16
EXT = ROWS + 2 * HALO
FOUR = 32
HALO4 = 8
EXT4 = FOUR + 2 * HALO4
WIDE4 = 896
C5 = 40
LANES5 = 128
NX = 4
NZ = 8


def call(body, outs, scratch, flops, *args):
    size = sum(a.size * a.dtype.itemsize for a in args)
    out_shape = [jax.ShapeDtypeStruct(s, F32) for s in outs]
    out = pl.pallas_call(
        body,
        out_shape=out_shape,
        in_specs=[pl.BlockSpec(memory_space=pltpu.VMEM)] * len(args),
        out_specs=[pl.BlockSpec(memory_space=pltpu.VMEM)] * len(outs),
        scratch_shapes=scratch,
        compiler_params=pltpu.CompilerParams(vmem_limit_bytes=LIMIT),
        cost_estimate=pl.CostEstimate(flops=flops, bytes_accessed=size, transcendentals=0),
    )(*args)
    return out


def split(x):
    high = x.astype(BF16)
    rest = x - high.astype(F32)
    middle = rest.astype(BF16)
    low = (rest - middle.astype(F32)).astype(BF16)
    return high, middle, low


def pick(x, selector):
    count = x.shape[0]
    out = jnp.dot(jnp.concatenate(split(x), axis=0), selector, preferred_element_type=F32)
    return out[:count] + out[count : 2 * count] + out[2 * count :]


def pick_rows(selector, x):
    first, second, third = [
        lax.dot_general(selector, part, NT, preferred_element_type=F32) for part in split(x)
    ]
    return first + second + third


def column_selector(rows, index_row):
    numbers = lax.broadcasted_iota(jnp.int32, (rows, index_row.shape[1]), 0)
    return jnp.where(numbers == index_row, 1.0, 0.0).astype(BF16)


def row_selector(index_column, columns):
    numbers = lax.broadcasted_iota(jnp.int32, (index_column.shape[0], columns), 1)
    return jnp.where(numbers == index_column, 1.0, 0.0).astype(BF16)


def blockmul(blocks_ref, vectors, transposed=False):
    out = []
    for i in range(6):
        total = None
        for j in range(6):
            block = blocks_ref[j, i : i + 1, :] if transposed else blocks_ref[i, j : j + 1, :]
            term = block * vectors[j]
            total = term if total is None else total + term
        out.append(total)
    return out


def rows_of(ref):
    return [ref[j] for j in range(6)]


def flat(vectors):
    return jnp.concatenate(vectors, axis=0)


def put(ref, vectors):
    for j in range(6):
        ref[j] = vectors[j]


FINE_SCRATCH = [
    pltpu.VMEM((3 * 6 * R, EXT), BF16),
    pltpu.VMEM((6 * R, 2 * ROWS), F32),
    pltpu.VMEM((6 * R, 2 * ROWS), F32),
]


def fine_product(vectors, mate_ref, off_ref, diag_ref, blocks_ref, cols_ref, scratch):
    parts_ref, even_ref, odd_ref = scratch
    halo = jnp.concatenate([mate_ref[...], off_ref[...]], axis=0).T
    extended = jnp.concatenate([flat(vectors), halo], axis=1)
    parts_ref[...] = jnp.concatenate(split(extended), axis=0)

    def gather(pair, ref):
        selector = jnp.concatenate(
            [column_selector(EXT, cols_ref[2 * pair + h]) for h in range(2)], axis=1
        )
        out = jnp.dot(parts_ref[...], selector, preferred_element_type=F32)
        count = 6 * R
        ref[...] = out[:count] + out[count : 2 * count] + out[2 * count :]

    def add(pair, ref, totals):
        totals = list(totals)
        for h in range(2):
            k = 2 * pair + h
            for j in range(6):
                value = ref[j * R : (j + 1) * R, h * ROWS : (h + 1) * ROWS]
                for i in range(6):
                    totals[i] = totals[i] + blocks_ref[k, i, j : j + 1, :] * value
        return tuple(totals)

    totals = tuple(blockmul(diag_ref, vectors))
    gather(0, even_ref)

    def step(t, totals):
        gather(2 * t + 1, odd_ref)
        totals = add(2 * t, even_ref, totals)
        gather(2 * t + 2, even_ref)
        return add(2 * t + 1, odd_ref, totals)

    totals = lax.fori_loop(0, (PAIRS - 1) // 2, step, totals)
    return add(PAIRS - 1, even_ref, totals)


def send_rows(vectors, index_ref):
    return pick_rows(row_selector(index_ref[...], vectors[0].shape[1]), flat(vectors))


def first_kernel(resid_ref, smooth_ref, index_ref, once_ref, mate_ref, off_ref):
    once = blockmul(smooth_ref, rows_of(resid_ref))
    put(once_ref, once)
    sent = send_rows(once, index_ref)
    mate_ref[...] = sent[:HALO]
    off_ref[...] = sent[HALO:]


def sweep_kernel(
    once_ref, mate_in, off_in, resid_ref, smooth_ref, diag_ref, blocks_ref, cols_ref, index_ref,
    twice_ref, mate_ref, off_ref, *scratch
):
    once = rows_of(once_ref)
    product = fine_product(once, mate_in, off_in, diag_ref, blocks_ref, cols_ref, scratch)
    left = [resid_ref[j] - product[j] for j in range(6)]
    update = blockmul(smooth_ref, left)
    twice = [a + b for a, b in zip(once, update)]
    put(twice_ref, twice)
    sent = send_rows(twice, index_ref)
    mate_ref[...] = sent[:HALO]
    off_ref[...] = sent[HALO:]


def restrict_kernel(
    twice_ref, mate_in, off_in, resid_ref, prolong_ref, diag_ref, blocks_ref, cols_ref, agg_ref,
    four_ref, *scratch
):
    twice = rows_of(twice_ref)
    product = fine_product(twice, mate_in, off_in, diag_ref, blocks_ref, cols_ref, scratch)
    left = [resid_ref[j] - product[j] for j in range(6)]
    restricted = blockmul(prolong_ref, left, transposed=True)
    four_ref[...] = pick_rows(column_selector(FOUR, agg_ref[...]), flat(restricted))


def last_kernel(
    refined_ref, mate_in, off_in, resid_ref, smooth_ref, diag_ref, blocks_ref, cols_ref,
    result_ref, *scratch
):
    refined = rows_of(refined_ref)
    product = fine_product(refined, mate_in, off_in, diag_ref, blocks_ref, cols_ref, scratch)
    left = [resid_ref[j] - product[j] for j in range(6)]
    update = blockmul(smooth_ref, left)
    put(result_ref, [a + b for a, b in zip(refined, update)])


def start_kernel(four_ref, smooth_ref, index_ref, rhs_ref, start_ref, sent_ref):
    columns = four_ref[...].T
    rhs = [columns[j * R : (j + 1) * R] for j in range(6)]
    start = blockmul(smooth_ref, rhs)
    put(rhs_ref, rhs)
    put(start_ref, start)
    sent_ref[...] = send_rows(start, index_ref)[:HALO4]


FOUR_SCRATCH = [pltpu.VMEM((6 * R, EXT4), F32), pltpu.VMEM((6 * R, WIDE4), F32)]


def four_product(vectors, first_in, second_in, diag_ref, blocks_ref, cols_ref, scratch):
    extended_ref, wide_ref = scratch
    extended_ref[:, :FOUR] = flat(vectors)
    extended_ref[:, FOUR:] = jnp.concatenate([first_in[...], second_in[...]], axis=0).T
    wide_ref[...] = pick(extended_ref[...], column_selector(EXT4, cols_ref[...]))
    totals = [None] * 6
    for tile in range(WIDE4 // 128):
        lanes = slice(tile * 128, (tile + 1) * 128)
        for j in range(6):
            value = wide_ref[j * R : (j + 1) * R, lanes]
            for i in range(6):
                term = blocks_ref[i, j : j + 1, lanes] * value
                totals[i] = term if totals[i] is None else totals[i] + term
    diagonal = blockmul(diag_ref, vectors)
    out = []
    for i in range(6):
        folded = totals[i] + pltpu.roll(totals[i], 64, 1)
        folded = folded + pltpu.roll(folded, 32, 1)
        out.append(folded[:, :FOUR] + diagonal[i])
    return out


def coarse_kernel(
    rhs_ref, start_ref, first_in, second_in, prolong_ref, diag_ref, blocks_ref, cols_ref, place_ref,
    out_ref, *scratch
):
    start = rows_of(start_ref)
    product = four_product(start, first_in, second_in, diag_ref, blocks_ref, cols_ref, scratch)
    left = [rhs_ref[j] - product[j] for j in range(6)]
    restricted = blockmul(prolong_ref, left, transposed=True)
    total = None
    for i in range(6):
        term = pick(restricted[i], row_selector(place_ref[i * FOUR : (i + 1) * FOUR, :], LANES5))
        total = term if total is None else total + term
    out_ref[...] = total


def project_kernel(coarse_ref, factor_ref, out_ref):
    rows = factor_ref[...].reshape(-1, factor_ref.shape[2])
    total = None
    for z in range(coarse_ref.shape[0]):
        columns = rows[:, z * LANES5 : (z + 1) * LANES5]
        term = lax.dot_general(
            coarse_ref[z], columns, NT, precision=HIGHEST, preferred_element_type=F32
        )
        total = term if total is None else total + term
    out_ref[...] = total


def solve_kernel(projected_ref, factor_ref, out_ref):
    rows = factor_ref[...].reshape(-1, factor_ref.shape[2])
    solved = jnp.dot(projected_ref[...], rows, precision=HIGHEST, preferred_element_type=F32)
    for z in range(out_ref.shape[0]):
        out_ref[z] = solved[:, z * LANES5 : (z + 1) * LANES5]


def middle_kernel(
    solved_ref, start_ref, prolong_ref, place_ref, index_ref, mid_ref, sent_ref
):
    solved = jnp.concatenate([solved_ref[0], solved_ref[1]], axis=1)
    parts = jnp.concatenate(split(solved), axis=0)
    picked = []
    for i in range(6):
        selector = column_selector(2 * LANES5, place_ref[i])
        out = jnp.dot(parts, selector, preferred_element_type=F32)
        picked.append(out[:R] + out[R : 2 * R] + out[2 * R :])
    update = blockmul(prolong_ref, picked)
    mid = [start_ref[j] + update[j] for j in range(6)]
    put(mid_ref, mid)
    sent_ref[...] = send_rows(mid, index_ref)[:HALO4]


def correct_kernel(
    rhs_ref, mid_ref, first_in, second_in, smooth4_ref, diag4_ref, blocks4_ref, cols4_ref,
    twice_ref, prolong_ref, agg_ref, index_ref,
    correction_ref, refined_ref, mate_ref, off_ref, *scratch
):
    mid = rows_of(mid_ref)
    product = four_product(mid, first_in, second_in, diag4_ref, blocks4_ref, cols4_ref, scratch)
    left = [rhs_ref[j] - product[j] for j in range(6)]
    update = blockmul(smooth4_ref, left)
    correction = [a + b for a, b in zip(mid, update)]
    put(correction_ref, correction)
    picked = pick(flat(correction), column_selector(FOUR, agg_ref[...]))
    added = blockmul(prolong_ref, [picked[j * R : (j + 1) * R] for j in range(6)])
    refined = [twice_ref[j] + added[j] for j in range(6)]
    put(refined_ref, refined)
    sent = send_rows(refined, index_ref)
    mate_ref[...] = sent[:HALO]
    off_ref[...] = sent[HALO:]


def pack_kernel(factor_ref, out_ref):
    rows, columns = factor_ref.shape
    width = columns // 6
    out_ref[...] = jnp.zeros(out_ref.shape, F32)
    for x in range(NX):
        for half in range(2):
            for z in range(NZ):
                for i in range(3):
                    start = (3 * half + i) * width + (z * NX + x) * C5
                    lanes = z * LANES5 + i * C5
                    out_ref[2 * x + half, :rows, lanes : lanes + C5] = factor_ref[
                        :, start : start + C5
                    ]


def on_device(
    resid3, diag3, smooth3, off3, cols3, send3, prolong3, agg3,
    diag4, smooth4, off4, cols4, send4, prolong4, agg4, coarse_factor,
):
    groups, subs = lax.axis_size("grp"), lax.axis_size("sub")
    both = ("grp", "sub")
    devices = groups * subs
    mates = [(i, i ^ 1) for i in range(subs)]
    offs = [(i, i + 1) for i in range(1, devices - 1, 2)]
    offs = offs + [(j, i) for i, j in offs]
    fours = [
        (g * subs + 2 * y, (g + 1) * subs + 2 * y + 1)
        for g in range(groups - 1)
        for y in range(subs // 2)
    ]
    fours = fours + [(j, i) for i, j in fours]
    even = lax.axis_index("sub") % 2 == 0

    swapped = jnp.where(cols3 >= ROWS + HALO, cols3 - HALO, cols3 + HALO)
    columns = jnp.where(even & (cols3 >= ROWS), swapped, cols3).reshape(NOFF, 1, ROWS)
    index = jnp.where(even, send3[::-1], send3).reshape(2 * HALO, 1)
    agg = agg3.reshape(1, ROWS)
    swapped4 = jnp.where(cols4 >= FOUR + HALO4, cols4 - HALO4, cols4 + HALO4)
    columns4 = jnp.where(even & (cols4 >= FOUR), swapped4, cols4).reshape(1, NOFF * FOUR)
    columns4 = jnp.pad(columns4, ((0, 0), (0, WIDE4 - NOFF * FOUR)), constant_values=-1)
    index4 = jnp.where(even, send4[1], send4[0])
    index4 = jnp.pad(index4, (0, HALO4), constant_values=-1).reshape(2 * HALO4, 1)
    blocks4 = jnp.transpose(off4, (1, 2, 0, 3)).reshape(6, 6, NOFF * FOUR)
    blocks4 = jnp.pad(blocks4, ((0, 0), (0, 0), (0, WIDE4 - NOFF * FOUR)))
    own4 = (agg4 - lax.axis_index("grp") * C5)[None, :]
    component = jnp.arange(6, dtype=jnp.int32)[:, None]
    half = lax.axis_index("sub") % 2
    lane = own4 + component % 3 * C5
    here = component // 3 == half
    place = jnp.where(here, lane, -1).reshape(6 * FOUR, 1)
    place_back = (lane + component // 3 * LANES5).reshape(6, 1, FOUR)
    along_z = [[z * NX + x for z in range(NZ)] for x in range(NX)]
    along_x_core = [
        [(z * NX + x) * subs + 2 * y + c for x in range(NX) for c in range(2)]
        for z in range(NZ)
        for y in range(subs // 2)
    ]

    vector = (6, R, ROWS)
    halo = (HALO, 6 * R)
    vector4 = (6, R, FOUR)
    halo4 = (HALO4, 6 * R)
    cost = 2 * ROWS * R * 36 * 27

    def exchange(mate, off):
        return lax.ppermute(mate, "sub", mates), lax.ppermute(off, both, offs)

    def exchange4(sent):
        received = lax.ppermute(sent, both, fours)
        return received, lax.ppermute(received, "sub", mates)

    def everywhere(value, count):
        return jnp.broadcast_to(value[None], (count,) + value.shape)

    once, mate, off = call(
        first_kernel, [vector, halo, halo], [], cost // 27, resid3, smooth3, index
    )
    mate, off = exchange(mate, off)

    (packed,) = call(
        pack_kernel, [(2 * NX, 32, NZ * LANES5)], [], 1, coarse_factor
    )
    twice, mate, off = call(
        sweep_kernel, [vector, halo, halo], FINE_SCRATCH, cost,
        once, mate, off, resid3, smooth3, diag3, off3, columns, index,
    )
    mate, off = exchange(mate, off)
    packed, mate, off = lax.optimization_barrier((packed, mate, off))
    factor = lax.all_to_all(packed, both, 0, 0, axis_index_groups=along_x_core)
    (partial_four,) = call(
        restrict_kernel, [(FOUR, 6 * R)], FINE_SCRATCH, cost,
        twice, mate, off, resid3, prolong3, diag3, off3, columns, agg,
    )
    four = partial_four
    for step in (1, 2, 4):
        four = four + lax.ppermute(four, "sub", [(i, i ^ step) for i in range(subs)])
    rhs4, start4, sent = call(
        start_kernel, [vector4, vector4, halo4], [], cost // 27, four, smooth4, index4
    )
    first, second = exchange4(sent)
    first, second, factor = lax.optimization_barrier((first, second, factor))
    (coarse,) = call(
        coarse_kernel, [(R, LANES5)], FOUR_SCRATCH, cost,
        rhs4, start4, first, second, prolong4, diag4, blocks4, columns4, place,
    )
    gathered = lax.all_to_all(
        everywhere(coarse, NZ), "grp", 0, 0, axis_index_groups=along_z
    )
    (partial_projected,) = call(
        project_kernel, [(R, 2 * NX * 32)], [], cost, gathered, factor
    )
    shares = lax.all_to_all(
        everywhere(partial_projected, 2 * NX), both, 0, 0, axis_index_groups=along_x_core
    )
    projected = jnp.sum(shares, axis=0)
    (partial_solved,) = call(
        solve_kernel, [(NZ, R, LANES5)], [], cost, projected, factor
    )
    shares = lax.all_to_all(partial_solved, "grp", 0, 0, axis_index_groups=along_z)
    shares = lax.all_to_all(everywhere(jnp.sum(shares, axis=0), subs), "sub", 0, 0)
    solved = jnp.sum(shares.reshape(subs // 2, 2, R, LANES5), axis=0)
    mid, sent = call(
        middle_kernel, [vector4, halo4], [], cost // 27,
        solved, start4, prolong4, place_back, index4,
    )
    first, second = exchange4(sent)
    correction, refined, mate, off = call(
        correct_kernel, [vector4, vector, halo, halo], FOUR_SCRATCH, cost,
        rhs4, mid, first, second, smooth4, diag4, blocks4, columns4, twice, prolong3, agg, index,
    )
    mate, off = exchange(mate, off)
    (result,) = call(
        last_kernel, [vector], FINE_SCRATCH, cost,
        refined, mate, off, resid3, smooth3, diag3, off3, columns,
    )
    return result, correction


def solution(mesh):
    split_rows = P(None, None, ("grp", "sub"))
    split_four = P(None, None, "grp")
    return jax.shard_map(
        on_device,
        mesh=mesh,
        in_specs=(
            split_rows,
            split_rows,
            split_rows,
            P(None, None, None, ("grp", "sub")),
            P(None, ("grp", "sub")),
            P(None, ("grp", "sub")),
            split_rows,
            P(("grp", "sub")),
            split_four,
            split_four,
            P(None, None, None, "grp"),
            P(None, "grp"),
            P(None, "grp"),
            split_four,
            P("grp"),
            P(("grp", "sub"), None),
        ),
        out_specs=(split_rows, split_four),
        check_vma=False,
    )
```

time: 676 us -> 131 us (0.19); the launches traced: 664 us -> 130 us
  waiting for transfers between devices: 403 us -> 32.7 us
  local copies, waits for them, and re-layouts: 92.4 us -> 5.48 us
  matrix products: 48.5 us -> 0 us
  other arithmetic: 31.1 us -> 0.27 us
  Pallas kernels: 0 us -> 16.8 us
  between operations: 15.3 us -> 0.99 us
  starting transfers between devices: 49.9 us -> 41.4 us
  blocking collectives: 24.4 us -> 32.2 us
    psum x2 -> x0, waiting for transfers between devices: 398 us -> none  [the longest x1 250 us: on_device(): solved = lax.psum(partial_sum, ('grp', 'sub'))]
    dot_general x9 -> x0, matrix products: 48.5 us -> none  [the longest x5 42.3 us: stencil(): jnp.einsum('oae,oeb->oab', offdiagonal_rows, selected_entries, precision=...]
    gather x17 -> x0, local copies, waits for them, and re-layouts: 42.5 us -> none  [the longest x5 32 us: stencil(): jnp.take(rows_first, jnp.transpose(column_list).reshape(-1), axis=0)]
    reshape x12 -> x6, local copies, waits for them, and re-layouts: 35.8 us -> 0.5 us  [the longest x1 0.24 us: on_device(): blocks4 = jnp.transpose(off4, (1, 2, 0, 3)).reshape(6, 6, NOFF * FOUR)]
    all_to_all x0 -> x2, blocking collectives: none -> 32.2 us  [the longest x1 19.6 us: on_device(): lax.all_to_all(everywhere(coarse, NZ), 'grp', 0, 0, axis_index_groups=alo...]
    psum x1 -> x0, blocking collectives: 24.4 us -> none  [on_device(): rhs_four = lax.psum(partial_four, 'sub')]
    ppermute x10 -> x13, starting transfers between devices: 49.8 us -> 29.4 us  [the longest x6 19.4 us: exchange(): return (lax.ppermute(mate, 'sub', mates), lax.ppermute(off, both, offs))]
    select_n x11 -> x5, other arithmetic: 17.6 us -> 0.1 us  [the longest x1 0.07 us: on_device(): place = jnp.where(here, lane, -1).reshape(6 * FOUR, 1)]
  transfers between devices with their start and end apart: 12 -> 16, of which waited for: 6 -> 12; matrix products, arithmetic and copies ran while one was open for 3% -> 2% of each run, Pallas kernels for 0% -> 4%
where the time goes in v1:
time: 131 us; the launch traced here: 130 us
  starting transfers between devices  41.4 us (32%)
  waiting for transfers between devices  32.7 us (25%)
  blocking collectives  32.2 us (25%)
  Pallas kernels  16.8 us (13%)
  local copies, waits for them, and re-layouts  5.48 us (4%)
    all_to_all x1, blocking collectives, on_device(): lax.all_to_all(everywhere(coarse, NZ), 'grp', 0, 0, axis_index_groups=alo...  19.6 us
    ppermute x6, starting transfers between devices, exchange(): return (lax.ppermute(mate, 'sub', mates), lax.ppermute(off, both, offs))  19.4 us
    pallas_call x11, Pallas kernels, call(): pl.pallas_call(body, out_shape=out_shape, in_specs=[pl.BlockSpec(memory_s...  16.8 us
    all_to_all x1, blocking collectives, on_device(): lax.all_to_all(everywhere(partial_projected, 2 * NX), both, 0, 0, axis_in...  12.6 us
    all_to_all x1, waiting for transfers between devices, on_device(): lax.all_to_all(partial_solved, 'grp', 0, 0, axis_index_groups=along_z)  7.28 us
    ppermute x3, waiting for transfers between devices, on_device(): lax.ppermute(four, 'sub', [(i, i ^ step) for i in range(subs)])  6.94 us
    ppermute x2, waiting for transfers between devices, exchange4(): received = lax.ppermute(sent, both, fours)  6.07 us
    all_to_all x1, waiting for transfers between devices, on_device(): lax.all_to_all(everywhere(jnp.sum(shares, axis=0), subs), 'sub', 0, 0)  6.06 us
  transfers between devices with their start and end apart: 16, of which 12 were waited for; matrix products, arithmetic and copies ran while one was open for 2% of the time, Pallas kernels for 4%

profile of v1, /device:TPU:32, one launch (start us, length us, event | category | flops | bytes accessed | tf_op | source)
XLA Modules:
  0.0 129.8 jit_solution(15563574184245323917)
XLA Ops:
  0.7 0.7 copy-done.13
  1.5 0.9 copy-done
  2.3 0.2 shard_map.167
  2.5 0.1 collective-permute-start
  2.6 6.8 %collective-permute-start.1 = (f32[16,192]{1,0:T(8,128)S(1)}, f32[16,192]{1,0:T(8,128)S(1)}, u32[]{:S(2)}, u32[]{:S(2)}) collective-permute-start(f32[16,192]{1,0:T(8,128)S(1)} %get-tuple-element.25), channel_id=1, source_target_pairs={{1,2},{3,4},{5,6},{7,8},{9,10},{11,12},{13,14},{15,16},{17,18},{19... | collective-permute-start | bytes 36872 | tf_op jit(solution)/shard_map/ppermute | solution.py:363
  9.4 1.4 %copy.36.blocks_ref = f32[26,6,6,128]{3,2,1,0:T(8,128)S(1)} copy(f32[26,6,6,128]{3,0,2,1:T(8,128)} %param.19) | data formatting | bytes 958464 | tf_op args[3]
  10.9 1.0 collective-permute-done.1.off_in
  11.9 2.7 %shard_map.168 = (f32[6,32,128]{2,1,0:T(8,128)S(1)}, f32[16,192]{1,0:T(8,128)S(1)}, f32[16,192]{1,0:T(8,128)S(1)}) custom-call(f32[6,32,128]{2,1,0:T(8,128)S(1)} %get-tuple-element.23.once_ref, f32[16,192]{1,0:T(8,128)S(1)} %collective-permute-done.mate_in, f32[16,192]{1,0:T(8,128)S(1)} %collective-permute-done.1.off_in, f32[6,32,128]{2,1,0:T(8,128)S(1)} %copy-done, ...), custom_call_target="tpu_custom_call" | custom-call | flops 7962624 | bytes 750720 | tf_op jit(solution)/shard_map/pallas_call | solution.py:33
  14.6 0.1 collective-permute-start.2
  14.7 6.8 %collective-permute-start.3 = (f32[16,192]{1,0:T(8,128)S(1)}, f32[16,192]{1,0:T(8,128)S(1)}, u32[]{:S(2)}, u32[]{:S(2)}) collective-permute-start(f32[16,192]{1,0:T(8,128)S(1)} %get-tuple-element.28), channel_id=1, source_target_pairs={{1,2},{3,4},{5,6},{7,8},{9,10},{11,12},{13,14},{15,16},{17,18},{19... | collective-permute-start | bytes 36872 | tf_op jit(solution)/shard_map/ppermute | solution.py:363
  21.5 2.1 %shard_map.169 = f32[8,32,1024]{2,1,0:T(8,128)} custom-call(f32[30,7680]{1,0:T(8,128)S(1)} %copy-done.2), custom_call_target="tpu_custom_call" | custom-call | flops 1 | bytes 921600 | tf_op jit(solution)/shard_map/pallas_call | solution.py:33
  23.6 0.4 collective-permute-done.3.off_in
  24.0 3.6 %all-to-all-start = ((f32[8,32,1024]{2,1,0:T(8,128)}), f32[8,32,1024]{2,1,0:T(8,128)S(1)}, u32[]{:S(2)}, u32[]{:S(2)}) async-start(f32[8,32,1024]{2,1,0:T(8,128)} %shard_map.169), calls=%async_computation | async-start | bytes 2097152 | tf_op jit(solution)/shard_map/all_to_all | solution.py:386
  27.6 0.6 copy-done.9
  28.2 2.7 %shard_map.170 = f32[32,192]{1,0:T(8,128)S(1)} custom-call(f32[6,32,128]{2,1,0:T(8,128)S(1)} %get-tuple-element.26.twice_ref, f32[16,192]{1,0:T(8,128)S(1)} %collective-permute-done.2.mate_in, f32[16,192]{1,0:T(8,128)S(1)} %collective-permute-done.3.off_in, f32[6,32,128]{2,1,0:T(8,128)S(1)} %copy-done.1, f32[6,6,128]{2,1,0:T(8,128)S(1)} %copy-done.8, ...), custom_call_target="tpu_custom_call" | custom-call | flops 7962624 | bytes 751104 | tf_op jit(solution)/shard_map/pallas_call | solution.py:33
  30.9 0.5 collective-permute-start.4
  31.4 0.9 collective-permute-done.4
  32.3 3.9 %collective-permute-done.5 = f32[32,192]{1,0:T(8,128)S(1)} collective-permute-done((f32[32,192]{1,0:T(8,128)S(1)}, f32[32,192]{1,0:T(8,128)S(1)}, u32[]{:S(2)}, u32[]{:S(2)}) %collective-permute-start.5) | collective-permute-done | bytes 24608 | tf_op jit(solution)/shard_map/ppermute | solution.py:393
  36.2 3.1 %collective-permute-start.6 = (f32[32,192]{1,0:T(8,128)S(1)}, f32[32,192]{1,0:T(8,128)S(1)}, u32[]{:S(2)}, u32[]{:S(2)}) collective-permute-start(f32[32,192]{1,0:T(8,128)S(1)} %add.102), channel_id=1, source_target_pairs={{0,4},{1,5},{2,6},{3,7},{4,0},{5,1},{6,2},{7,3},{8,12},{9,13},{10,... | collective-permute-start | bytes 73736 | tf_op jit(solution)/shard_map/ppermute | solution.py:393
  39.4 2.2 %collective-permute-done.6 = f32[32,192]{1,0:T(8,128)S(1)} collective-permute-done((f32[32,192]{1,0:T(8,128)S(1)}, f32[32,192]{1,0:T(8,128)S(1)}, u32[]{:S(2)}, u32[]{:S(2)}) %collective-permute-start.6) | collective-permute-done | bytes 24608 | tf_op jit(solution)/shard_map/ppermute | solution.py:393
  41.6 0.2 shard_map.171
  41.9 2.0 %collective-permute-start.7 = (f32[8,192]{1,0:T(8,128)S(1)}, f32[8,192]{1,0:T(8,128)S(1)}, u32[]{:S(2)}, u32[]{:S(2)}) collective-permute-start(f32[8,192]{1,0:T(8,128)S(1)} %get-tuple-element.33), channel_id=1, source_target_pairs={{0,9},{2,11},{4,13},{6,15},{8,17},{10,19},{12,21},{14,23},{16,25},... | collective-permute-start | bytes 18440 | tf_op jit(solution)/shard_map/ppermute | solution.py:366
  43.9 3.0 %collective-permute-done.7.first_in = f32[8,192]{1,0:T(8,128)S(1)} collective-permute-done((f32[8,192]{1,0:T(8,128)S(1)}, f32[8,192]{1,0:T(8,128)S(1)}, u32[]{:S(2)}, u32[]{:S(2)}) %collective-permute-start.7) | collective-permute-done | bytes 6176 | tf_op jit(solution)/shard_map/ppermute | solution.py:366
  46.9 0.6 collective-permute-start.8
  47.6 0.2 reshape.173
  47.9 0.1 select_n.99.place_ref
  48.1 0.3 collective-permute-done.8.second_in
  48.4 0.4 copy-done.5
  48.8 1.2 shard_map.172
  50.0 19.6 %all_to_all.25.coarse_ref = f32[8,32,128]{2,1,0:T(8,128)S(1)} all-to-all(f32[8,32,128]{2,1,0:T(8,128)S(1)} %broadcast_in_dim.20), channel_id=1, replica_groups={{0,32,64,96,128,160,192,224},{8,40,72,104,136,168,200,232},{16,48,80,11..., dimensions={0} | all-to-all | bytes 262144 | tf_op jit(solution)/shard_map/all_to_all | solution.py:403
  69.6 1.1 shard_map.173
  70.8 12.6 %all_to_all.26 = f32[8,32,256]{2,1,0:T(8,128)S(1)} all-to-all(f32[8,32,256]{2,1,0:T(8,128)S(1)} %broadcast_in_dim.21), channel_id=1, replica_groups={{0,1,8,9,16,17,24,25},{2,3,10,11,18,19,26,27},{4,5,12,13,20,21,28,29},{..., dimensions={0} | all-to-all | bytes 524288 | tf_op jit(solution)/shard_map/all_to_all | solution.py:409
  83.3 1.3 %shard_map.174 = f32[8,32,128]{2,1,0:T(8,128)} custom-call(f32[32,256]{1,0:T(8,128)S(1)} %reduce_sum.27.projected_ref, f32[8,32,1024]{2,1,0:T(8,128)S(1)} %all-to-all-done.factor_ref), custom_call_target="tpu_custom_call" | custom-call | flops 7962624 | bytes 1081344 | tf_op jit(solution)/shard_map/pallas_call | solution.py:33
  84.7 4.8 %all-to-all-start.3 = ((f32[8,32,128]{2,1,0:T(8,128)}), f32[8,32,128]{2,1,0:T(8,128)S(1)}, u32[]{:S(2)}, u32[]{:S(2)}) async-start(f32[8,32,128]{2,1,0:T(8,128)} %shard_map.174), calls=%async_computation.3 | async-start | bytes 262144 | tf_op jit(solution)/shard_map/all_to_all | solution.py:416
  89.5 7.3 %all-to-all-done.3 = f32[8,32,128]{2,1,0:T(8,128)S(1)} async-done(((f32[8,32,128]{2,1,0:T(8,128)}), f32[8,32,128]{2,1,0:T(8,128)S(1)}, u32[]{:S(2)}, u32[]{:S(2)}) %all-to-all-start.3) | async-done | bytes 131104 | tf_op jit(solution)/shard_map/all_to_all | solution.py:416
  96.8 0.7 broadcast_in_dim.36
  97.5 3.6 %all-to-all-start.4 = ((f32[8,32,128]{2,1,0:T(8,128)}), f32[8,32,128]{2,1,0:T(8,128)S(1)}, u32[]{:S(2)}, u32[]{:S(2)}) async-start(f32[8,32,128]{2,1,0:T(8,128)} %broadcast_in_dim.36), calls=%async_computation.4 | async-start | bytes 262144 | tf_op jit(solution)/shard_map/all_to_all | solution.py:417
  101.1 6.1 %all-to-all-done.4 = f32[8,32,128]{2,1,0:T(8,128)S(1)} async-done(((f32[8,32,128]{2,1,0:T(8,128)}), f32[8,32,128]{2,1,0:T(8,128)S(1)}, u32[]{:S(2)}, u32[]{:S(2)}) %all-to-all-start.4) | async-done | bytes 131104 | tf_op jit(solution)/shard_map/all_to_all | solution.py:417
  107.2 0.4 shard_map.175
  107.6 2.0 %collective-permute-start.9 = (f32[8,192]{1,0:T(8,128)S(1)}, f32[8,192]{1,0:T(8,128)S(1)}, u32[]{:S(2)}, u32[]{:S(2)}) collective-permute-start(f32[8,192]{1,0:T(8,128)S(1)} %get-tuple-element.39), channel_id=1, source_target_pairs={{0,9},{2,11},{4,13},{6,15},{8,17},{10,19},{12,21},{14,23},{16,25},... | collective-permute-start | bytes 18440 | tf_op jit(solution)/shard_map/ppermute | solution.py:366
  109.6 3.0 %collective-permute-done.9.first_in = f32[8,192]{1,0:T(8,128)S(1)} collective-permute-done((f32[8,192]{1,0:T(8,128)S(1)}, f32[8,192]{1,0:T(8,128)S(1)}, u32[]{:S(2)}, u32[]{:S(2)}) %collective-permute-start.9) | collective-permute-done | bytes 6176 | tf_op jit(solution)/shard_map/ppermute | solution.py:366
  112.7 1.8 %collective-permute-start.10 = (f32[8,192]{1,0:T(8,128)S(1)}, f32[8,192]{1,0:T(8,128)S(1)}, u32[]{:S(2)}, u32[]{:S(2)}) collective-permute-start(f32[8,192]{1,0:T(8,128)S(1)} %collective-permute-done.9.first_in), channel_id=1, source_target_pairs={{0,1},{1,0},{2,3},{3,2},{4,5},{5,4},{6,7},{7,6},{8,9},{9,8},{10,11... | collective-permute-start | bytes 18440 | tf_op jit(solution)/shard_map/ppermute | solution.py:367
  114.4 0.8 collective-permute-done.10.second_in
  115.3 1.7 %shard_map.176 = (f32[6,32,32]{2,1,0:T(8,128)}, f32[6,32,128]{2,1,0:T(8,128)S(1)}, f32[16,192]{1,0:T(8,128)S(1)}, f32[16,192]{1,0:T(8,128)S(1)}) custom-call(f32[6,32,32]{2,1,0:T(8,128)S(1)} %get-tuple-element.31.rhs_ref, f32[6,32,32]{2,1,0:T(8,128)S(1)} %get-tuple-element.38.mid_ref, f32[8,192]{1,0:T(8,128)S(1)} %collective-permute-done.9.first_in, ...), custom_call_target="tpu_custom_call" | custom-call | flops 7962624 | bytes 320640 | tf_op jit(solution)/shard_map/pallas_call | solution.py:33
  116.9 0.3 collective-permute-start.11
  117.3 5.4 %collective-permute-start.12 = (f32[16,192]{1,0:T(8,128)S(1)}, f32[16,192]{1,0:T(8,128)S(1)}, u32[]{:S(2)}, u32[]{:S(2)}) collective-permute-start(f32[16,192]{1,0:T(8,128)S(1)} %get-tuple-element.42), channel_id=1, source_target_pairs={{1,2},{3,4},{5,6},{7,8},{9,10},{11,12},{13,14},{15,16},{17,18},{19... | collective-permute-start | bytes 36872 | tf_op jit(solution)/shard_map/ppermute | solution.py:363
  122.7 3.9 %collective-permute-done.12.off_in = f32[16,192]{1,0:T(8,128)S(1)} collective-permute-done((f32[16,192]{1,0:T(8,128)S(1)}, f32[16,192]{1,0:T(8,128)S(1)}, u32[]{:S(2)}, u32[]{:S(2)}) %collective-permute-start.12) | collective-permute-done | bytes 12320 | tf_op jit(solution)/shard_map/ppermute | solution.py:363
  126.6 3.2 %shard_map.177 = f32[6,32,128]{2,1,0:T(8,128)} custom-call(f32[6,32,128]{2,1,0:T(8,128)S(1)} %get-tuple-element.40.refined_ref, f32[16,192]{1,0:T(8,128)S(1)} %collective-permute-done.11.mate_in, f32[16,192]{1,0:T(8,128)S(1)} %collective-permute-done.12.off_in, f32[6,32,128]{2,1,0:T(8,128)S(1)} %copy-done.1, f32[6,6,128]{2,1,0:T(8,128)S(1)} %copy-done.3, ...), custom_call_target="tpu_custom_call" | custom-call | flops 7962624 | bytes 750592 | tf_op jit(solution)/shard_map/pallas_call | solution.py:33
  (59 shorter events, 0.7 us)
Async XLA Ops:
  0.6 0.7 copy-start.13
  0.6 0.8 copy-start.3
  1.4 0.9 copy-start
  2.3 7.0 %copy-start.11 = (s32[26,128]{1,0:T(8,128)S(1)}, s32[26,128]{1,0:T(8,128)}, u32[]{:S(2)}) copy-start(s32[26,128]{1,0:T(8,128)} %param.20) | copy-start | bytes 39940
  2.5 8.4 %collective-permute-start = (f32[16,192]{1,0:T(8,128)S(1)}, f32[16,192]{1,0:T(8,128)S(1)}, u32[]{:S(2)}, u32[]{:S(2)}) collective-permute-start(f32[16,192]{1,0:T(8,128)S(1)} %get-tuple-element.24), channel_id=1, source_target_pairs={{0,1},{1,0},{2,3},{3,2},{4,5},{5,4},{6,7},{7,6},{8,9},{9,8},{10,11... | collective-permute-start | bytes 36872 | tf_op jit(solution)/shard_map/ppermute | solution.py:363
  2.6 9.3 %collective-permute-start.1 = (f32[16,192]{1,0:T(8,128)S(1)}, f32[16,192]{1,0:T(8,128)S(1)}, u32[]{:S(2)}, u32[]{:S(2)}) collective-permute-start(f32[16,192]{1,0:T(8,128)S(1)} %get-tuple-element.25), channel_id=1, source_target_pairs={{1,2},{3,4},{5,6},{7,8},{9,10},{11,12},{13,14},{15,16},{17,18},{19... | collective-permute-start | bytes 36872 | tf_op jit(solution)/shard_map/ppermute | solution.py:363
  9.4 12.1 %copy-start.2 = (f32[30,7680]{1,0:T(8,128)S(1)}, f32[30,7680]{1,0:T(8,128)}, u32[]{:S(2)}) copy-start(f32[30,7680]{1,0:T(8,128)} %factor_ref.1) | copy-start | bytes 2764804
  10.8 1.0 copy-start.4
  11.9 9.6 %copy-start.12 = (s32[26,32]{1,0:T(8,128)S(1)}, s32[26,32]{1,0:T(8,128)}, u32[]{:S(2)}) copy-start(s32[26,32]{1,0:T(8,128)} %param.27) | copy-start | bytes 9988
  14.6 9.0 %collective-permute-start.2 = (f32[16,192]{1,0:T(8,128)S(1)}, f32[16,192]{1,0:T(8,128)S(1)}, u32[]{:S(2)}, u32[]{:S(2)}) collective-permute-start(f32[16,192]{1,0:T(8,128)S(1)} %get-tuple-element.27), channel_id=1, source_target_pairs={{0,1},{1,0},{2,3},{3,2},{4,5},{5,4},{6,7},{7,6},{8,9},{9,8},{10,11... | collective-permute-start | bytes 36872 | tf_op jit(solution)/shard_map/ppermute | solution.py:363
  14.7 9.3 %collective-permute-start.3 = (f32[16,192]{1,0:T(8,128)S(1)}, f32[16,192]{1,0:T(8,128)S(1)}, u32[]{:S(2)}, u32[]{:S(2)}) collective-permute-start(f32[16,192]{1,0:T(8,128)S(1)} %get-tuple-element.28), channel_id=1, source_target_pairs={{1,2},{3,4},{5,6},{7,8},{9,10},{11,12},{13,14},{15,16},{17,18},{19... | collective-permute-start | bytes 36872 | tf_op jit(solution)/shard_map/ppermute | solution.py:363
  23.6 4.0 %copy-start.14 = (s32[2,8]{1,0:T(2,128)S(1)}, s32[2,8]{1,0:T(2,128)}, u32[]{:S(2)}) copy-start(s32[2,8]{1,0:T(2,128)} %param.28) | copy-start | bytes 196
  23.6 4.0 %copy-start.1 = (f32[6,32,128]{2,1,0:T(8,128)S(1)}, f32[6,32,128]{2,1,0:T(8,128)}, u32[]{:S(2)}) copy-start(f32[6,32,128]{2,1,0:T(8,128)} %resid_ref.7) | copy-start | bytes 294916
  23.6 4.0 %copy-start.8 = (f32[6,6,128]{2,1,0:T(8,128)S(1)}, f32[6,6,128]{2,1,0:T(8,128)}, u32[]{:S(2)}) copy-start(f32[6,6,128]{2,1,0:T(8,128)} %prolong_ref.7) | copy-start | bytes 55300
  24.0 24.4 %all-to-all-start = ((f32[8,32,1024]{2,1,0:T(8,128)}), f32[8,32,1024]{2,1,0:T(8,128)S(1)}, u32[]{:S(2)}, u32[]{:S(2)}) async-start(f32[8,32,1024]{2,1,0:T(8,128)} %shard_map.169), calls=%async_computation | async-start | bytes 2097152 | tf_op jit(solution)/shard_map/all_to_all | solution.py:386
  27.6 0.7 copy-start.9
  28.2 3.2 %copy-start.15 = (s32[32]{0:T(128)S(1)}, s32[32]{0:T(128)}, u32[]{:S(2)}) copy-start(s32[32]{0:T(128)} %param.30) | copy-start | bytes 388
  28.2 19.4 %copy-start.10 = (f32[26,6,6,32]{3,0,2,1:T(8,128)S(1)}, f32[26,6,6,32]{3,0,2,1:T(8,128)}, u32[]{:S(2)}) copy-start(f32[26,6,6,32]{3,0,2,1:T(8,128)} %param.26) | copy-start | bytes 359428
  30.9 1.3 %collective-permute-start.4 = (f32[32,192]{1,0:T(8,128)S(1)}, f32[32,192]{1,0:T(8,128)S(1)}, u32[]{:S(2)}, u32[]{:S(2)}) collective-permute-start(f32[32,192]{1,0:T(8,128)S(1)} %shard_map.170), channel_id=1, source_target_pairs={{0,1},{1,0},{2,3},{3,2},{4,5},{5,4},{6,7},{7,6},{8,9},{9,8},{10,11... | collective-permute-start | bytes 73736 | tf_op jit(solution)/shard_map/ppermute | solution.py:393
  32.3 3.9 %collective-permute-start.5 = (f32[32,192]{1,0:T(8,128)S(1)}, f32[32,192]{1,0:T(8,128)S(1)}, u32[]{:S(2)}, u32[]{:S(2)}) collective-permute-start(f32[32,192]{1,0:T(8,128)S(1)} %add.101), channel_id=1, source_target_pairs={{0,2},{1,3},{2,0},{3,1},{4,6},{5,7},{6,4},{7,5},{8,10},{9,11},{10,... | collective-permute-start | bytes 73736 | tf_op jit(solution)/shard_map/ppermute | solution.py:393
  36.2 5.4 %collective-permute-start.6 = (f32[32,192]{1,0:T(8,128)S(1)}, f32[32,192]{1,0:T(8,128)S(1)}, u32[]{:S(2)}, u32[]{:S(2)}) collective-permute-start(f32[32,192]{1,0:T(8,128)S(1)} %add.102), channel_id=1, source_target_pairs={{0,4},{1,5},{2,6},{3,7},{4,0},{5,1},{6,2},{7,3},{8,12},{9,13},{10,... | collective-permute-start | bytes 73736 | tf_op jit(solution)/shard_map/ppermute | solution.py:393
  39.4 2.2 %copy-start.6 = (f32[6,6,32]{2,1,0:T(8,128)S(1)}, f32[6,6,32]{2,1,0:T(8,128)}, u32[]{:S(2)}) copy-start(f32[6,6,32]{2,1,0:T(8,128)} %smooth4_ref.1) | copy-start | bytes 13828
  41.9 5.0 %collective-permute-start.7 = (f32[8,192]{1,0:T(8,128)S(1)}, f32[8,192]{1,0:T(8,128)S(1)}, u32[]{:S(2)}, u32[]{:S(2)}) collective-permute-start(f32[8,192]{1,0:T(8,128)S(1)} %get-tuple-element.33), channel_id=1, source_target_pairs={{0,9},{2,11},{4,13},{6,15},{8,17},{10,19},{12,21},{14,23},{16,25},... | collective-permute-start | bytes 18440 | tf_op jit(solution)/shard_map/ppermute | solution.py:366
  46.9 1.5 %collective-permute-start.8 = (f32[8,192]{1,0:T(8,128)S(1)}, f32[8,192]{1,0:T(8,128)S(1)}, u32[]{:S(2)}, u32[]{:S(2)}) collective-permute-start(f32[8,192]{1,0:T(8,128)S(1)} %collective-permute-done.7.first_in), channel_id=1, source_target_pairs={{0,1},{1,0},{2,3},{3,2},{4,5},{5,4},{6,7},{7,6},{8,9},{9,8},{10,11... | collective-permute-start | bytes 18440 | tf_op jit(solution)/shard_map/ppermute | solution.py:367
  48.1 0.7 copy-start.5
  48.1 0.7 copy-start.7
  84.7 12.1 %all-to-all-start.3 = ((f32[8,32,128]{2,1,0:T(8,128)}), f32[8,32,128]{2,1,0:T(8,128)S(1)}, u32[]{:S(2)}, u32[]{:S(2)}) async-start(f32[8,32,128]{2,1,0:T(8,128)} %shard_map.174), calls=%async_computation.3 | async-start | bytes 262144 | tf_op jit(solution)/shard_map/all_to_all | solution.py:416
  97.5 9.7 %all-to-all-start.4 = ((f32[8,32,128]{2,1,0:T(8,128)}), f32[8,32,128]{2,1,0:T(8,128)S(1)}, u32[]{:S(2)}, u32[]{:S(2)}) async-start(f32[8,32,128]{2,1,0:T(8,128)} %broadcast_in_dim.36), calls=%async_computation.4 | async-start | bytes 262144 | tf_op jit(solution)/shard_map/all_to_all | solution.py:417
  107.6 5.0 %collective-permute-start.9 = (f32[8,192]{1,0:T(8,128)S(1)}, f32[8,192]{1,0:T(8,128)S(1)}, u32[]{:S(2)}, u32[]{:S(2)}) collective-permute-start(f32[8,192]{1,0:T(8,128)S(1)} %get-tuple-element.39), channel_id=1, source_target_pairs={{0,9},{2,11},{4,13},{6,15},{8,17},{10,19},{12,21},{14,23},{16,25},... | collective-permute-start | bytes 18440 | tf_op jit(solution)/shard_map/ppermute | solution.py:366
  112.7 2.6 %collective-permute-start.10 = (f32[8,192]{1,0:T(8,128)S(1)}, f32[8,192]{1,0:T(8,128)S(1)}, u32[]{:S(2)}, u32[]{:S(2)}) collective-permute-start(f32[8,192]{1,0:T(8,128)S(1)} %collective-permute-done.9.first_in), channel_id=1, source_target_pairs={{0,1},{1,0},{2,3},{3,2},{4,5},{5,4},{6,7},{7,6},{8,9},{9,8},{10,11... | collective-permute-start | bytes 18440 | tf_op jit(solution)/shard_map/ppermute | solution.py:367
  116.9 5.7 %collective-permute-start.11 = (f32[16,192]{1,0:T(8,128)S(1)}, f32[16,192]{1,0:T(8,128)S(1)}, u32[]{:S(2)}, u32[]{:S(2)}) collective-permute-start(f32[16,192]{1,0:T(8,128)S(1)} %get-tuple-element.41), channel_id=1, source_target_pairs={{0,1},{1,0},{2,3},{3,2},{4,5},{5,4},{6,7},{7,6},{8,9},{9,8},{10,11... | collective-permute-start | bytes 36872 | tf_op jit(solution)/shard_map/ppermute | solution.py:363
  117.3 9.3 %collective-permute-start.12 = (f32[16,192]{1,0:T(8,128)S(1)}, f32[16,192]{1,0:T(8,128)S(1)}, u32[]{:S(2)}, u32[]{:S(2)}) collective-permute-start(f32[16,192]{1,0:T(8,128)S(1)} %get-tuple-element.42), channel_id=1, source_target_pairs={{1,2},{3,4},{5,6},{7,8},{9,10},{11,12},{13,14},{15,16},{17,18},{19... | collective-permute-start | bytes 36872 | tf_op jit(solution)/shard_map/ppermute | solution.py:363

commit v2 on v1

v2 whole, which is shorter than its diff:
```python
import jax
import jax.numpy as jnp
from jax import lax
from jax.experimental import pallas as pl
from jax.experimental.pallas import tpu as pltpu
from jax.sharding import PartitionSpec as P

F32 = jnp.float32
BF16 = jnp.bfloat16
LIMIT = 16 * 1024 * 1024
NT = (((1,), (1,)), ((), ()))
HIGHEST = lax.Precision.HIGHEST

ROWS = 128
R = 32
NOFF = 26
PAIRS = NOFF // 2
HALO = 16
FOUR = 32
HALO4 = 8
WIDE4 = 896
C5 = 40
LANES5 = 128
NX = 4
NZ = 8


def call(body, outs, scratch, cost, *args):
    out_shape = [s if isinstance(s, jax.ShapeDtypeStruct) else jax.ShapeDtypeStruct(s, F32) for s in outs]
    return pl.pallas_call(
        body,
        out_shape=out_shape,
        in_specs=[pl.BlockSpec(memory_space=pltpu.VMEM)] * len(args),
        out_specs=[pl.BlockSpec(memory_space=pltpu.VMEM)] * len(outs),
        scratch_shapes=scratch,
        compiler_params=pltpu.CompilerParams(vmem_limit_bytes=LIMIT),
        cost_estimate=pl.CostEstimate(flops=1, bytes_accessed=cost, transcendentals=0),
    )(*args)


def split(x):
    high = x.astype(BF16)
    rest = x - high.astype(F32)
    middle = rest.astype(BF16)
    low = (rest - middle.astype(F32)).astype(BF16)
    return high, middle, low


def pick(x, selector):
    count = x.shape[0]
    out = jnp.dot(jnp.concatenate(split(x), axis=0), selector, preferred_element_type=F32)
    return out[:count] + out[count : 2 * count] + out[2 * count :]


def pick_rows(selector, x):
    first, second, third = [
        lax.dot_general(selector, part, NT, preferred_element_type=F32) for part in split(x)
    ]
    return first + second + third


def two_parts(x, high_ref, low_ref):
    count = x.shape[0]
    parts = jnp.concatenate(split(x), axis=0)
    out = jnp.dot(parts, high_ref[...], preferred_element_type=F32)
    out = out + jnp.dot(parts, low_ref[...], preferred_element_type=F32)
    return out[:count] + out[count : 2 * count] + out[2 * count :]


def column_selector(rows, index_row):
    numbers = lax.broadcasted_iota(jnp.int32, (rows, index_row.shape[1]), 0)
    return jnp.where(numbers == index_row, 1.0, 0.0).astype(BF16)


def row_selector(index_column, columns):
    numbers = lax.broadcasted_iota(jnp.int32, (index_column.shape[0], columns), 1)
    return jnp.where(numbers == index_column, 1.0, 0.0).astype(BF16)


def blockmul(blocks_ref, vectors, transposed=False):
    out = []
    for i in range(6):
        total = None
        for j in range(6):
            block = blocks_ref[j, i : i + 1, :] if transposed else blocks_ref[i, j : j + 1, :]
            term = block * vectors[j]
            total = term if total is None else total + term
        out.append(total)
    return out


def rows_of(ref):
    return [ref[j] for j in range(6)]


def flat(vectors):
    return jnp.concatenate(vectors, axis=0)


def put(ref, vectors):
    for j in range(6):
        ref[j] = vectors[j]


OWN_SCRATCH = [
    pltpu.VMEM((6 * R, 3 * ROWS), BF16),
    pltpu.VMEM((PAIRS, 6 * R, 2 * ROWS), F32),
]


def own_kernel(vector_ref, diag_ref, blocks_ref, cols_ref, out_ref, parts_ref, picked_ref):
    vectors = rows_of(vector_ref)
    parts_ref[...] = jnp.concatenate(split(flat(vectors)), axis=1)
    for pair in range(PAIRS):
        selector = jnp.concatenate(
            [column_selector(ROWS, cols_ref[2 * pair + h]) for h in range(2)], axis=1
        )
        stacked = jnp.concatenate([selector] * 3, axis=0)
        picked_ref[pair] = jnp.dot(parts_ref[...], stacked, preferred_element_type=F32)
    totals = blockmul(diag_ref, vectors)
    for k in range(NOFF):
        lanes = slice(k % 2 * ROWS, (k % 2 + 1) * ROWS)
        for j in range(6):
            value = picked_ref[k // 2, j * R : (j + 1) * R, lanes]
            for i in range(6):
                totals[i] = totals[i] + blocks_ref[i, j, k : k + 1, :] * value
    put(out_ref, totals)


def ends_kernel(blocks_ref, cols_ref, high_ref, low_ref):
    numbers = lax.broadcasted_iota(jnp.int32, (2 * HALO, ROWS), 0) + ROWS
    for i in range(6):
        totals = [jnp.zeros((2 * HALO, ROWS), F32)] * 6
        for k in range(NOFF):
            mask = numbers == cols_ref[k]
            for j in range(6):
                totals[j] = totals[j] + jnp.where(mask, blocks_ref[i, j, k : k + 1, :], 0.0)
        for j in range(6):
            rows = slice(j * 2 * HALO, (j + 1) * 2 * HALO)
            lanes = slice(i * ROWS, (i + 1) * ROWS)
            high = totals[j].astype(BF16)
            high_ref[rows, lanes] = high
            low_ref[rows, lanes] = (totals[j] - high.astype(F32)).astype(BF16)


def fine_product(own_ref, mate_ref, off_ref, high_ref, low_ref):
    halo = jnp.concatenate([mate_ref[...], off_ref[...]], axis=0).T
    wide = jnp.concatenate([halo[j * R : (j + 1) * R] for j in range(6)], axis=1)
    out = two_parts(wide, high_ref, low_ref)
    return [own_ref[i] + out[:, i * ROWS : (i + 1) * ROWS] for i in range(6)]


def send_rows(vectors, index_ref):
    return pick_rows(row_selector(index_ref[...], vectors[0].shape[1]), flat(vectors))


def first_kernel(resid_ref, smooth_ref, index_ref, once_ref, mate_ref, off_ref):
    once = blockmul(smooth_ref, rows_of(resid_ref))
    put(once_ref, once)
    sent = send_rows(once, index_ref)
    mate_ref[...] = sent[:HALO]
    off_ref[...] = sent[HALO:]


def sweep_kernel(
    once_ref, own_ref, mate_in, off_in, high_ref, low_ref, resid_ref, smooth_ref, index_ref,
    twice_ref, mate_ref, off_ref
):
    once = rows_of(once_ref)
    product = fine_product(own_ref, mate_in, off_in, high_ref, low_ref)
    left = [resid_ref[j] - product[j] for j in range(6)]
    update = blockmul(smooth_ref, left)
    twice = [a + b for a, b in zip(once, update)]
    put(twice_ref, twice)
    sent = send_rows(twice, index_ref)
    mate_ref[...] = sent[:HALO]
    off_ref[...] = sent[HALO:]


def restrict_kernel(
    own_ref, mate_in, off_in, high_ref, low_ref, resid_ref, prolong_ref, agg_ref, four_ref
):
    product = fine_product(own_ref, mate_in, off_in, high_ref, low_ref)
    left = [resid_ref[j] - product[j] for j in range(6)]
    restricted = blockmul(prolong_ref, left, transposed=True)
    four_ref[...] = pick_rows(column_selector(FOUR, agg_ref[...]), flat(restricted))


def last_kernel(
    refined_ref, own_ref, mate_in, off_in, high_ref, low_ref, resid_ref, smooth_ref, result_ref
):
    refined = rows_of(refined_ref)
    product = fine_product(own_ref, mate_in, off_in, high_ref, low_ref)
    left = [resid_ref[j] - product[j] for j in range(6)]
    update = blockmul(smooth_ref, left)
    put(result_ref, [a + b for a, b in zip(refined, update)])


def start_kernel(four_ref, smooth_ref, index_ref, rhs_ref, start_ref, sent_ref):
    columns = four_ref[...].T
    rhs = [columns[j * R : (j + 1) * R] for j in range(6)]
    start = blockmul(smooth_ref, rhs)
    put(rhs_ref, rhs)
    put(start_ref, start)
    sent_ref[...] = send_rows(start, index_ref)[:HALO4]


FOUR_SCRATCH = [pltpu.VMEM((6 * R, WIDE4), F32)]


def fold(x):
    x = x + pltpu.roll(x, 64, 1)
    return x + pltpu.roll(x, 32, 1)


def lay_four_kernel(blocks_ref, out_ref):
    out_ref[...] = jnp.zeros(out_ref.shape, F32)
    for i in range(6):
        for j in range(6):
            for q in range(4):
                count = (NOFF + 3 - q) // 4
                out_ref[i, j, :count, q * FOUR : (q + 1) * FOUR] = blocks_ref[
                    i, j, pl.ds(q, count, stride=4), :
                ]


def own_four_kernel(vector_ref, diag_ref, blocks_ref, cols_ref, out_ref, wide_ref):
    vectors = rows_of(vector_ref)
    wide_ref[...] = pick(flat(vectors), column_selector(FOUR, cols_ref[...]))
    totals = [None] * 6
    for tile in range(WIDE4 // 128):
        lanes = slice(tile * 128, (tile + 1) * 128)
        for j in range(6):
            value = wide_ref[j * R : (j + 1) * R, lanes]
            for i in range(6):
                term = blocks_ref[i, j, tile : tile + 1, :] * value
                totals[i] = term if totals[i] is None else totals[i] + term
    diagonal = blockmul(diag_ref, vectors)
    put(out_ref, [fold(totals[i])[:, :FOUR] + diagonal[i] for i in range(6)])


def ends_four_kernel(blocks_ref, cols_ref, high_ref, low_ref):
    numbers = lax.broadcasted_iota(jnp.int32, (2 * HALO4, 128), 0) + FOUR
    lane = lax.broadcasted_iota(jnp.int32, (2 * HALO4, 128), 1)
    for half in range(2):
        columns = [jnp.zeros((2 * HALO4, 128), F32)] * 6
        for i in range(4 * half, min(4 * half + 4, 6)):
            totals = [jnp.zeros((2 * HALO4, 128), F32)] * 6
            for tile in range(WIDE4 // 128):
                lanes = slice(tile * 128, (tile + 1) * 128)
                mask = numbers == cols_ref[:, lanes]
                for j in range(6):
                    totals[j] = totals[j] + jnp.where(mask, blocks_ref[i, j, tile : tile + 1, :], 0.0)
            start = i % 4 * FOUR
            here = (lane >= start) & (lane < start + FOUR)
            for j in range(6):
                columns[j] = jnp.where(here, fold(totals[j]), columns[j])
        for j in range(6):
            rows = slice(j * 2 * HALO4, (j + 1) * 2 * HALO4)
            high = columns[j].astype(BF16)
            high_ref[rows, half * 128 : (half + 1) * 128] = high
            low_ref[rows, half * 128 : (half + 1) * 128] = (
                columns[j] - high.astype(F32)
            ).astype(BF16)


def four_product(own_ref, first_in, second_in, high_ref, low_ref):
    halo = jnp.concatenate([first_in[...], second_in[...]], axis=0).T
    wide = jnp.concatenate([halo[j * R : (j + 1) * R] for j in range(6)], axis=1)
    out = two_parts(wide, high_ref, low_ref)
    return [own_ref[i] + out[:, i * FOUR : (i + 1) * FOUR] for i in range(6)]


def coarse_kernel(
    rhs_ref, own_ref, first_in, second_in, high_ref, low_ref, prolong_ref, place_ref, out_ref
):
    product = four_product(own_ref, first_in, second_in, high_ref, low_ref)
    left = [rhs_ref[j] - product[j] for j in range(6)]
    restricted = blockmul(prolong_ref, left, transposed=True)
    total = None
    for i in range(6):
        term = pick(restricted[i], row_selector(place_ref[i * FOUR : (i + 1) * FOUR, :], LANES5))
        total = term if total is None else total + term
    for copy in range(out_ref.shape[0]):
        out_ref[copy] = total


def project_kernel(coarse_ref, factor_ref, out_ref):
    rows = factor_ref[...].reshape(-1, factor_ref.shape[2])
    total = None
    for z in range(coarse_ref.shape[0]):
        columns = rows[:, z * LANES5 : (z + 1) * LANES5]
        term = lax.dot_general(
            coarse_ref[z], columns, NT, precision=HIGHEST, preferred_element_type=F32
        )
        total = term if total is None else total + term
    for copy in range(out_ref.shape[0]):
        out_ref[copy] = total


def solve_kernel(projected_ref, factor_ref, out_ref):
    rows = factor_ref[...].reshape(-1, factor_ref.shape[2])
    solved = jnp.dot(projected_ref[...], rows, precision=HIGHEST, preferred_element_type=F32)
    for z in range(out_ref.shape[0]):
        out_ref[z] = solved[:, z * LANES5 : (z + 1) * LANES5]


def sum_kernel(shares_ref, out_ref):
    total = shares_ref[0]
    for z in range(1, shares_ref.shape[0]):
        total = total + shares_ref[z]
    for copy in range(out_ref.shape[0]):
        out_ref[copy] = total


def middle_kernel(
    solved_ref, start_ref, prolong_ref, place_ref, index_ref, mid_ref, sent_ref
):
    solved = jnp.concatenate([solved_ref[0], solved_ref[1]], axis=1)
    parts = jnp.concatenate(split(solved), axis=0)
    picked = []
    for i in range(6):
        selector = column_selector(2 * LANES5, place_ref[i])
        out = jnp.dot(parts, selector, preferred_element_type=F32)
        picked.append(out[:R] + out[R : 2 * R] + out[2 * R :])
    update = blockmul(prolong_ref, picked)
    mid = [start_ref[j] + update[j] for j in range(6)]
    put(mid_ref, mid)
    sent_ref[...] = send_rows(mid, index_ref)[:HALO4]


def correct_kernel(
    rhs_ref, mid_ref, own_ref, first_in, second_in, high_ref, low_ref, smooth4_ref,
    twice_ref, prolong_ref, agg_ref, index_ref,
    correction_ref, refined_ref, mate_ref, off_ref
):
    mid = rows_of(mid_ref)
    product = four_product(own_ref, first_in, second_in, high_ref, low_ref)
    left = [rhs_ref[j] - product[j] for j in range(6)]
    update = blockmul(smooth4_ref, left)
    correction = [a + b for a, b in zip(mid, update)]
    put(correction_ref, correction)
    picked = pick(flat(correction), column_selector(FOUR, agg_ref[...]))
    added = blockmul(prolong_ref, [picked[j * R : (j + 1) * R] for j in range(6)])
    refined = [twice_ref[j] + added[j] for j in range(6)]
    put(refined_ref, refined)
    sent = send_rows(refined, index_ref)
    mate_ref[...] = sent[:HALO]
    off_ref[...] = sent[HALO:]


def pack_kernel(factor_in, out_ref, factor_ref, sems):
    rows, columns = factor_ref.shape
    width = columns // 6
    copies = []
    for i in range(6):
        chunk = slice(i * width, (i + 1) * width)
        copies.append(
            pltpu.make_async_copy(factor_in.at[:, chunk], factor_ref.at[:, chunk], sems.at[i])
        )
        copies[i].start()
    lane = lax.broadcasted_iota(jnp.int32, (rows, LANES5), 1)
    for half in range(2):
        for i in range(3):
            copies[3 * half + i].wait()
        for x in range(NX):
            out_ref[2 * x + half, 24:, :] = jnp.zeros((8, NZ * LANES5), F32)
            for z in range(NZ):
                total = jnp.zeros((rows, LANES5), F32)
                for i in range(3):
                    start = (3 * half + i) * width + (z * NX + x) * C5
                    base, within = start // LANES5 * LANES5, start % LANES5
                    value = factor_ref[:, base : base + LANES5]
                    if within + C5 > LANES5:
                        after = factor_ref[:, base + LANES5 : base + 2 * LANES5]
                        value = jnp.where(lane >= within, value, after)
                    shift = (i * C5 - within) % LANES5
                    if shift:
                        value = pltpu.roll(value, shift, 1)
                    here = (lane >= i * C5) & (lane < (i + 1) * C5)
                    total = jnp.where(here, value, total)
                out_ref[2 * x + half, :rows, z * LANES5 : (z + 1) * LANES5] = total


def pack(factor, cost):
    shape = (2 * NX, 32, NZ * LANES5)
    return pl.pallas_call(
        pack_kernel,
        in_specs=[pl.BlockSpec(memory_space=pltpu.HBM)],
        out_specs=pl.BlockSpec(memory_space=pltpu.VMEM),
        out_shape=jax.ShapeDtypeStruct(shape, F32),
        scratch_shapes=[pltpu.VMEM(factor.shape, F32), pltpu.SemaphoreType.DMA((6,))],
        compiler_params=pltpu.CompilerParams(vmem_limit_bytes=LIMIT),
        cost_estimate=pl.CostEstimate(flops=1, bytes_accessed=cost, transcendentals=0),
    )(pltpu.with_memory_space_constraint(factor, pltpu.HBM))


def on_device(
    resid3, diag3, smooth3, off3, cols3, send3, prolong3, agg3,
    diag4, smooth4, off4, cols4, send4, prolong4, agg4, coarse_factor,
):
    groups, subs = lax.axis_size("grp"), lax.axis_size("sub")
    both = ("grp", "sub")
    devices = groups * subs
    mates = [(i, i ^ 1) for i in range(subs)]
    offs = [(i, i + 1) for i in range(1, devices - 1, 2)]
    offs = offs + [(j, i) for i, j in offs]
    fours = [
        (g * subs + 2 * y, (g + 1) * subs + 2 * y + 1)
        for g in range(groups - 1)
        for y in range(subs // 2)
    ]
    fours = fours + [(j, i) for i, j in fours]
    even = lax.axis_index("sub") % 2 == 0

    swapped = jnp.where(cols3 >= ROWS + HALO, cols3 - HALO, cols3 + HALO)
    columns = jnp.where(even & (cols3 >= ROWS), swapped, cols3).reshape(NOFF, 1, ROWS)
    index = jnp.where(even, send3[::-1], send3).reshape(2 * HALO, 1)
    agg = agg3.reshape(1, ROWS)
    swapped4 = jnp.where(cols4 >= FOUR + HALO4, cols4 - HALO4, cols4 + HALO4)
    columns4 = jnp.where(even & (cols4 >= FOUR), swapped4, cols4).reshape(1, NOFF * FOUR)
    columns4 = jnp.pad(columns4, ((0, 0), (0, WIDE4 - NOFF * FOUR)), constant_values=-1)
    index4 = jnp.where(even, send4[1], send4[0])
    index4 = jnp.pad(index4, (0, HALO4), constant_values=-1).reshape(2 * HALO4, 1)
    blocks4 = jnp.transpose(off4, (1, 2, 0, 3))
    inside4 = (agg4 - lax.axis_index("grp") * C5)[None, :]
    component = jnp.arange(6, dtype=jnp.int32)[:, None]
    half = lax.axis_index("sub") % 2
    lane = inside4 + component % 3 * C5
    here = component // 3 == half
    place = jnp.where(here, lane, -1).reshape(6 * FOUR, 1)
    place_back = (lane + component // 3 * LANES5).reshape(6, 1, FOUR)
    along_z = [[z * NX + x for z in range(NZ)] for x in range(NX)]
    along_x_core = [
        [(z * NX + x) * subs + 2 * y + c for x in range(NX) for c in range(2)]
        for z in range(NZ)
        for y in range(subs // 2)
    ]

    vector = (6, R, ROWS)
    halo = (HALO, 6 * R)
    vector4 = (6, R, FOUR)
    halo4 = (HALO4, 6 * R)
    cost = 8 * 1024 * 1024
    ends = jax.ShapeDtypeStruct((12 * HALO, 6 * ROWS), BF16)

    def exchange(mate, off):
        return lax.ppermute(mate, "sub", mates), lax.ppermute(off, both, offs)

    def exchange4(sent, vector):
        received = lax.ppermute(sent, both, fours)
        (own,) = call(
            own_four_kernel, [vector4], FOUR_SCRATCH, cost // 2, vector, diag4, blocks4, columns4
        )
        received, own = lax.optimization_barrier((received, own))
        return received, lax.ppermute(received, "sub", mates), own

    blocks3 = jnp.transpose(off3, (1, 2, 0, 3))
    once, mate, off = call(
        first_kernel, [vector, halo, halo], [], cost // 8, resid3, smooth3, index
    )
    mate, off = exchange(mate, off)
    high, low = call(ends_kernel, [ends, ends], [], cost, blocks3, columns)
    packed = pack(coarse_factor, cost)
    (own,) = call(own_kernel, [vector], OWN_SCRATCH, cost, once, diag3, blocks3, columns)
    mate, off, high, low, own, packed = lax.optimization_barrier(
        (mate, off, high, low, own, packed)
    )
    twice, mate, off = call(
        sweep_kernel, [vector, halo, halo], [], cost // 8,
        once, own, mate, off, high, low, resid3, smooth3, index,
    )
    mate, off = exchange(mate, off)
    packed, mate = lax.optimization_barrier((packed, mate))
    factor = lax.all_to_all(packed, both, 0, 0, axis_index_groups=along_x_core)
    (own,) = call(own_kernel, [vector], OWN_SCRATCH, cost, twice, diag3, blocks3, columns)
    (partial_four,) = call(
        restrict_kernel, [(FOUR, 6 * R)], [], cost // 8,
        own, mate, off, high, low, resid3, prolong3, agg,
    )
    ends4 = jax.ShapeDtypeStruct((12 * HALO4, 2 * 128), BF16)
    (blocks4,) = call(lay_four_kernel, [(6, 6, 8, 128)], [], cost // 4, blocks4)
    high4, low4 = call(ends_four_kernel, [ends4, ends4], [], cost // 4, blocks4, columns4)
    four = partial_four
    for step in (1, 2, 4):
        if step == 4:
            four, high4, low4, blocks4, columns4 = lax.optimization_barrier(
                (four, high4, low4, blocks4, columns4)
            )
        four = four + lax.ppermute(four, "sub", [(i, i ^ step) for i in range(subs)])
    rhs4, start4, sent = call(
        start_kernel, [vector4, vector4, halo4], [], cost // 8, four, smooth4, index4
    )
    first, second, own4 = exchange4(sent, start4)
    first, second, factor = lax.optimization_barrier((first, second, factor))
    (coarse,) = call(
        coarse_kernel, [(NZ, R, LANES5)], [], cost // 8,
        rhs4, own4, first, second, high4, low4, prolong4, place,
    )
    gathered = lax.all_to_all(coarse, "grp", 0, 0, axis_index_groups=along_z)
    (partial_projected,) = call(
        project_kernel, [(2 * NX, R, 2 * NX * 32)], [], cost // 2, gathered, factor
    )
    shares = lax.all_to_all(partial_projected, both, 0, 0, axis_index_groups=along_x_core)
    projected = jnp.sum(shares, axis=0)
    (partial_solved,) = call(
        solve_kernel, [(NZ, R, LANES5)], [], cost // 2, projected, factor
    )
    shares = lax.all_to_all(partial_solved, "grp", 0, 0, axis_index_groups=along_z)
    (partial_sums,) = call(sum_kernel, [(subs, R, LANES5)], [], cost // 8, shares)
    shares = lax.all_to_all(partial_sums, "sub", 0, 0)
    solved = jnp.sum(shares.reshape(subs // 2, 2, R, LANES5), axis=0)
    mid, sent = call(
        middle_kernel, [vector4, halo4], [], cost // 8,
        solved, start4, prolong4, place_back, index4,
    )
    first, second, own4 = exchange4(sent, mid)
    correction, refined, mate, off = call(
        correct_kernel, [vector4, vector, halo, halo], [], cost // 4,
        rhs4, mid, own4, first, second, high4, low4, smooth4, twice, prolong3, agg, index,
    )
    mate, off = exchange(mate, off)
    (own,) = call(own_kernel, [vector], OWN_SCRATCH, cost, refined, diag3, blocks3, columns)
    (result,) = call(
        last_kernel, [vector], [], cost // 8,
        refined, own, mate, off, high, low, resid3, smooth3,
    )
    return result, correction


def solution(mesh):
    split_rows = P(None, None, ("grp", "sub"))
    split_four = P(None, None, "grp")
    return jax.shard_map(
        on_device,
        mesh=mesh,
        in_specs=(
            split_rows,
            split_rows,
            split_rows,
            P(None, None, None, ("grp", "sub")),
            P(None, ("grp", "sub")),
            P(None, ("grp", "sub")),
            split_rows,
            P(("grp", "sub")),
            split_four,
            split_four,
            P(None, None, None, "grp"),
            P(None, "grp"),
            P(None, "grp"),
            split_four,
            P("grp"),
            P(("grp", "sub"), None),
        ),
        out_specs=(split_rows, split_four),
        check_vma=False,
    )
```

time: 131 us -> 121 us (0.924)
  starting transfers between devices: 41.4 us -> 36.3 us
  local copies, waits for them, and re-layouts: 5.48 us -> 2.04 us
  Pallas kernels: 16.8 us -> 19.8 us
  waiting for transfers between devices: 32.7 us -> 29.9 us
  blocking collectives: 32.2 us -> 30.6 us
    ppermute x6, starting transfers between devices: 19.4 us -> 15.7 us  [exchange(): return (lax.ppermute(mate, 'sub', mates), lax.ppermute(off, both, offs))]
    pallas_call x0 -> x1, Pallas kernels: none -> 3.06 us  [pack(): pl.pallas_call(pack_kernel, in_specs=[pl.BlockSpec(memory_space=pltpu.HBM...]
    unnamed x33 -> x32, local copies, waits for them, and re-layouts: 4.11 us -> 1.63 us
    ppermute x6, waiting for transfers between devices: 5.24 us -> 3.03 us  [exchange(): return (lax.ppermute(mate, 'sub', mates), lax.ppermute(off, both, offs))]
    all_to_all x2, blocking collectives: 32.2 us -> 30.6 us  [the longest x1 18.8 us: on_device(): gathered = lax.all_to_all(coarse, 'grp', 0, 0, axis_index_groups=along_z)]
    ppermute x2, waiting for transfers between devices: 6.07 us -> 4.69 us  [exchange4(): received = lax.ppermute(sent, both, fours)]
    pallas_call x11 -> x19, Pallas kernels: 16.8 us -> 16.8 us  [call(): pl.pallas_call(body, out_shape=out_shape, in_specs=[pl.BlockSpec(memory_s...]
  transfers between devices with their start and end apart: 16 -> 16, of which waited for: 12 -> 11; matrix products, arithmetic and copies ran while one was open for 2% -> 0% of each run, Pallas kernels for 4% -> 10%
where the time goes in v2:
time: 121 us; the launch traced here: 120 us
  starting transfers between devices  36.3 us (30%)
  blocking collectives  30.6 us (25%)
  waiting for transfers between devices  29.9 us (25%)
  Pallas kernels  19.8 us (16%)
  local copies, waits for them, and re-layouts  2.04 us (2%)
    all_to_all x1, blocking collectives, on_device(): gathered = lax.all_to_all(coarse, 'grp', 0, 0, axis_index_groups=along_z)  18.8 us
    pallas_call x19, Pallas kernels, call(): pl.pallas_call(body, out_shape=out_shape, in_specs=[pl.BlockSpec(memory_s...  16.8 us
    ppermute x6, starting transfers between devices, exchange(): return (lax.ppermute(mate, 'sub', mates), lax.ppermute(off, both, offs))  15.7 us
    all_to_all x1, blocking collectives, on_device(): lax.all_to_all(partial_projected, both, 0, 0, axis_index_groups=along_x_c...  11.7 us
    all_to_all x1, waiting for transfers between devices, on_device(): lax.all_to_all(partial_solved, 'grp', 0, 0, axis_index_groups=along_z)  7.28 us
    ppermute x3, waiting for transfers between devices, on_device(): lax.ppermute(four, 'sub', [(i, i ^ step) for i in range(subs)])  7.28 us
    all_to_all x1, waiting for transfers between devices, on_device(): shares = lax.all_to_all(partial_sums, 'sub', 0, 0)  6.06 us
    all_to_all x1, starting transfers between devices, on_device(): lax.all_to_all(partial_solved, 'grp', 0, 0, axis_index_groups=along_z)  4.73 us
  transfers between devices with their start and end apart: 16, of which 11 were waited for; matrix products, arithmetic and copies ran while one was open for 0% of the time, Pallas kernels for 10%

profile of v2, /device:TPU:32, one launch (start us, length us, event | category | flops | bytes accessed | tf_op | source)
XLA Modules:
  0.0 120.0 jit_solution(6809741568333788263)
XLA Ops:
  0.7 0.6 copy-done.13
  1.5 0.9 copy-done.1
  2.3 0.2 shard_map.167
  2.6 6.8 %collective-permute-start.1 = (f32[16,192]{1,0:T(8,128)S(1)}, f32[16,192]{1,0:T(8,128)S(1)}, u32[]{:S(2)}, u32[]{:S(2)}) collective-permute-start(f32[16,192]{1,0:T(8,128)S(1)} %get-tuple-element.43), channel_id=1, source_target_pairs={{1,2},{3,4},{5,6},{7,8},{9,10},{11,12},{13,14},{15,16},{17,18},{19... | collective-permute-start | bytes 36872 | tf_op jit(solution)/shard_map/ppermute | solution.py:448
  9.4 3.1 %shard_map.170 = f32[8,32,1024]{2,1,0:T(8,128)} custom-call(f32[30,7680]{1,0:T(8,128)} %factor_in.1), custom_call_target="tpu_custom_call" | custom-call | flops 1 | bytes 8388608 | tf_op jit(solution)/shard_map/pallas_call | solution.py:387
  12.5 1.7 %shard_map.168 = (bf16[192,768]{1,0:T(8,128)(2,1)S(1)}, bf16[192,768]{1,0:T(8,128)(2,1)S(1)}) custom-call(f32[6,6,26,128]{3,2,1,0:T(8,128)S(1)} %bitcast.8, s32[26,1,128]{2,1,0:T(1,128)S(1)} %reshape.164.cols_ref), custom_call_target="tpu_custom_call" | custom-call | flops 1 | bytes 8388608 | tf_op jit(solution)/shard_map/pallas_call | solution.py:30
  14.3 1.7 %shard_map.169.own_ref = f32[6,32,128]{2,1,0:T(8,128)S(1)} custom-call(f32[6,32,128]{2,1,0:T(8,128)S(1)} %get-tuple-element.41.vector_ref.once_ref, f32[6,6,128]{2,1,0:T(8,128)S(1)} %copy-done.4, f32[6,6,26,128]{3,2,1,0:T(8,128)S(1)} %bitcast.9, s32[26,1,128]{2,1,0:T(1,128)S(1)} %reshape.164.cols_ref), custom_call_target="tpu_custom_call" | custom-call | flops 1 | bytes 8388608 | tf_op jit(solution)/shard_map/pallas_call | solution.py:30
  16.0 0.6 shard_map.171
  16.8 3.0 %collective-permute-start.3 = (f32[16,192]{1,0:T(8,128)S(1)}, f32[16,192]{1,0:T(8,128)S(1)}, u32[]{:S(2)}, u32[]{:S(2)}) collective-permute-start(f32[16,192]{1,0:T(8,128)S(1)} %get-tuple-element.55), channel_id=1, source_target_pairs={{1,2},{3,4},{5,6},{7,8},{9,10},{11,12},{13,14},{15,16},{17,18},{19... | collective-permute-start | bytes 36872 | tf_op jit(solution)/shard_map/ppermute | solution.py:448
  19.8 3.6 %all-to-all-start = ((f32[8,32,1024]{2,1,0:T(8,128)}), f32[8,32,1024]{2,1,0:T(8,128)S(1)}, u32[]{:S(2)}, u32[]{:S(2)}) async-start(f32[8,32,1024]{2,1,0:T(8,128)} %shard_map.170), calls=%async_computation | async-start | bytes 2097152 | tf_op jit(solution)/shard_map/all_to_all | solution.py:475
  23.4 1.7 %shard_map.172.own_ref = f32[6,32,128]{2,1,0:T(8,128)S(1)} custom-call(f32[6,32,128]{2,1,0:T(8,128)S(1)} %get-tuple-element.51.vector_ref.twice_ref, f32[6,6,128]{2,1,0:T(8,128)S(1)} %copy-done.4, f32[6,6,26,128]{3,2,1,0:T(8,128)S(1)} %bitcast.10, s32[26,1,128]{2,1,0:T(1,128)S(1)} %reshape.164.cols_ref), custom_call_target="tpu_custom_call" | custom-call | flops 1 | bytes 8388608 | tf_op jit(solution)/shard_map/pallas_call | solution.py:30
  25.2 0.9 collective-permute-done.3.off_in
  26.0 0.6 shard_map.173
  26.8 0.2 shard_map.174.blocks_ref
  27.0 0.9 collective-permute-done.4
  27.9 0.2 collective-permute-start.5
  28.1 0.3 shard_map.175
  28.5 3.4 %collective-permute-done.5 = f32[32,192]{1,0:T(8,128)S(1)} collective-permute-done((f32[32,192]{1,0:T(8,128)S(1)}, f32[32,192]{1,0:T(8,128)S(1)}, u32[]{:S(2)}, u32[]{:S(2)}) %collective-permute-start.5) | collective-permute-done | bytes 24608 | tf_op jit(solution)/shard_map/ppermute | solution.py:490
  31.9 2.3 %collective-permute-start.6 = (f32[32,192]{1,0:T(8,128)S(1)}, f32[32,192]{1,0:T(8,128)S(1)}, u32[]{:S(2)}, u32[]{:S(2)}) collective-permute-start(f32[32,192]{1,0:T(8,128)S(1)} %add.100), channel_id=1, source_target_pairs={{0,4},{1,5},{2,6},{3,7},{4,0},{5,1},{6,2},{7,3},{8,12},{9,13},{10,... | collective-permute-start | bytes 73736 | tf_op jit(solution)/shard_map/ppermute | solution.py:490
  34.3 3.0 %collective-permute-done.6 = f32[32,192]{1,0:T(8,128)S(1)} collective-permute-done((f32[32,192]{1,0:T(8,128)S(1)}, f32[32,192]{1,0:T(8,128)S(1)}, u32[]{:S(2)}, u32[]{:S(2)}) %collective-permute-start.6) | collective-permute-done | bytes 24608 | tf_op jit(solution)/shard_map/ppermute | solution.py:490
  37.3 0.2 shard_map.176
  37.5 2.0 %collective-permute-start.7 = (f32[8,192]{1,0:T(8,128)S(1)}, f32[8,192]{1,0:T(8,128)S(1)}, u32[]{:S(2)}, u32[]{:S(2)}) collective-permute-start(f32[8,192]{1,0:T(8,128)S(1)} %get-tuple-element.60), channel_id=1, source_target_pairs={{0,9},{2,11},{4,13},{6,15},{8,17},{10,19},{12,21},{14,23},{16,25},... | collective-permute-start | bytes 18440 | tf_op jit(solution)/shard_map/ppermute | solution.py:451
  39.6 0.7 shard_map.177.own_ref
  40.2 2.3 %collective-permute-done.7.first_in = f32[8,192]{1,0:T(8,128)S(1)} collective-permute-done((f32[8,192]{1,0:T(8,128)S(1)}, f32[8,192]{1,0:T(8,128)S(1)}, u32[]{:S(2)}, u32[]{:S(2)}) %collective-permute-start.7) | collective-permute-done | bytes 6176 | tf_op jit(solution)/shard_map/ppermute | solution.py:451
  42.6 0.3 collective-permute-start.8
  43.0 0.7 collective-permute-done.8.second_in
  43.8 0.7 shard_map.178
  44.4 18.8 %all_to_all.25.coarse_ref = f32[8,32,128]{2,1,0:T(8,128)S(1)} all-to-all(f32[8,32,128]{2,1,0:T(8,128)S(1)} %shard_map.178), channel_id=1, replica_groups={{0,32,64,96,128,160,192,224},{8,40,72,104,136,168,200,232},{16,48,80,11..., dimensions={0} | all-to-all | bytes 262144 | tf_op jit(solution)/shard_map/all_to_all | solution.py:500
  63.3 1.1 shard_map.179
  64.4 11.7 %all_to_all.26 = f32[8,32,256]{2,1,0:T(8,128)S(1)} all-to-all(f32[8,32,256]{2,1,0:T(8,128)S(1)} %shard_map.179), channel_id=1, replica_groups={{0,1,8,9,16,17,24,25},{2,3,10,11,18,19,26,27},{4,5,12,13,20,21,28,29},{..., dimensions={0} | all-to-all | bytes 524288 | tf_op jit(solution)/shard_map/all_to_all | solution.py:504
  76.1 1.3 %shard_map.180 = f32[8,32,128]{2,1,0:T(8,128)} custom-call(f32[32,256]{1,0:T(8,128)S(1)} %reduce_sum.18.projected_ref, f32[8,32,1024]{2,1,0:T(8,128)S(1)} %all-to-all-done.factor_ref), custom_call_target="tpu_custom_call" | custom-call | flops 1 | bytes 4194304 | tf_op jit(solution)/shard_map/pallas_call | solution.py:30
  77.4 4.7 %all-to-all-start.3 = ((f32[8,32,128]{2,1,0:T(8,128)}), f32[8,32,128]{2,1,0:T(8,128)S(1)}, u32[]{:S(2)}, u32[]{:S(2)}) async-start(f32[8,32,128]{2,1,0:T(8,128)} %shard_map.180), calls=%async_computation.3 | async-start | bytes 262144 | tf_op jit(solution)/shard_map/all_to_all | solution.py:509
  82.2 7.3 %all-to-all-done.3.shares_ref = f32[8,32,128]{2,1,0:T(8,128)S(1)} async-done(((f32[8,32,128]{2,1,0:T(8,128)}), f32[8,32,128]{2,1,0:T(8,128)S(1)}, u32[]{:S(2)}, u32[]{:S(2)}) %all-to-all-start.3) | async-done | bytes 131104 | tf_op jit(solution)/shard_map/all_to_all | solution.py:509
  89.5 0.7 shard_map.181
  90.1 3.7 %all-to-all-start.4 = ((f32[8,32,128]{2,1,0:T(8,128)}), f32[8,32,128]{2,1,0:T(8,128)S(1)}, u32[]{:S(2)}, u32[]{:S(2)}) async-start(f32[8,32,128]{2,1,0:T(8,128)} %shard_map.181), calls=%async_computation.4 | async-start | bytes 262144 | tf_op jit(solution)/shard_map/all_to_all | solution.py:511
  93.9 6.1 %all-to-all-done.4 = f32[8,32,128]{2,1,0:T(8,128)S(1)} async-done(((f32[8,32,128]{2,1,0:T(8,128)}), f32[8,32,128]{2,1,0:T(8,128)S(1)}, u32[]{:S(2)}, u32[]{:S(2)}) %all-to-all-start.4) | async-done | bytes 131104 | tf_op jit(solution)/shard_map/all_to_all | solution.py:511
  100.0 0.4 shard_map.182
  100.4 2.0 %collective-permute-start.9 = (f32[8,192]{1,0:T(8,128)S(1)}, f32[8,192]{1,0:T(8,128)S(1)}, u32[]{:S(2)}, u32[]{:S(2)}) collective-permute-start(f32[8,192]{1,0:T(8,128)S(1)} %get-tuple-element.73), channel_id=1, source_target_pairs={{0,9},{2,11},{4,13},{6,15},{8,17},{10,19},{12,21},{14,23},{16,25},... | collective-permute-start | bytes 18440 | tf_op jit(solution)/shard_map/ppermute | solution.py:451
  102.4 0.7 shard_map.183.own_ref
  103.1 2.4 %collective-permute-done.9.first_in = f32[8,192]{1,0:T(8,128)S(1)} collective-permute-done((f32[8,192]{1,0:T(8,128)S(1)}, f32[8,192]{1,0:T(8,128)S(1)}, u32[]{:S(2)}, u32[]{:S(2)}) %collective-permute-start.9) | collective-permute-done | bytes 6176 | tf_op jit(solution)/shard_map/ppermute | solution.py:451
  105.5 1.8 %collective-permute-start.10 = (f32[8,192]{1,0:T(8,128)S(1)}, f32[8,192]{1,0:T(8,128)S(1)}, u32[]{:S(2)}, u32[]{:S(2)}) collective-permute-start(f32[8,192]{1,0:T(8,128)S(1)} %collective-permute-done.9.first_in), channel_id=1, source_target_pairs={{0,1},{1,0},{2,3},{3,2},{4,5},{5,4},{6,7},{7,6},{8,9},{9,8},{10,11... | collective-permute-start | bytes 18440 | tf_op jit(solution)/shard_map/ppermute | solution.py:456
  107.2 0.8 collective-permute-done.10.second_in
  108.0 1.3 %shard_map.184 = (f32[6,32,32]{2,1,0:T(8,128)}, f32[6,32,128]{2,1,0:T(8,128)S(1)}, f32[16,192]{1,0:T(8,128)S(1)}, f32[16,192]{1,0:T(8,128)S(1)}) custom-call(f32[6,32,32]{2,1,0:T(8,128)S(1)} %get-tuple-element.59.rhs_ref, f32[6,32,32]{2,1,0:T(8,128)S(1)} %get-tuple-element.72.vector_ref.mid_ref, f32[6,32,32]{2,1,0:T(8,128)S(1)} %shard_map.183.own_ref, ...), custom_call_target="tpu_custom_call" | custom-call | flops 1 | bytes 2097152 | tf_op jit(solution)/shard_map/pallas_call | solution.py:30
  109.3 0.3 collective-permute-start.11
  109.7 5.4 %collective-permute-start.12 = (f32[16,192]{1,0:T(8,128)S(1)}, f32[16,192]{1,0:T(8,128)S(1)}, u32[]{:S(2)}, u32[]{:S(2)}) collective-permute-start(f32[16,192]{1,0:T(8,128)S(1)} %get-tuple-element.78), channel_id=1, source_target_pairs={{1,2},{3,4},{5,6},{7,8},{9,10},{11,12},{13,14},{15,16},{17,18},{19... | collective-permute-start | bytes 36872 | tf_op jit(solution)/shard_map/ppermute | solution.py:448
  115.1 1.7 %shard_map.185.own_ref = f32[6,32,128]{2,1,0:T(8,128)S(1)} custom-call(f32[6,32,128]{2,1,0:T(8,128)S(1)} %get-tuple-element.76.vector_ref.refined_ref, f32[6,6,128]{2,1,0:T(8,128)S(1)} %copy-done.4, f32[6,6,26,128]{3,2,1,0:T(8,128)S(1)} %bitcast.11, s32[26,1,128]{2,1,0:T(1,128)S(1)} %reshape.164.cols_ref), custom_call_target="tpu_custom_call" | custom-call | flops 1 | bytes 8388608 | tf_op jit(solution)/shard_map/pallas_call | solution.py:30
  116.8 2.1 %collective-permute-done.12.off_in = f32[16,192]{1,0:T(8,128)S(1)} collective-permute-done((f32[16,192]{1,0:T(8,128)S(1)}, f32[16,192]{1,0:T(8,128)S(1)}, u32[]{:S(2)}, u32[]{:S(2)}) %collective-permute-start.12) | collective-permute-done | bytes 12320 | tf_op jit(solution)/shard_map/ppermute | solution.py:448
  118.9 1.1 shard_map.186
  (61 shorter events, 1.1 us)
Async XLA Ops:
  0.6 0.7 copy-start.13
  0.6 0.8 copy-start.5
  1.4 0.9 copy-start.1
  2.3 7.0 %copy-start.11 = (s32[26,128]{1,0:T(8,128)S(1)}, s32[26,128]{1,0:T(8,128)}, u32[]{:S(2)}) copy-start(s32[26,128]{1,0:T(8,128)} %param.20) | copy-start | bytes 39940
  2.5 13.5 %collective-permute-start = (f32[16,192]{1,0:T(8,128)S(1)}, f32[16,192]{1,0:T(8,128)S(1)}, u32[]{:S(2)}, u32[]{:S(2)}) collective-permute-start(f32[16,192]{1,0:T(8,128)S(1)} %get-tuple-element.42), channel_id=1, source_target_pairs={{0,1},{1,0},{2,3},{3,2},{4,5},{5,4},{6,7},{7,6},{8,9},{9,8},{10,11... | collective-permute-start | bytes 36872 | tf_op jit(solution)/shard_map/ppermute | solution.py:448
  2.6 13.4 %collective-permute-start.1 = (f32[16,192]{1,0:T(8,128)S(1)}, f32[16,192]{1,0:T(8,128)S(1)}, u32[]{:S(2)}, u32[]{:S(2)}) collective-permute-start(f32[16,192]{1,0:T(8,128)S(1)} %get-tuple-element.43), channel_id=1, source_target_pairs={{1,2},{3,4},{5,6},{7,8},{9,10},{11,12},{13,14},{15,16},{17,18},{19... | collective-permute-start | bytes 36872 | tf_op jit(solution)/shard_map/ppermute | solution.py:448
  9.4 3.1 %copy-start = (f32[26,6,6,128]{3,0,2,1:T(8,128)S(1)}, f32[26,6,6,128]{3,0,2,1:T(8,128)}, u32[]{:S(2)}) copy-start(f32[26,6,6,128]{3,0,2,1:T(8,128)} %param.19) | copy-start | bytes 1437700
  12.5 1.8 %copy-start.4 = (f32[6,6,128]{2,1,0:T(8,128)S(1)}, f32[6,6,128]{2,1,0:T(8,128)}, u32[]{:S(2)}) copy-start(f32[6,6,128]{2,1,0:T(8,128)} %diag_ref.9) | copy-start | bytes 55300
  14.3 1.8 %copy-start.2 = (f32[6,32,128]{2,1,0:T(8,128)S(1)}, f32[6,32,128]{2,1,0:T(8,128)}, u32[]{:S(2)}) copy-start(f32[6,32,128]{2,1,0:T(8,128)} %resid_ref.7) | copy-start | bytes 294916
  16.0 0.7 copy-start.12
  16.6 3.2 %collective-permute-start.2 = (f32[16,192]{1,0:T(8,128)S(1)}, f32[16,192]{1,0:T(8,128)S(1)}, u32[]{:S(2)}, u32[]{:S(2)}) collective-permute-start(f32[16,192]{1,0:T(8,128)S(1)} %get-tuple-element.53), channel_id=1, source_target_pairs={{0,1},{1,0},{2,3},{3,2},{4,5},{5,4},{6,7},{7,6},{8,9},{9,8},{10,11... | collective-permute-start | bytes 36872 | tf_op jit(solution)/shard_map/ppermute | solution.py:448
  16.7 6.6 %copy-start.14 = (s32[2,8]{1,0:T(2,128)S(1)}, s32[2,8]{1,0:T(2,128)}, u32[]{:S(2)}) copy-start(s32[2,8]{1,0:T(2,128)} %param.28) | copy-start | bytes 196
  16.8 9.3 %collective-permute-start.3 = (f32[16,192]{1,0:T(8,128)S(1)}, f32[16,192]{1,0:T(8,128)S(1)}, u32[]{:S(2)}, u32[]{:S(2)}) collective-permute-start(f32[16,192]{1,0:T(8,128)S(1)} %get-tuple-element.55), channel_id=1, source_target_pairs={{1,2},{3,4},{5,6},{7,8},{9,10},{11,12},{13,14},{15,16},{17,18},{19... | collective-permute-start | bytes 36872 | tf_op jit(solution)/shard_map/ppermute | solution.py:448
  19.8 24.0 %all-to-all-start = ((f32[8,32,1024]{2,1,0:T(8,128)}), f32[8,32,1024]{2,1,0:T(8,128)S(1)}, u32[]{:S(2)}, u32[]{:S(2)}) async-start(f32[8,32,1024]{2,1,0:T(8,128)} %shard_map.170), calls=%async_computation | async-start | bytes 2097152 | tf_op jit(solution)/shard_map/all_to_all | solution.py:475
  23.4 2.6 %copy-start.8 = (f32[6,6,128]{2,1,0:T(8,128)S(1)}, f32[6,6,128]{2,1,0:T(8,128)}, u32[]{:S(2)}) copy-start(f32[6,6,128]{2,1,0:T(8,128)} %prolong_ref.7) | copy-start | bytes 55300
  23.4 2.6 %copy-start.10 = (s32[128]{0:T(128)S(1)}, s32[128]{0:T(128)}, u32[]{:S(2)}) copy-start(s32[128]{0:T(128)} %param.23) | copy-start | bytes 1540
  25.1 1.6 %copy-start.3 = (f32[26,6,6,32]{3,0,2,1:T(8,128)S(1)}, f32[26,6,6,32]{3,0,2,1:T(8,128)}, u32[]{:S(2)}) copy-start(f32[26,6,6,32]{3,0,2,1:T(8,128)} %param.26) | copy-start | bytes 359428
  26.0 0.7 copy-start.15
  26.6 1.3 %collective-permute-start.4 = (f32[32,192]{1,0:T(8,128)S(1)}, f32[32,192]{1,0:T(8,128)S(1)}, u32[]{:S(2)}, u32[]{:S(2)}) collective-permute-start(f32[32,192]{1,0:T(8,128)S(1)} %shard_map.173), channel_id=1, source_target_pairs={{0,1},{1,0},{2,3},{3,2},{4,5},{5,4},{6,7},{7,6},{8,9},{9,8},{10,11... | collective-permute-start | bytes 73736 | tf_op jit(solution)/shard_map/ppermute | solution.py:490
  27.9 3.9 %collective-permute-start.5 = (f32[32,192]{1,0:T(8,128)S(1)}, f32[32,192]{1,0:T(8,128)S(1)}, u32[]{:S(2)}, u32[]{:S(2)}) collective-permute-start(f32[32,192]{1,0:T(8,128)S(1)} %add.99), channel_id=1, source_target_pairs={{0,2},{1,3},{2,0},{3,1},{4,6},{5,7},{6,4},{7,5},{8,10},{9,11},{10,... | collective-permute-start | bytes 73736 | tf_op jit(solution)/shard_map/ppermute | solution.py:490
  31.9 5.4 %collective-permute-start.6 = (f32[32,192]{1,0:T(8,128)S(1)}, f32[32,192]{1,0:T(8,128)S(1)}, u32[]{:S(2)}, u32[]{:S(2)}) collective-permute-start(f32[32,192]{1,0:T(8,128)S(1)} %add.100), channel_id=1, source_target_pairs={{0,4},{1,5},{2,6},{3,7},{4,0},{5,1},{6,2},{7,3},{8,12},{9,13},{10,... | collective-permute-start | bytes 73736 | tf_op jit(solution)/shard_map/ppermute | solution.py:490
  34.3 3.0 %copy-start.9 = (f32[6,6,32]{2,1,0:T(8,128)S(1)}, f32[6,6,32]{2,1,0:T(8,128)}, u32[]{:S(2)}) copy-start(f32[6,6,32]{2,1,0:T(8,128)} %smooth4_ref.1) | copy-start | bytes 13828
  37.3 2.3 %copy-start.7 = (f32[6,6,32]{2,1,0:T(8,128)S(1)}, f32[6,6,32]{2,1,0:T(8,128)}, u32[]{:S(2)}) copy-start(f32[6,6,32]{2,1,0:T(8,128)} %diag_ref.8) | copy-start | bytes 13828
  37.5 5.0 %collective-permute-start.7 = (f32[8,192]{1,0:T(8,128)S(1)}, f32[8,192]{1,0:T(8,128)S(1)}, u32[]{:S(2)}, u32[]{:S(2)}) collective-permute-start(f32[8,192]{1,0:T(8,128)S(1)} %get-tuple-element.60), channel_id=1, source_target_pairs={{0,9},{2,11},{4,13},{6,15},{8,17},{10,19},{12,21},{14,23},{16,25},... | collective-permute-start | bytes 18440 | tf_op jit(solution)/shard_map/ppermute | solution.py:451
  42.6 1.2 collective-permute-start.8
  42.9 0.8 copy-start.6
  77.4 12.0 %all-to-all-start.3 = ((f32[8,32,128]{2,1,0:T(8,128)}), f32[8,32,128]{2,1,0:T(8,128)S(1)}, u32[]{:S(2)}, u32[]{:S(2)}) async-start(f32[8,32,128]{2,1,0:T(8,128)} %shard_map.180), calls=%async_computation.3 | async-start | bytes 262144 | tf_op jit(solution)/shard_map/all_to_all | solution.py:509
  90.1 9.8 %all-to-all-start.4 = ((f32[8,32,128]{2,1,0:T(8,128)}), f32[8,32,128]{2,1,0:T(8,128)S(1)}, u32[]{:S(2)}, u32[]{:S(2)}) async-start(f32[8,32,128]{2,1,0:T(8,128)} %shard_map.181), calls=%async_computation.4 | async-start | bytes 262144 | tf_op jit(solution)/shard_map/all_to_all | solution.py:511
  100.4 5.0 %collective-permute-start.9 = (f32[8,192]{1,0:T(8,128)S(1)}, f32[8,192]{1,0:T(8,128)S(1)}, u32[]{:S(2)}, u32[]{:S(2)}) collective-permute-start(f32[8,192]{1,0:T(8,128)S(1)} %get-tuple-element.73), channel_id=1, source_target_pairs={{0,9},{2,11},{4,13},{6,15},{8,17},{10,19},{12,21},{14,23},{16,25},... | collective-permute-start | bytes 18440 | tf_op jit(solution)/shard_map/ppermute | solution.py:451
  105.5 2.6 %collective-permute-start.10 = (f32[8,192]{1,0:T(8,128)S(1)}, f32[8,192]{1,0:T(8,128)S(1)}, u32[]{:S(2)}, u32[]{:S(2)}) collective-permute-start(f32[8,192]{1,0:T(8,128)S(1)} %collective-permute-done.9.first_in), channel_id=1, source_target_pairs={{0,1},{1,0},{2,3},{3,2},{4,5},{5,4},{6,7},{7,6},{8,9},{9,8},{10,11... | collective-permute-start | bytes 18440 | tf_op jit(solution)/shard_map/ppermute | solution.py:456
  109.3 7.5 %collective-permute-start.11 = (f32[16,192]{1,0:T(8,128)S(1)}, f32[16,192]{1,0:T(8,128)S(1)}, u32[]{:S(2)}, u32[]{:S(2)}) collective-permute-start(f32[16,192]{1,0:T(8,128)S(1)} %get-tuple-element.77), channel_id=1, source_target_pairs={{0,1},{1,0},{2,3},{3,2},{4,5},{5,4},{6,7},{7,6},{8,9},{9,8},{10,11... | collective-permute-start | bytes 36872 | tf_op jit(solution)/shard_map/ppermute | solution.py:448
  109.7 9.3 %collective-permute-start.12 = (f32[16,192]{1,0:T(8,128)S(1)}, f32[16,192]{1,0:T(8,128)S(1)}, u32[]{:S(2)}, u32[]{:S(2)}) collective-permute-start(f32[16,192]{1,0:T(8,128)S(1)} %get-tuple-element.78), channel_id=1, source_target_pairs={{1,2},{3,4},{5,6},{7,8},{9,10},{11,12},{13,14},{15,16},{17,18},{19... | collective-permute-start | bytes 36872 | tf_op jit(solution)/shard_map/ppermute | solution.py:448

commit v3 on v2

--- a/solution.py
+++ b/solution.py
@@ -108,8 +108,7 @@
 ]
 
 
-def own_kernel(vector_ref, diag_ref, blocks_ref, cols_ref, out_ref, parts_ref, picked_ref):
-    vectors = rows_of(vector_ref)
+def own_pick(vectors, cols_ref, parts_ref, picked_ref):
     parts_ref[...] = jnp.concatenate(split(flat(vectors)), axis=1)
     for pair in range(PAIRS):
         selector = jnp.concatenate(
@@ -117,6 +116,9 @@
         )
         stacked = jnp.concatenate([selector] * 3, axis=0)
         picked_ref[pair] = jnp.dot(parts_ref[...], stacked, preferred_element_type=F32)
+
+
+def own_add(vectors, diag_ref, blocks_ref, picked_ref, out_ref):
     totals = blockmul(diag_ref, vectors)
     for k in range(NOFF):
         lanes = slice(k % 2 * ROWS, (k % 2 + 1) * ROWS)
@@ -125,6 +127,12 @@
             for i in range(6):
                 totals[i] = totals[i] + blocks_ref[i, j, k : k + 1, :] * value
     put(out_ref, totals)
+
+
+def own_kernel(vector_ref, diag_ref, blocks_ref, cols_ref, out_ref, parts_ref, picked_ref):
+    vectors = rows_of(vector_ref)
+    own_pick(vectors, cols_ref, parts_ref, picked_ref)
+    own_add(vectors, diag_ref, blocks_ref, picked_ref, out_ref)
 
 
 def ends_kernel(blocks_ref, cols_ref, high_ref, low_ref):
@@ -349,20 +357,11 @@
     off_ref[...] = sent[HALO:]
 
 
-def pack_kernel(factor_in, out_ref, factor_ref, sems):
+def pack_columns(factor_ref, out_ref):
     rows, columns = factor_ref.shape
     width = columns // 6
-    copies = []
-    for i in range(6):
-        chunk = slice(i * width, (i + 1) * width)
-        copies.append(
-            pltpu.make_async_copy(factor_in.at[:, chunk], factor_ref.at[:, chunk], sems.at[i])
-        )
-        copies[i].start()
     lane = lax.broadcasted_iota(jnp.int32, (rows, LANES5), 1)
     for half in range(2):
-        for i in range(3):
-            copies[3 * half + i].wait()
         for x in range(NX):
             out_ref[2 * x + half, 24:, :] = jnp.zeros((8, NZ * LANES5), F32)
             for z in range(NZ):
@@ -382,17 +381,53 @@
                 out_ref[2 * x + half, :rows, z * LANES5 : (z + 1) * LANES5] = total
 
 
-def pack(factor, cost):
-    shape = (2 * NX, 32, NZ * LANES5)
+def window_kernel(
+    vector_ref, cols_ref, diag_in, blocks_in, factor_in,
+    own_ref, high_ref, low_ref, packed_out,
+    parts_ref, picked_ref, diag_ref, blocks_ref, factor_ref, packed_ref, sems
+):
+    fetches = [
+        pltpu.make_async_copy(source, target, sems.at[k])
+        for k, (source, target) in enumerate(
+            [(blocks_in, blocks_ref), (diag_in, diag_ref), (factor_in, factor_ref)]
+        )
+    ]
+    for fetch in fetches:
+        fetch.start()
+    vectors = rows_of(vector_ref)
+    own_pick(vectors, cols_ref, parts_ref, picked_ref)
+    for fetch in fetches:
+        fetch.wait()
+    pack_columns(factor_ref, packed_ref)
+    store = pltpu.make_async_copy(packed_ref, packed_out, sems.at[3])
+    store.start()
+    ends_kernel(blocks_ref, cols_ref, high_ref, low_ref)
+    own_add(vectors, diag_ref, blocks_ref, picked_ref, own_ref)
+    store.wait()
+
+
+def window(cost, vector, diagonal, blocks, columns, factor):
+    ends = jax.ShapeDtypeStruct((12 * HALO, 6 * ROWS), BF16)
+    packed = (2 * NX, 32, NZ * LANES5)
+    vmem = pl.BlockSpec(memory_space=pltpu.VMEM)
+    hbm = pl.BlockSpec(memory_space=pltpu.HBM)
     return pl.pallas_call(
-        pack_kernel,
-        in_specs=[pl.BlockSpec(memory_space=pltpu.HBM)],
-        out_specs=pl.BlockSpec(memory_space=pltpu.VMEM),
-        out_shape=jax.ShapeDtypeStruct(shape, F32),
-        scratch_shapes=[pltpu.VMEM(factor.shape, F32), pltpu.SemaphoreType.DMA((6,))],
+        window_kernel,
+        in_specs=[vmem] * 2 + [hbm] * 3,
+        out_specs=[vmem] * 3 + [hbm],
+        out_shape=[
+            jax.ShapeDtypeStruct(vector.shape, F32), ends, ends, jax.ShapeDtypeStruct(packed, F32)
+        ],
+        scratch_shapes=OWN_SCRATCH
+        + [pltpu.VMEM(x.shape, F32) for x in (diagonal, blocks, factor)]
+        + [pltpu.VMEM(packed, F32), pltpu.SemaphoreType.DMA((4,))],
         compiler_params=pltpu.CompilerParams(vmem_limit_bytes=LIMIT),
-        cost_estimate=pl.CostEstimate(flops=1, bytes_accessed=cost, transcendentals=0),
-    )(pltpu.with_memory_space_constraint(factor, pltpu.HBM))
+        cost_estimate=pl.CostEstimate(flops=1, bytes_accessed=2 * cost, transcendentals=0),
+    )(
+        vector,
+        columns,
+        *[pltpu.with_memory_space_constraint(x, pltpu.HBM) for x in (diagonal, blocks, factor)],
+    )
 
 
 def on_device(
@@ -442,7 +477,6 @@
     vector4 = (6, R, FOUR)
     halo4 = (HALO4, 6 * R)
     cost = 8 * 1024 * 1024
-    ends = jax.ShapeDtypeStruct((12 * HALO, 6 * ROWS), BF16)
 
     def exchange(mate, off):
         return lax.ppermute(mate, "sub", mates), lax.ppermute(off, both, offs)
@@ -460,9 +494,7 @@
         first_kernel, [vector, halo, halo], [], cost // 8, resid3, smooth3, index
     )
     mate, off = exchange(mate, off)
-    high, low = call(ends_kernel, [ends, ends], [], cost, blocks3, columns)
-    packed = pack(coarse_factor, cost)
-    (own,) = call(own_kernel, [vector], OWN_SCRATCH, cost, once, diag3, blocks3, columns)
+    own, high, low, packed = window(cost, once, diag3, blocks3, columns, coarse_factor)
     mate, off, high, low, own, packed = lax.optimization_barrier(
         (mate, off, high, low, own, packed)
     )

time: 121 us -> 120 us (level)
  waiting for transfers between devices: 29.9 us -> 28.6 us
    pallas_call x19 -> x17, Pallas kernels: 16.8 us -> 13.3 us  [call(): pl.pallas_call(body, out_shape=out_shape, in_specs=[pl.BlockSpec(memory_s...]
    pallas_call x1, Pallas kernels: 3.06 us -> 5.41 us  [window(): pl.pallas_call(window_kernel, in_specs=[vmem] * 2 + [hbm] * 3, out_specs=...]
where the time goes in v3:
time: 120 us; the launch traced here: 119 us
  starting transfers between devices  37.4 us (31%)
  blocking collectives  31.2 us (26%)
  waiting for transfers between devices  28.6 us (24%)
  Pallas kernels  18.7 us (16%)
  local copies, waits for them, and re-layouts  2.04 us (2%)
    all_to_all x1, blocking collectives, on_device(): gathered = lax.all_to_all(coarse, 'grp', 0, 0, axis_index_groups=along_z)  18.9 us
    ppermute x6, starting transfers between devices, exchange(): return (lax.ppermute(mate, 'sub', mates), lax.ppermute(off, both, offs))  16.5 us
    pallas_call x17, Pallas kernels, call(): pl.pallas_call(body, out_shape=out_shape, in_specs=[pl.BlockSpec(memory_s...  13.3 us
    all_to_all x1, blocking collectives, on_device(): lax.all_to_all(partial_projected, both, 0, 0, axis_index_groups=along_x_c...  12.3 us
    all_to_all x1, waiting for transfers between devices, on_device(): lax.all_to_all(partial_solved, 'grp', 0, 0, axis_index_groups=along_z)  7.28 us
    ppermute x3, waiting for transfers between devices, on_device(): lax.ppermute(four, 'sub', [(i, i ^ step) for i in range(subs)])  6.92 us
    all_to_all x1, waiting for transfers between devices, on_device(): shares = lax.all_to_all(partial_sums, 'sub', 0, 0)  5.98 us
    pallas_call x1, Pallas kernels, window(): pl.pallas_call(window_kernel, in_specs=[vmem] * 2 + [hbm] * 3, out_specs=...  5.41 us
  transfers between devices with their start and end apart: 16, of which 11 were waited for; matrix products, arithmetic and copies ran while one was open for 0% of the time, Pallas kernels for 10%

profile of v3, /device:TPU:32, one launch (start us, length us, event | category | flops | bytes accessed | tf_op | source)
XLA Modules:
  0.0 119.3 jit_solution(8707910928093628534)
XLA Ops:
  0.7 0.6 copy-done.13
  1.5 0.9 copy-done.1
  2.3 0.2 shard_map.167
  2.6 6.8 %collective-permute-start.1 = (f32[16,192]{1,0:T(8,128)S(1)}, f32[16,192]{1,0:T(8,128)S(1)}, u32[]{:S(2)}, u32[]{:S(2)}) collective-permute-start(f32[16,192]{1,0:T(8,128)S(1)} %get-tuple-element.45), channel_id=1, source_target_pairs={{1,2},{3,4},{5,6},{7,8},{9,10},{11,12},{13,14},{15,16},{17,18},{19... | collective-permute-start | bytes 36872 | tf_op jit(solution)/shard_map/ppermute | solution.py:482
  9.4 5.4 %shard_map.168 = (f32[6,32,128]{2,1,0:T(8,128)S(1)}, bf16[192,768]{1,0:T(8,128)(2,1)S(1)}, bf16[192,768]{1,0:T(8,128)(2,1)S(1)}, f32[8,32,1024]{2,1,0:T(8,128)}) custom-call(f32[6,32,128]{2,1,0:T(8,128)S(1)} %get-tuple-element.43.vector_ref.once_ref, s32[26,1,128]{2,1,0:T(1,128)S(1)} %reshape.164.cols_ref, f32[6,6,128]{2,1,0:T(8,128)} %diag_ref.7, ...), custom_call_target="tpu_custom_call" | custom-call | flops 1 | bytes 16777216 | tf_op jit(solution)/shard_map/pallas_call | solution.py:414
  14.9 0.6 shard_map.169
  15.6 3.9 %collective-permute-start.3 = (f32[16,192]{1,0:T(8,128)S(1)}, f32[16,192]{1,0:T(8,128)S(1)}, u32[]{:S(2)}, u32[]{:S(2)}) collective-permute-start(f32[16,192]{1,0:T(8,128)S(1)} %get-tuple-element.59), channel_id=1, source_target_pairs={{1,2},{3,4},{5,6},{7,8},{9,10},{11,12},{13,14},{15,16},{17,18},{19... | collective-permute-start | bytes 36872 | tf_op jit(solution)/shard_map/ppermute | solution.py:482
  19.5 3.6 %all-to-all-start = ((f32[8,32,1024]{2,1,0:T(8,128)}), f32[8,32,1024]{2,1,0:T(8,128)S(1)}, u32[]{:S(2)}, u32[]{:S(2)}) async-start(f32[8,32,1024]{2,1,0:T(8,128)} %get-tuple-element.70), calls=%async_computation | async-start | bytes 2097152 | tf_op jit(solution)/shard_map/all_to_all | solution.py:507
  23.2 1.7 %shard_map.170.own_ref = f32[6,32,128]{2,1,0:T(8,128)S(1)} custom-call(f32[6,32,128]{2,1,0:T(8,128)S(1)} %get-tuple-element.55.vector_ref.twice_ref, f32[6,6,128]{2,1,0:T(8,128)S(1)} %copy-done.4, f32[6,6,26,128]{3,2,1,0:T(8,128)S(1)} %bitcast.9, s32[26,1,128]{2,1,0:T(1,128)S(1)} %reshape.164.cols_ref), custom_call_target="tpu_custom_call" | custom-call | flops 1 | bytes 8388608 | tf_op jit(solution)/shard_map/pallas_call | solution.py:30
  24.9 0.1 collective-permute-done.3.off_in
  25.0 0.6 shard_map.171
  25.6 0.4 collective-permute-start.4
  26.0 0.2 shard_map.172.blocks_ref
  26.3 0.6 collective-permute-done.4
  26.9 0.2 collective-permute-start.5
  27.2 0.3 shard_map.173
  27.5 3.3 %collective-permute-done.5 = f32[32,192]{1,0:T(8,128)S(1)} collective-permute-done((f32[32,192]{1,0:T(8,128)S(1)}, f32[32,192]{1,0:T(8,128)S(1)}, u32[]{:S(2)}, u32[]{:S(2)}) %collective-permute-start.5) | collective-permute-done | bytes 24608 | tf_op jit(solution)/shard_map/ppermute | solution.py:522
  30.8 2.4 %collective-permute-start.6 = (f32[32,192]{1,0:T(8,128)S(1)}, f32[32,192]{1,0:T(8,128)S(1)}, u32[]{:S(2)}, u32[]{:S(2)}) collective-permute-start(f32[32,192]{1,0:T(8,128)S(1)} %add.100), channel_id=1, source_target_pairs={{0,4},{1,5},{2,6},{3,7},{4,0},{5,1},{6,2},{7,3},{8,12},{9,13},{10,... | collective-permute-start | bytes 73736 | tf_op jit(solution)/shard_map/ppermute | solution.py:522
  33.3 3.0 %collective-permute-done.6 = f32[32,192]{1,0:T(8,128)S(1)} collective-permute-done((f32[32,192]{1,0:T(8,128)S(1)}, f32[32,192]{1,0:T(8,128)S(1)}, u32[]{:S(2)}, u32[]{:S(2)}) %collective-permute-start.6) | collective-permute-done | bytes 24608 | tf_op jit(solution)/shard_map/ppermute | solution.py:522
  36.3 0.2 shard_map.174
  36.5 2.0 %collective-permute-start.7 = (f32[8,192]{1,0:T(8,128)S(1)}, f32[8,192]{1,0:T(8,128)S(1)}, u32[]{:S(2)}, u32[]{:S(2)}) collective-permute-start(f32[8,192]{1,0:T(8,128)S(1)} %get-tuple-element.64), channel_id=1, source_target_pairs={{0,9},{2,11},{4,13},{6,15},{8,17},{10,19},{12,21},{14,23},{16,25},... | collective-permute-start | bytes 18440 | tf_op jit(solution)/shard_map/ppermute | solution.py:485
  38.6 0.7 shard_map.175.own_ref
  39.2 2.3 %collective-permute-done.7.first_in = f32[8,192]{1,0:T(8,128)S(1)} collective-permute-done((f32[8,192]{1,0:T(8,128)S(1)}, f32[8,192]{1,0:T(8,128)S(1)}, u32[]{:S(2)}, u32[]{:S(2)}) %collective-permute-start.7) | collective-permute-done | bytes 6176 | tf_op jit(solution)/shard_map/ppermute | solution.py:485
  41.6 0.4 collective-permute-start.8
  42.1 0.1 select_n.99.place_ref
  42.2 0.6 collective-permute-done.8.second_in
  42.8 0.7 shard_map.176
  43.5 18.9 %all_to_all.25.coarse_ref = f32[8,32,128]{2,1,0:T(8,128)S(1)} all-to-all(f32[8,32,128]{2,1,0:T(8,128)S(1)} %shard_map.176), channel_id=1, replica_groups={{0,32,64,96,128,160,192,224},{8,40,72,104,136,168,200,232},{16,48,80,11..., dimensions={0} | all-to-all | bytes 262144 | tf_op jit(solution)/shard_map/all_to_all | solution.py:532
  62.4 1.1 shard_map.177
  63.5 12.3 %all_to_all.26 = f32[8,32,256]{2,1,0:T(8,128)S(1)} all-to-all(f32[8,32,256]{2,1,0:T(8,128)S(1)} %shard_map.177), channel_id=1, replica_groups={{0,1,8,9,16,17,24,25},{2,3,10,11,18,19,26,27},{4,5,12,13,20,21,28,29},{..., dimensions={0} | all-to-all | bytes 524288 | tf_op jit(solution)/shard_map/all_to_all | solution.py:536
  75.9 1.3 %shard_map.178 = f32[8,32,128]{2,1,0:T(8,128)} custom-call(f32[32,256]{1,0:T(8,128)S(1)} %reduce_sum.18.projected_ref, f32[8,32,1024]{2,1,0:T(8,128)S(1)} %all-to-all-done.factor_ref), custom_call_target="tpu_custom_call" | custom-call | flops 1 | bytes 4194304 | tf_op jit(solution)/shard_map/pallas_call | solution.py:30
  77.2 4.7 %all-to-all-start.3 = ((f32[8,32,128]{2,1,0:T(8,128)}), f32[8,32,128]{2,1,0:T(8,128)S(1)}, u32[]{:S(2)}, u32[]{:S(2)}) async-start(f32[8,32,128]{2,1,0:T(8,128)} %shard_map.178), calls=%async_computation.3 | async-start | bytes 262144 | tf_op jit(solution)/shard_map/all_to_all | solution.py:541
  81.9 7.3 %all-to-all-done.3.shares_ref = f32[8,32,128]{2,1,0:T(8,128)S(1)} async-done(((f32[8,32,128]{2,1,0:T(8,128)}), f32[8,32,128]{2,1,0:T(8,128)S(1)}, u32[]{:S(2)}, u32[]{:S(2)}) %all-to-all-start.3) | async-done | bytes 131104 | tf_op jit(solution)/shard_map/all_to_all | solution.py:541
  89.2 0.7 shard_map.179
  89.9 3.4 %all-to-all-start.4 = ((f32[8,32,128]{2,1,0:T(8,128)}), f32[8,32,128]{2,1,0:T(8,128)S(1)}, u32[]{:S(2)}, u32[]{:S(2)}) async-start(f32[8,32,128]{2,1,0:T(8,128)} %shard_map.179), calls=%async_computation.4 | async-start | bytes 262144 | tf_op jit(solution)/shard_map/all_to_all | solution.py:543
  93.3 6.0 %all-to-all-done.4 = f32[8,32,128]{2,1,0:T(8,128)S(1)} async-done(((f32[8,32,128]{2,1,0:T(8,128)}), f32[8,32,128]{2,1,0:T(8,128)S(1)}, u32[]{:S(2)}, u32[]{:S(2)}) %all-to-all-start.4) | async-done | bytes 131104 | tf_op jit(solution)/shard_map/all_to_all | solution.py:543
  99.3 0.4 shard_map.180
  99.8 2.0 %collective-permute-start.9 = (f32[8,192]{1,0:T(8,128)S(1)}, f32[8,192]{1,0:T(8,128)S(1)}, u32[]{:S(2)}, u32[]{:S(2)}) collective-permute-start(f32[8,192]{1,0:T(8,128)S(1)} %get-tuple-element.77), channel_id=1, source_target_pairs={{0,9},{2,11},{4,13},{6,15},{8,17},{10,19},{12,21},{14,23},{16,25},... | collective-permute-start | bytes 18440 | tf_op jit(solution)/shard_map/ppermute | solution.py:485
  101.8 0.7 shard_map.181.own_ref
  102.4 2.4 %collective-permute-done.9.first_in = f32[8,192]{1,0:T(8,128)S(1)} collective-permute-done((f32[8,192]{1,0:T(8,128)S(1)}, f32[8,192]{1,0:T(8,128)S(1)}, u32[]{:S(2)}, u32[]{:S(2)}) %collective-permute-start.9) | collective-permute-done | bytes 6176 | tf_op jit(solution)/shard_map/ppermute | solution.py:485
  104.8 1.8 %collective-permute-start.10 = (f32[8,192]{1,0:T(8,128)S(1)}, f32[8,192]{1,0:T(8,128)S(1)}, u32[]{:S(2)}, u32[]{:S(2)}) collective-permute-start(f32[8,192]{1,0:T(8,128)S(1)} %collective-permute-done.9.first_in), channel_id=1, source_target_pairs={{0,1},{1,0},{2,3},{3,2},{4,5},{5,4},{6,7},{7,6},{8,9},{9,8},{10,11... | collective-permute-start | bytes 18440 | tf_op jit(solution)/shard_map/ppermute | solution.py:490
  106.6 0.8 collective-permute-done.10.second_in
  107.4 1.3 %shard_map.182 = (f32[6,32,32]{2,1,0:T(8,128)}, f32[6,32,128]{2,1,0:T(8,128)S(1)}, f32[16,192]{1,0:T(8,128)S(1)}, f32[16,192]{1,0:T(8,128)S(1)}) custom-call(f32[6,32,32]{2,1,0:T(8,128)S(1)} %get-tuple-element.63.rhs_ref, f32[6,32,32]{2,1,0:T(8,128)S(1)} %get-tuple-element.76.vector_ref.mid_ref, f32[6,32,32]{2,1,0:T(8,128)S(1)} %shard_map.181.own_ref, ...), custom_call_target="tpu_custom_call" | custom-call | flops 1 | bytes 2097152 | tf_op jit(solution)/shard_map/pallas_call | solution.py:30
  108.7 0.3 collective-permute-start.11
  109.0 5.4 %collective-permute-start.12 = (f32[16,192]{1,0:T(8,128)S(1)}, f32[16,192]{1,0:T(8,128)S(1)}, u32[]{:S(2)}, u32[]{:S(2)}) collective-permute-start(f32[16,192]{1,0:T(8,128)S(1)} %get-tuple-element.82), channel_id=1, source_target_pairs={{1,2},{3,4},{5,6},{7,8},{9,10},{11,12},{13,14},{15,16},{17,18},{19... | collective-permute-start | bytes 36872 | tf_op jit(solution)/shard_map/ppermute | solution.py:482
  114.4 1.7 %shard_map.183.own_ref = f32[6,32,128]{2,1,0:T(8,128)S(1)} custom-call(f32[6,32,128]{2,1,0:T(8,128)S(1)} %get-tuple-element.80.vector_ref.refined_ref, f32[6,6,128]{2,1,0:T(8,128)S(1)} %copy-done.4, f32[6,6,26,128]{3,2,1,0:T(8,128)S(1)} %bitcast.10, s32[26,1,128]{2,1,0:T(1,128)S(1)} %reshape.164.cols_ref), custom_call_target="tpu_custom_call" | custom-call | flops 1 | bytes 8388608 | tf_op jit(solution)/shard_map/pallas_call | solution.py:30
  116.1 2.2 %collective-permute-done.12.off_in = f32[16,192]{1,0:T(8,128)S(1)} collective-permute-done((f32[16,192]{1,0:T(8,128)S(1)}, f32[16,192]{1,0:T(8,128)S(1)}, u32[]{:S(2)}, u32[]{:S(2)}) %collective-permute-start.12) | collective-permute-done | bytes 12320 | tf_op jit(solution)/shard_map/ppermute | solution.py:482
  118.3 1.1 shard_map.184
  (59 shorter events, 0.9 us)
Async XLA Ops:
  0.6 0.7 copy-start.13
  0.6 0.8 copy-start.5
  1.4 0.9 copy-start.1
  2.3 7.0 %copy-start.11 = (s32[26,128]{1,0:T(8,128)S(1)}, s32[26,128]{1,0:T(8,128)}, u32[]{:S(2)}) copy-start(s32[26,128]{1,0:T(8,128)} %param.20) | copy-start | bytes 39940
  2.5 12.3 %collective-permute-start = (f32[16,192]{1,0:T(8,128)S(1)}, f32[16,192]{1,0:T(8,128)S(1)}, u32[]{:S(2)}, u32[]{:S(2)}) collective-permute-start(f32[16,192]{1,0:T(8,128)S(1)} %get-tuple-element.44), channel_id=1, source_target_pairs={{0,1},{1,0},{2,3},{3,2},{4,5},{5,4},{6,7},{7,6},{8,9},{9,8},{10,11... | collective-permute-start | bytes 36872 | tf_op jit(solution)/shard_map/ppermute | solution.py:482
  2.6 12.2 %collective-permute-start.1 = (f32[16,192]{1,0:T(8,128)S(1)}, f32[16,192]{1,0:T(8,128)S(1)}, u32[]{:S(2)}, u32[]{:S(2)}) collective-permute-start(f32[16,192]{1,0:T(8,128)S(1)} %get-tuple-element.45), channel_id=1, source_target_pairs={{1,2},{3,4},{5,6},{7,8},{9,10},{11,12},{13,14},{15,16},{17,18},{19... | collective-permute-start | bytes 36872 | tf_op jit(solution)/shard_map/ppermute | solution.py:482
  9.4 5.5 %copy-start.2 = (f32[6,32,128]{2,1,0:T(8,128)S(1)}, f32[6,32,128]{2,1,0:T(8,128)}, u32[]{:S(2)}) copy-start(f32[6,32,128]{2,1,0:T(8,128)} %resid_ref.7) | copy-start | bytes 294916
  14.9 0.7 copy-start.12
  15.5 4.1 %collective-permute-start.2 = (f32[16,192]{1,0:T(8,128)S(1)}, f32[16,192]{1,0:T(8,128)S(1)}, u32[]{:S(2)}, u32[]{:S(2)}) collective-permute-start(f32[16,192]{1,0:T(8,128)S(1)} %get-tuple-element.57), channel_id=1, source_target_pairs={{0,1},{1,0},{2,3},{3,2},{4,5},{5,4},{6,7},{7,6},{8,9},{9,8},{10,11... | collective-permute-start | bytes 36872 | tf_op jit(solution)/shard_map/ppermute | solution.py:482
  15.6 7.5 %copy-start.14 = (s32[2,8]{1,0:T(2,128)S(1)}, s32[2,8]{1,0:T(2,128)}, u32[]{:S(2)}) copy-start(s32[2,8]{1,0:T(2,128)} %param.28) | copy-start | bytes 196
  15.6 7.5 %copy-start = (f32[26,6,6,128]{3,0,2,1:T(8,128)S(1)}, f32[26,6,6,128]{3,0,2,1:T(8,128)}, u32[]{:S(2)}) copy-start(f32[26,6,6,128]{3,0,2,1:T(8,128)} %param.19) | copy-start | bytes 1437700
  15.6 9.4 %collective-permute-start.3 = (f32[16,192]{1,0:T(8,128)S(1)}, f32[16,192]{1,0:T(8,128)S(1)}, u32[]{:S(2)}, u32[]{:S(2)}) collective-permute-start(f32[16,192]{1,0:T(8,128)S(1)} %get-tuple-element.59), channel_id=1, source_target_pairs={{1,2},{3,4},{5,6},{7,8},{9,10},{11,12},{13,14},{15,16},{17,18},{19... | collective-permute-start | bytes 36872 | tf_op jit(solution)/shard_map/ppermute | solution.py:482
  19.5 3.6 %copy-start.4 = (f32[6,6,128]{2,1,0:T(8,128)S(1)}, f32[6,6,128]{2,1,0:T(8,128)}, u32[]{:S(2)}) copy-start(f32[6,6,128]{2,1,0:T(8,128)} %diag_ref.7) | copy-start | bytes 55300
  19.5 23.3 %all-to-all-start = ((f32[8,32,1024]{2,1,0:T(8,128)}), f32[8,32,1024]{2,1,0:T(8,128)S(1)}, u32[]{:S(2)}, u32[]{:S(2)}) async-start(f32[8,32,1024]{2,1,0:T(8,128)} %get-tuple-element.70), calls=%async_computation | async-start | bytes 2097152 | tf_op jit(solution)/shard_map/all_to_all | solution.py:507
  23.2 1.9 %copy-start.8 = (f32[6,6,128]{2,1,0:T(8,128)S(1)}, f32[6,6,128]{2,1,0:T(8,128)}, u32[]{:S(2)}) copy-start(f32[6,6,128]{2,1,0:T(8,128)} %prolong_ref.7) | copy-start | bytes 55300
  23.2 1.9 %copy-start.10 = (s32[128]{0:T(128)S(1)}, s32[128]{0:T(128)}, u32[]{:S(2)}) copy-start(s32[128]{0:T(128)} %param.23) | copy-start | bytes 1540
  24.9 1.1 copy-start.3
  25.0 1.0 copy-start.15
  25.6 1.3 %collective-permute-start.4 = (f32[32,192]{1,0:T(8,128)S(1)}, f32[32,192]{1,0:T(8,128)S(1)}, u32[]{:S(2)}, u32[]{:S(2)}) collective-permute-start(f32[32,192]{1,0:T(8,128)S(1)} %shard_map.171), channel_id=1, source_target_pairs={{0,1},{1,0},{2,3},{3,2},{4,5},{5,4},{6,7},{7,6},{8,9},{9,8},{10,11... | collective-permute-start | bytes 73736 | tf_op jit(solution)/shard_map/ppermute | solution.py:522
  26.9 3.9 %collective-permute-start.5 = (f32[32,192]{1,0:T(8,128)S(1)}, f32[32,192]{1,0:T(8,128)S(1)}, u32[]{:S(2)}, u32[]{:S(2)}) collective-permute-start(f32[32,192]{1,0:T(8,128)S(1)} %add.99), channel_id=1, source_target_pairs={{0,2},{1,3},{2,0},{3,1},{4,6},{5,7},{6,4},{7,5},{8,10},{9,11},{10,... | collective-permute-start | bytes 73736 | tf_op jit(solution)/shard_map/ppermute | solution.py:522
  30.8 5.4 %collective-permute-start.6 = (f32[32,192]{1,0:T(8,128)S(1)}, f32[32,192]{1,0:T(8,128)S(1)}, u32[]{:S(2)}, u32[]{:S(2)}) collective-permute-start(f32[32,192]{1,0:T(8,128)S(1)} %add.100), channel_id=1, source_target_pairs={{0,4},{1,5},{2,6},{3,7},{4,0},{5,1},{6,2},{7,3},{8,12},{9,13},{10,... | collective-permute-start | bytes 73736 | tf_op jit(solution)/shard_map/ppermute | solution.py:522
  33.3 3.0 %copy-start.9 = (f32[6,6,32]{2,1,0:T(8,128)S(1)}, f32[6,6,32]{2,1,0:T(8,128)}, u32[]{:S(2)}) copy-start(f32[6,6,32]{2,1,0:T(8,128)} %smooth4_ref.1) | copy-start | bytes 13828
  36.3 2.3 %copy-start.7 = (f32[6,6,32]{2,1,0:T(8,128)S(1)}, f32[6,6,32]{2,1,0:T(8,128)}, u32[]{:S(2)}) copy-start(f32[6,6,32]{2,1,0:T(8,128)} %diag_ref.6) | copy-start | bytes 13828
  36.5 5.0 %collective-permute-start.7 = (f32[8,192]{1,0:T(8,128)S(1)}, f32[8,192]{1,0:T(8,128)S(1)}, u32[]{:S(2)}, u32[]{:S(2)}) collective-permute-start(f32[8,192]{1,0:T(8,128)S(1)} %get-tuple-element.64), channel_id=1, source_target_pairs={{0,9},{2,11},{4,13},{6,15},{8,17},{10,19},{12,21},{14,23},{16,25},... | collective-permute-start | bytes 18440 | tf_op jit(solution)/shard_map/ppermute | solution.py:485
  41.6 1.3 %collective-permute-start.8 = (f32[8,192]{1,0:T(8,128)S(1)}, f32[8,192]{1,0:T(8,128)S(1)}, u32[]{:S(2)}, u32[]{:S(2)}) collective-permute-start(f32[8,192]{1,0:T(8,128)S(1)} %collective-permute-done.7.first_in), channel_id=1, source_target_pairs={{0,1},{1,0},{2,3},{3,2},{4,5},{5,4},{6,7},{7,6},{8,9},{9,8},{10,11... | collective-permute-start | bytes 18440 | tf_op jit(solution)/shard_map/ppermute | solution.py:490
  42.1 0.8 copy-start.6
  77.2 12.0 %all-to-all-start.3 = ((f32[8,32,128]{2,1,0:T(8,128)}), f32[8,32,128]{2,1,0:T(8,128)S(1)}, u32[]{:S(2)}, u32[]{:S(2)}) async-start(f32[8,32,128]{2,1,0:T(8,128)} %shard_map.178), calls=%async_computation.3 | async-start | bytes 262144 | tf_op jit(solution)/shard_map/all_to_all | solution.py:541
  89.9 9.4 %all-to-all-start.4 = ((f32[8,32,128]{2,1,0:T(8,128)}), f32[8,32,128]{2,1,0:T(8,128)S(1)}, u32[]{:S(2)}, u32[]{:S(2)}) async-start(f32[8,32,128]{2,1,0:T(8,128)} %shard_map.179), calls=%async_computation.4 | async-start | bytes 262144 | tf_op jit(solution)/shard_map/all_to_all | solution.py:543
  99.8 5.0 %collective-permute-start.9 = (f32[8,192]{1,0:T(8,128)S(1)}, f32[8,192]{1,0:T(8,128)S(1)}, u32[]{:S(2)}, u32[]{:S(2)}) collective-permute-start(f32[8,192]{1,0:T(8,128)S(1)} %get-tuple-element.77), channel_id=1, source_target_pairs={{0,9},{2,11},{4,13},{6,15},{8,17},{10,19},{12,21},{14,23},{16,25},... | collective-permute-start | bytes 18440 | tf_op jit(solution)/shard_map/ppermute | solution.py:485
  104.8 2.6 %collective-permute-start.10 = (f32[8,192]{1,0:T(8,128)S(1)}, f32[8,192]{1,0:T(8,128)S(1)}, u32[]{:S(2)}, u32[]{:S(2)}) collective-permute-start(f32[8,192]{1,0:T(8,128)S(1)} %collective-permute-done.9.first_in), channel_id=1, source_target_pairs={{0,1},{1,0},{2,3},{3,2},{4,5},{5,4},{6,7},{7,6},{8,9},{9,8},{10,11... | collective-permute-start | bytes 18440 | tf_op jit(solution)/shard_map/ppermute | solution.py:490
  108.7 7.4 %collective-permute-start.11 = (f32[16,192]{1,0:T(8,128)S(1)}, f32[16,192]{1,0:T(8,128)S(1)}, u32[]{:S(2)}, u32[]{:S(2)}) collective-permute-start(f32[16,192]{1,0:T(8,128)S(1)} %get-tuple-element.81), channel_id=1, source_target_pairs={{0,1},{1,0},{2,3},{3,2},{4,5},{5,4},{6,7},{7,6},{8,9},{9,8},{10,11... | collective-permute-start | bytes 36872 | tf_op jit(solution)/shard_map/ppermute | solution.py:482
  109.0 9.3 %collective-permute-start.12 = (f32[16,192]{1,0:T(8,128)S(1)}, f32[16,192]{1,0:T(8,128)S(1)}, u32[]{:S(2)}, u32[]{:S(2)}) collective-permute-start(f32[16,192]{1,0:T(8,128)S(1)} %get-tuple-element.82), channel_id=1, source_target_pairs={{1,2},{3,4},{5,6},{7,8},{9,10},{11,12},{13,14},{15,16},{17,18},{19... | collective-permute-start | bytes 36872 | tf_op jit(solution)/shard_map/ppermute | solution.py:482

commit v4 on v3

--- a/solution.py
+++ b/solution.py
@@ -162,12 +162,28 @@
     return pick_rows(row_selector(index_ref[...], vectors[0].shape[1]), flat(vectors))
 
 
-def first_kernel(resid_ref, smooth_ref, index_ref, once_ref, mate_ref, off_ref):
+def first_kernel(
+    resid_in, smooth_in, lists_in, once_ref, mate_ref, off_ref, resid_ref, smooth_ref, lists_ref, sems
+):
+    fetches = [
+        pltpu.make_async_copy(source, target, sems.at[k])
+        for k, (source, target) in enumerate(
+            [(resid_in, resid_ref), (smooth_in, smooth_ref), (lists_in, lists_ref)]
+        )
+    ]
+    for fetch in fetches:
+        fetch.start()
+    for fetch in fetches:
+        fetch.wait()
     once = blockmul(smooth_ref, rows_of(resid_ref))
     put(once_ref, once)
-    sent = send_rows(once, index_ref)
-    mate_ref[...] = sent[:HALO]
-    off_ref[...] = sent[HALO:]
+    x = flat(once)
+    lower, upper = [
+        pick(x, column_selector(ROWS, lists_ref[side : side + 1, :])).T for side in range(2)
+    ]
+    even = lax.axis_index("sub") % 2 == 0
+    mate_ref[...] = jnp.where(even, upper, lower)
+    off_ref[...] = jnp.where(even, lower, upper)
 
 
 def sweep_kernel(
@@ -490,9 +506,20 @@
         return received, lax.ppermute(received, "sub", mates), own
 
     blocks3 = jnp.transpose(off3, (1, 2, 0, 3))
-    once, mate, off = call(
-        first_kernel, [vector, halo, halo], [], cost // 8, resid3, smooth3, index
-    )
+    once, mate, off = pl.pallas_call(
+        first_kernel,
+        in_specs=[pl.BlockSpec(memory_space=pltpu.HBM)] * 3,
+        out_specs=[pl.BlockSpec(memory_space=pltpu.VMEM)] * 3,
+        out_shape=[jax.ShapeDtypeStruct(shape, F32) for shape in (vector, halo, halo)],
+        scratch_shapes=[
+            pltpu.VMEM(resid3.shape, F32),
+            pltpu.VMEM(smooth3.shape, F32),
+            pltpu.VMEM(send3.shape, jnp.int32),
+            pltpu.SemaphoreType.DMA((3,)),
+        ],
+        compiler_params=pltpu.CompilerParams(vmem_limit_bytes=LIMIT),
+        cost_estimate=pl.CostEstimate(flops=1, bytes_accessed=cost // 8, transcendentals=0),
+    )(*[pltpu.with_memory_space_constraint(x, pltpu.HBM) for x in (resid3, smooth3, send3)])
     mate, off = exchange(mate, off)
     own, high, low, packed = window(cost, once, diag3, blocks3, columns, coarse_factor)
     mate, off, high, low, own, packed = lax.optimization_barrier(

time: 120 us -> 121 us (level)
    pallas_call x0 -> x1, Pallas kernels: none -> 1.26 us  [on_device(): pl.pallas_call(first_kernel, in_specs=[pl.BlockSpec(memory_space=pltpu.HB...]
    pallas_call x17 -> x16, Pallas kernels: 13.3 us -> 13.2 us  [call(): pl.pallas_call(body, out_shape=out_shape, in_specs=[pl.BlockSpec(memory_s...]
  transfers between devices with their start and end apart: 16 -> 16, of which waited for: 11 -> 11; matrix products, arithmetic and copies ran while one was open for 0% -> 1% of each run, Pallas kernels for 10% -> 10%
where the time goes in v4:
time: 121 us; the launch traced here: 120 us
  starting transfers between devices  36.5 us (30%)
  blocking collectives  30.6 us (25%)
  waiting for transfers between devices  29.8 us (25%)
  Pallas kernels  19.8 us (16%)
  local copies, waits for them, and re-layouts  1.8 us (1%)
    all_to_all x1, blocking collectives, on_device(): gathered = lax.all_to_all(coarse, 'grp', 0, 0, axis_index_groups=along_z)  18.8 us
    ppermute x6, starting transfers between devices, exchange(): return (lax.ppermute(mate, 'sub', mates), lax.ppermute(off, both, offs))  15.8 us
    pallas_call x16, Pallas kernels, call(): pl.pallas_call(body, out_shape=out_shape, in_specs=[pl.BlockSpec(memory_s...  13.2 us
    all_to_all x1, blocking collectives, on_device(): lax.all_to_all(partial_projected, both, 0, 0, axis_index_groups=along_x_c...  11.8 us
    all_to_all x1, waiting for transfers between devices, on_device(): lax.all_to_all(partial_solved, 'grp', 0, 0, axis_index_groups=along_z)  7.28 us
    ppermute x3, waiting for transfers between devices, on_device(): lax.ppermute(four, 'sub', [(i, i ^ step) for i in range(subs)])  7.22 us
    all_to_all x1, waiting for transfers between devices, on_device(): shares = lax.all_to_all(partial_sums, 'sub', 0, 0)  6.06 us
    pallas_call x1, Pallas kernels, window(): pl.pallas_call(window_kernel, in_specs=[vmem] * 2 + [hbm] * 3, out_specs=...  5.41 us
  transfers between devices with their start and end apart: 16, of which 11 were waited for; matrix products, arithmetic and copies ran while one was open for 1% of the time, Pallas kernels for 10%

profile of v4, /device:TPU:32, one launch (start us, length us, event | category | flops | bytes accessed | tf_op | source)
XLA Modules:
  0.0 119.8 jit_solution(7570345390335700637)
XLA Ops:
  0.6 1.3 %shard_map.167 = (f32[6,32,128]{2,1,0:T(8,128)S(1)}, f32[16,192]{1,0:T(8,128)S(1)}, f32[16,192]{1,0:T(8,128)S(1)}) custom-call(f32[6,32,128]{2,1,0:T(8,128)} %resid_ref.5, f32[6,6,128]{2,1,0:T(8,128)} %smooth_ref.5, s32[2,16]{1,0:T(2,128)} %lists_in.1), custom_call_target="tpu_custom_call" | custom-call | flops 1 | bytes 1048576 | tf_op jit(solution)/shard_map/pallas_call | solution.py:509
  1.9 0.1 collective-permute-start
  2.0 6.7 %collective-permute-start.1 = (f32[16,192]{1,0:T(8,128)S(1)}, f32[16,192]{1,0:T(8,128)S(1)}, u32[]{:S(2)}, u32[]{:S(2)}) collective-permute-start(f32[16,192]{1,0:T(8,128)S(1)} %get-tuple-element.45), channel_id=1, source_target_pairs={{1,2},{3,4},{5,6},{7,8},{9,10},{11,12},{13,14},{15,16},{17,18},{19... | collective-permute-start | bytes 36872 | tf_op jit(solution)/shard_map/ppermute | solution.py:498
  8.8 0.7 copy-done.12
  9.5 5.4 %shard_map.168 = (f32[6,32,128]{2,1,0:T(8,128)S(1)}, bf16[192,768]{1,0:T(8,128)(2,1)S(1)}, bf16[192,768]{1,0:T(8,128)(2,1)S(1)}, f32[8,32,1024]{2,1,0:T(8,128)}) custom-call(f32[6,32,128]{2,1,0:T(8,128)S(1)} %get-tuple-element.43.vector_ref.once_ref, s32[26,1,128]{2,1,0:T(1,128)S(1)} %reshape.163.cols_ref, f32[6,6,128]{2,1,0:T(8,128)} %diag_ref.7, ...), custom_call_target="tpu_custom_call" | custom-call | flops 1 | bytes 16777216 | tf_op jit(solution)/shard_map/pallas_call | solution.py:430
  15.1 0.6 copy-done.4
  15.7 0.6 shard_map.169
  16.5 3.2 %collective-permute-start.3 = (f32[16,192]{1,0:T(8,128)S(1)}, f32[16,192]{1,0:T(8,128)S(1)}, u32[]{:S(2)}, u32[]{:S(2)}) collective-permute-start(f32[16,192]{1,0:T(8,128)S(1)} %get-tuple-element.59), channel_id=1, source_target_pairs={{1,2},{3,4},{5,6},{7,8},{9,10},{11,12},{13,14},{15,16},{17,18},{19... | collective-permute-start | bytes 36872 | tf_op jit(solution)/shard_map/ppermute | solution.py:498
  19.7 3.6 %all-to-all-start = ((f32[8,32,1024]{2,1,0:T(8,128)}), f32[8,32,1024]{2,1,0:T(8,128)S(1)}, u32[]{:S(2)}, u32[]{:S(2)}) async-start(f32[8,32,1024]{2,1,0:T(8,128)} %get-tuple-element.70), calls=%async_computation | async-start | bytes 2097152 | tf_op jit(solution)/shard_map/all_to_all | solution.py:534
  23.3 1.7 %shard_map.170.own_ref = f32[6,32,128]{2,1,0:T(8,128)S(1)} custom-call(f32[6,32,128]{2,1,0:T(8,128)S(1)} %get-tuple-element.55.vector_ref.twice_ref, f32[6,6,128]{2,1,0:T(8,128)S(1)} %copy-done.3, f32[6,6,26,128]{3,2,1,0:T(8,128)S(1)} %bitcast.9, s32[26,1,128]{2,1,0:T(1,128)S(1)} %reshape.163.cols_ref), custom_call_target="tpu_custom_call" | custom-call | flops 1 | bytes 8388608 | tf_op jit(solution)/shard_map/pallas_call | solution.py:30
  25.0 0.8 collective-permute-done.3.off_in
  25.9 0.6 shard_map.171
  26.6 0.2 shard_map.172.blocks_ref
  26.9 0.9 collective-permute-done.4
  27.8 0.2 collective-permute-start.5
  28.0 0.3 shard_map.173
  28.3 3.4 %collective-permute-done.5 = f32[32,192]{1,0:T(8,128)S(1)} collective-permute-done((f32[32,192]{1,0:T(8,128)S(1)}, f32[32,192]{1,0:T(8,128)S(1)}, u32[]{:S(2)}, u32[]{:S(2)}) %collective-permute-start.5) | collective-permute-done | bytes 24608 | tf_op jit(solution)/shard_map/ppermute | solution.py:549
  31.7 2.4 %collective-permute-start.6 = (f32[32,192]{1,0:T(8,128)S(1)}, f32[32,192]{1,0:T(8,128)S(1)}, u32[]{:S(2)}, u32[]{:S(2)}) collective-permute-start(f32[32,192]{1,0:T(8,128)S(1)} %add.100), channel_id=1, source_target_pairs={{0,4},{1,5},{2,6},{3,7},{4,0},{5,1},{6,2},{7,3},{8,12},{9,13},{10,... | collective-permute-start | bytes 73736 | tf_op jit(solution)/shard_map/ppermute | solution.py:549
  34.1 3.0 %collective-permute-done.6 = f32[32,192]{1,0:T(8,128)S(1)} collective-permute-done((f32[32,192]{1,0:T(8,128)S(1)}, f32[32,192]{1,0:T(8,128)S(1)}, u32[]{:S(2)}, u32[]{:S(2)}) %collective-permute-start.6) | collective-permute-done | bytes 24608 | tf_op jit(solution)/shard_map/ppermute | solution.py:549
  37.1 0.2 shard_map.174
  37.4 2.0 %collective-permute-start.7 = (f32[8,192]{1,0:T(8,128)S(1)}, f32[8,192]{1,0:T(8,128)S(1)}, u32[]{:S(2)}, u32[]{:S(2)}) collective-permute-start(f32[8,192]{1,0:T(8,128)S(1)} %get-tuple-element.64), channel_id=1, source_target_pairs={{0,9},{2,11},{4,13},{6,15},{8,17},{10,19},{12,21},{14,23},{16,25},... | collective-permute-start | bytes 18440 | tf_op jit(solution)/shard_map/ppermute | solution.py:501
  39.4 0.7 shard_map.175.own_ref
  40.1 2.3 %collective-permute-done.7.first_in = f32[8,192]{1,0:T(8,128)S(1)} collective-permute-done((f32[8,192]{1,0:T(8,128)S(1)}, f32[8,192]{1,0:T(8,128)S(1)}, u32[]{:S(2)}, u32[]{:S(2)}) %collective-permute-start.7) | collective-permute-done | bytes 6176 | tf_op jit(solution)/shard_map/ppermute | solution.py:501
  42.4 0.3 collective-permute-start.8
  42.8 0.1 select_n.99.place_ref
  42.9 0.7 collective-permute-done.8.second_in
  43.6 0.7 shard_map.176
  44.3 18.8 %all_to_all.25.coarse_ref = f32[8,32,128]{2,1,0:T(8,128)S(1)} all-to-all(f32[8,32,128]{2,1,0:T(8,128)S(1)} %shard_map.176), channel_id=1, replica_groups={{0,32,64,96,128,160,192,224},{8,40,72,104,136,168,200,232},{16,48,80,11..., dimensions={0} | all-to-all | bytes 262144 | tf_op jit(solution)/shard_map/all_to_all | solution.py:559
  63.1 1.1 shard_map.177
  64.2 11.8 %all_to_all.26 = f32[8,32,256]{2,1,0:T(8,128)S(1)} all-to-all(f32[8,32,256]{2,1,0:T(8,128)S(1)} %shard_map.177), channel_id=1, replica_groups={{0,1,8,9,16,17,24,25},{2,3,10,11,18,19,26,27},{4,5,12,13,20,21,28,29},{..., dimensions={0} | all-to-all | bytes 524288 | tf_op jit(solution)/shard_map/all_to_all | solution.py:563
  76.0 1.3 %shard_map.178 = f32[8,32,128]{2,1,0:T(8,128)} custom-call(f32[32,256]{1,0:T(8,128)S(1)} %reduce_sum.18.projected_ref, f32[8,32,1024]{2,1,0:T(8,128)S(1)} %all-to-all-done.factor_ref), custom_call_target="tpu_custom_call" | custom-call | flops 1 | bytes 4194304 | tf_op jit(solution)/shard_map/pallas_call | solution.py:30
  77.3 4.7 %all-to-all-start.3 = ((f32[8,32,128]{2,1,0:T(8,128)}), f32[8,32,128]{2,1,0:T(8,128)S(1)}, u32[]{:S(2)}, u32[]{:S(2)}) async-start(f32[8,32,128]{2,1,0:T(8,128)} %shard_map.178), calls=%async_computation.3 | async-start | bytes 262144 | tf_op jit(solution)/shard_map/all_to_all | solution.py:568
  82.0 7.3 %all-to-all-done.3.shares_ref = f32[8,32,128]{2,1,0:T(8,128)S(1)} async-done(((f32[8,32,128]{2,1,0:T(8,128)}), f32[8,32,128]{2,1,0:T(8,128)S(1)}, u32[]{:S(2)}, u32[]{:S(2)}) %all-to-all-start.3) | async-done | bytes 131104 | tf_op jit(solution)/shard_map/all_to_all | solution.py:568
  89.3 0.7 shard_map.179
  90.0 3.7 %all-to-all-start.4 = ((f32[8,32,128]{2,1,0:T(8,128)}), f32[8,32,128]{2,1,0:T(8,128)S(1)}, u32[]{:S(2)}, u32[]{:S(2)}) async-start(f32[8,32,128]{2,1,0:T(8,128)} %shard_map.179), calls=%async_computation.4 | async-start | bytes 262144 | tf_op jit(solution)/shard_map/all_to_all | solution.py:570
  93.8 6.1 %all-to-all-done.4 = f32[8,32,128]{2,1,0:T(8,128)S(1)} async-done(((f32[8,32,128]{2,1,0:T(8,128)}), f32[8,32,128]{2,1,0:T(8,128)S(1)}, u32[]{:S(2)}, u32[]{:S(2)}) %all-to-all-start.4) | async-done | bytes 131104 | tf_op jit(solution)/shard_map/all_to_all | solution.py:570
  99.8 0.4 shard_map.180
  100.3 2.0 %collective-permute-start.9 = (f32[8,192]{1,0:T(8,128)S(1)}, f32[8,192]{1,0:T(8,128)S(1)}, u32[]{:S(2)}, u32[]{:S(2)}) collective-permute-start(f32[8,192]{1,0:T(8,128)S(1)} %get-tuple-element.77), channel_id=1, source_target_pairs={{0,9},{2,11},{4,13},{6,15},{8,17},{10,19},{12,21},{14,23},{16,25},... | collective-permute-start | bytes 18440 | tf_op jit(solution)/shard_map/ppermute | solution.py:501
  102.3 0.7 shard_map.181.own_ref
  103.0 2.4 %collective-permute-done.9.first_in = f32[8,192]{1,0:T(8,128)S(1)} collective-permute-done((f32[8,192]{1,0:T(8,128)S(1)}, f32[8,192]{1,0:T(8,128)S(1)}, u32[]{:S(2)}, u32[]{:S(2)}) %collective-permute-start.9) | collective-permute-done | bytes 6176 | tf_op jit(solution)/shard_map/ppermute | solution.py:501
  105.3 1.8 %collective-permute-start.10 = (f32[8,192]{1,0:T(8,128)S(1)}, f32[8,192]{1,0:T(8,128)S(1)}, u32[]{:S(2)}, u32[]{:S(2)}) collective-permute-start(f32[8,192]{1,0:T(8,128)S(1)} %collective-permute-done.9.first_in), channel_id=1, source_target_pairs={{0,1},{1,0},{2,3},{3,2},{4,5},{5,4},{6,7},{7,6},{8,9},{9,8},{10,11... | collective-permute-start | bytes 18440 | tf_op jit(solution)/shard_map/ppermute | solution.py:506
  107.1 0.8 collective-permute-done.10.second_in
  107.9 1.3 %shard_map.182 = (f32[6,32,32]{2,1,0:T(8,128)}, f32[6,32,128]{2,1,0:T(8,128)S(1)}, f32[16,192]{1,0:T(8,128)S(1)}, f32[16,192]{1,0:T(8,128)S(1)}) custom-call(f32[6,32,32]{2,1,0:T(8,128)S(1)} %get-tuple-element.63.rhs_ref, f32[6,32,32]{2,1,0:T(8,128)S(1)} %get-tuple-element.76.vector_ref.mid_ref, f32[6,32,32]{2,1,0:T(8,128)S(1)} %shard_map.181.own_ref, ...), custom_call_target="tpu_custom_call" | custom-call | flops 1 | bytes 2097152 | tf_op jit(solution)/shard_map/pallas_call | solution.py:30
  109.2 0.3 collective-permute-start.11
  109.5 5.4 %collective-permute-start.12 = (f32[16,192]{1,0:T(8,128)S(1)}, f32[16,192]{1,0:T(8,128)S(1)}, u32[]{:S(2)}, u32[]{:S(2)}) collective-permute-start(f32[16,192]{1,0:T(8,128)S(1)} %get-tuple-element.82), channel_id=1, source_target_pairs={{1,2},{3,4},{5,6},{7,8},{9,10},{11,12},{13,14},{15,16},{17,18},{19... | collective-permute-start | bytes 36872 | tf_op jit(solution)/shard_map/ppermute | solution.py:498
  114.9 1.7 %shard_map.183.own_ref = f32[6,32,128]{2,1,0:T(8,128)S(1)} custom-call(f32[6,32,128]{2,1,0:T(8,128)S(1)} %get-tuple-element.80.vector_ref.refined_ref, f32[6,6,128]{2,1,0:T(8,128)S(1)} %copy-done.3, f32[6,6,26,128]{3,2,1,0:T(8,128)S(1)} %bitcast.10, s32[26,1,128]{2,1,0:T(1,128)S(1)} %reshape.163.cols_ref), custom_call_target="tpu_custom_call" | custom-call | flops 1 | bytes 8388608 | tf_op jit(solution)/shard_map/pallas_call | solution.py:30
  116.6 2.1 %collective-permute-done.12.off_in = f32[16,192]{1,0:T(8,128)S(1)} collective-permute-done((f32[16,192]{1,0:T(8,128)S(1)}, f32[16,192]{1,0:T(8,128)S(1)}, u32[]{:S(2)}, u32[]{:S(2)}) %collective-permute-start.12) | collective-permute-done | bytes 12320 | tf_op jit(solution)/shard_map/ppermute | solution.py:498
  118.8 1.1 shard_map.184
  (57 shorter events, 0.9 us)
Async XLA Ops:
  1.9 7.6 %copy-start.10 = (s32[26,128]{1,0:T(8,128)S(1)}, s32[26,128]{1,0:T(8,128)}, u32[]{:S(2)}) copy-start(s32[26,128]{1,0:T(8,128)} %param.20) | copy-start | bytes 39940
  1.9 13.2 %collective-permute-start = (f32[16,192]{1,0:T(8,128)S(1)}, f32[16,192]{1,0:T(8,128)S(1)}, u32[]{:S(2)}, u32[]{:S(2)}) collective-permute-start(f32[16,192]{1,0:T(8,128)S(1)} %get-tuple-element.44), channel_id=1, source_target_pairs={{0,1},{1,0},{2,3},{3,2},{4,5},{5,4},{6,7},{7,6},{8,9},{9,8},{10,11... | collective-permute-start | bytes 36872 | tf_op jit(solution)/shard_map/ppermute | solution.py:498
  2.0 13.1 %collective-permute-start.1 = (f32[16,192]{1,0:T(8,128)S(1)}, f32[16,192]{1,0:T(8,128)S(1)}, u32[]{:S(2)}, u32[]{:S(2)}) collective-permute-start(f32[16,192]{1,0:T(8,128)S(1)} %get-tuple-element.45), channel_id=1, source_target_pairs={{1,2},{3,4},{5,6},{7,8},{9,10},{11,12},{13,14},{15,16},{17,18},{19... | collective-permute-start | bytes 36872 | tf_op jit(solution)/shard_map/ppermute | solution.py:498
  8.8 0.7 copy-start.12
  9.5 5.5 %copy-start.1 = (f32[6,32,128]{2,1,0:T(8,128)S(1)}, f32[6,32,128]{2,1,0:T(8,128)}, u32[]{:S(2)}) copy-start(f32[6,32,128]{2,1,0:T(8,128)} %resid_ref.5) | copy-start | bytes 294916
  15.0 0.7 copy-start.4
  15.7 0.7 copy-start.11
  16.3 3.3 %collective-permute-start.2 = (f32[16,192]{1,0:T(8,128)S(1)}, f32[16,192]{1,0:T(8,128)S(1)}, u32[]{:S(2)}, u32[]{:S(2)}) collective-permute-start(f32[16,192]{1,0:T(8,128)S(1)} %get-tuple-element.57), channel_id=1, source_target_pairs={{0,1},{1,0},{2,3},{3,2},{4,5},{5,4},{6,7},{7,6},{8,9},{9,8},{10,11... | collective-permute-start | bytes 36872 | tf_op jit(solution)/shard_map/ppermute | solution.py:498
  16.4 6.8 %copy-start.13 = (s32[2,8]{1,0:T(2,128)S(1)}, s32[2,8]{1,0:T(2,128)}, u32[]{:S(2)}) copy-start(s32[2,8]{1,0:T(2,128)} %param.28) | copy-start | bytes 196
  16.4 6.8 %copy-start = (f32[26,6,6,128]{3,0,2,1:T(8,128)S(1)}, f32[26,6,6,128]{3,0,2,1:T(8,128)}, u32[]{:S(2)}) copy-start(f32[26,6,6,128]{3,0,2,1:T(8,128)} %param.19) | copy-start | bytes 1437700
  16.5 9.4 %collective-permute-start.3 = (f32[16,192]{1,0:T(8,128)S(1)}, f32[16,192]{1,0:T(8,128)S(1)}, u32[]{:S(2)}, u32[]{:S(2)}) collective-permute-start(f32[16,192]{1,0:T(8,128)S(1)} %get-tuple-element.59), channel_id=1, source_target_pairs={{1,2},{3,4},{5,6},{7,8},{9,10},{11,12},{13,14},{15,16},{17,18},{19... | collective-permute-start | bytes 36872 | tf_op jit(solution)/shard_map/ppermute | solution.py:498
  19.6 3.6 %copy-start.3 = (f32[6,6,128]{2,1,0:T(8,128)S(1)}, f32[6,6,128]{2,1,0:T(8,128)}, u32[]{:S(2)}) copy-start(f32[6,6,128]{2,1,0:T(8,128)} %diag_ref.7) | copy-start | bytes 55300
  19.7 23.9 %all-to-all-start = ((f32[8,32,1024]{2,1,0:T(8,128)}), f32[8,32,1024]{2,1,0:T(8,128)S(1)}, u32[]{:S(2)}, u32[]{:S(2)}) async-start(f32[8,32,1024]{2,1,0:T(8,128)} %get-tuple-element.70), calls=%async_computation | async-start | bytes 2097152 | tf_op jit(solution)/shard_map/all_to_all | solution.py:534
  23.3 2.6 %copy-start.7 = (f32[6,6,128]{2,1,0:T(8,128)S(1)}, f32[6,6,128]{2,1,0:T(8,128)}, u32[]{:S(2)}) copy-start(f32[6,6,128]{2,1,0:T(8,128)} %prolong_ref.7) | copy-start | bytes 55300
  23.3 2.6 %copy-start.9 = (s32[128]{0:T(128)S(1)}, s32[128]{0:T(128)}, u32[]{:S(2)}) copy-start(s32[128]{0:T(128)} %param.23) | copy-start | bytes 1540
  25.0 1.6 %copy-start.2 = (f32[26,6,6,32]{3,0,2,1:T(8,128)S(1)}, f32[26,6,6,32]{3,0,2,1:T(8,128)}, u32[]{:S(2)}) copy-start(f32[26,6,6,32]{3,0,2,1:T(8,128)} %param.26) | copy-start | bytes 359428
  25.9 0.7 copy-start.14
  26.5 1.3 %collective-permute-start.4 = (f32[32,192]{1,0:T(8,128)S(1)}, f32[32,192]{1,0:T(8,128)S(1)}, u32[]{:S(2)}, u32[]{:S(2)}) collective-permute-start(f32[32,192]{1,0:T(8,128)S(1)} %shard_map.171), channel_id=1, source_target_pairs={{0,1},{1,0},{2,3},{3,2},{4,5},{5,4},{6,7},{7,6},{8,9},{9,8},{10,11... | collective-permute-start | bytes 73736 | tf_op jit(solution)/shard_map/ppermute | solution.py:549
  27.8 3.9 %collective-permute-start.5 = (f32[32,192]{1,0:T(8,128)S(1)}, f32[32,192]{1,0:T(8,128)S(1)}, u32[]{:S(2)}, u32[]{:S(2)}) collective-permute-start(f32[32,192]{1,0:T(8,128)S(1)} %add.99), channel_id=1, source_target_pairs={{0,2},{1,3},{2,0},{3,1},{4,6},{5,7},{6,4},{7,5},{8,10},{9,11},{10,... | collective-permute-start | bytes 73736 | tf_op jit(solution)/shard_map/ppermute | solution.py:549
  31.7 5.4 %collective-permute-start.6 = (f32[32,192]{1,0:T(8,128)S(1)}, f32[32,192]{1,0:T(8,128)S(1)}, u32[]{:S(2)}, u32[]{:S(2)}) collective-permute-start(f32[32,192]{1,0:T(8,128)S(1)} %add.100), channel_id=1, source_target_pairs={{0,4},{1,5},{2,6},{3,7},{4,0},{5,1},{6,2},{7,3},{8,12},{9,13},{10,... | collective-permute-start | bytes 73736 | tf_op jit(solution)/shard_map/ppermute | solution.py:549
  34.1 3.0 %copy-start.8 = (f32[6,6,32]{2,1,0:T(8,128)S(1)}, f32[6,6,32]{2,1,0:T(8,128)}, u32[]{:S(2)}) copy-start(f32[6,6,32]{2,1,0:T(8,128)} %smooth4_ref.1) | copy-start | bytes 13828
  37.1 2.3 %copy-start.6 = (f32[6,6,32]{2,1,0:T(8,128)S(1)}, f32[6,6,32]{2,1,0:T(8,128)}, u32[]{:S(2)}) copy-start(f32[6,6,32]{2,1,0:T(8,128)} %diag_ref.6) | copy-start | bytes 13828
  37.4 5.0 %collective-permute-start.7 = (f32[8,192]{1,0:T(8,128)S(1)}, f32[8,192]{1,0:T(8,128)S(1)}, u32[]{:S(2)}, u32[]{:S(2)}) collective-permute-start(f32[8,192]{1,0:T(8,128)S(1)} %get-tuple-element.64), channel_id=1, source_target_pairs={{0,9},{2,11},{4,13},{6,15},{8,17},{10,19},{12,21},{14,23},{16,25},... | collective-permute-start | bytes 18440 | tf_op jit(solution)/shard_map/ppermute | solution.py:501
  42.4 1.2 collective-permute-start.8
  42.8 0.8 copy-start.5
  77.3 12.0 %all-to-all-start.3 = ((f32[8,32,128]{2,1,0:T(8,128)}), f32[8,32,128]{2,1,0:T(8,128)S(1)}, u32[]{:S(2)}, u32[]{:S(2)}) async-start(f32[8,32,128]{2,1,0:T(8,128)} %shard_map.178), calls=%async_computation.3 | async-start | bytes 262144 | tf_op jit(solution)/shard_map/all_to_all | solution.py:568
  90.0 9.8 %all-to-all-start.4 = ((f32[8,32,128]{2,1,0:T(8,128)}), f32[8,32,128]{2,1,0:T(8,128)S(1)}, u32[]{:S(2)}, u32[]{:S(2)}) async-start(f32[8,32,128]{2,1,0:T(8,128)} %shard_map.179), calls=%async_computation.4 | async-start | bytes 262144 | tf_op jit(solution)/shard_map/all_to_all | solution.py:570
  100.3 5.0 %collective-permute-start.9 = (f32[8,192]{1,0:T(8,128)S(1)}, f32[8,192]{1,0:T(8,128)S(1)}, u32[]{:S(2)}, u32[]{:S(2)}) collective-permute-start(f32[8,192]{1,0:T(8,128)S(1)} %get-tuple-element.77), channel_id=1, source_target_pairs={{0,9},{2,11},{4,13},{6,15},{8,17},{10,19},{12,21},{14,23},{16,25},... | collective-permute-start | bytes 18440 | tf_op jit(solution)/shard_map/ppermute | solution.py:501
  105.3 2.6 %collective-permute-start.10 = (f32[8,192]{1,0:T(8,128)S(1)}, f32[8,192]{1,0:T(8,128)S(1)}, u32[]{:S(2)}, u32[]{:S(2)}) collective-permute-start(f32[8,192]{1,0:T(8,128)S(1)} %collective-permute-done.9.first_in), channel_id=1, source_target_pairs={{0,1},{1,0},{2,3},{3,2},{4,5},{5,4},{6,7},{7,6},{8,9},{9,8},{10,11... | collective-permute-start | bytes 18440 | tf_op jit(solution)/shard_map/ppermute | solution.py:506
  109.2 7.5 %collective-permute-start.11 = (f32[16,192]{1,0:T(8,128)S(1)}, f32[16,192]{1,0:T(8,128)S(1)}, u32[]{:S(2)}, u32[]{:S(2)}) collective-permute-start(f32[16,192]{1,0:T(8,128)S(1)} %get-tuple-element.81), channel_id=1, source_target_pairs={{0,1},{1,0},{2,3},{3,2},{4,5},{5,4},{6,7},{7,6},{8,9},{9,8},{10,11... | collective-permute-start | bytes 36872 | tf_op jit(solution)/shard_map/ppermute | solution.py:498
  109.5 9.3 %collective-permute-start.12 = (f32[16,192]{1,0:T(8,128)S(1)}, f32[16,192]{1,0:T(8,128)S(1)}, u32[]{:S(2)}, u32[]{:S(2)}) collective-permute-start(f32[16,192]{1,0:T(8,128)S(1)} %get-tuple-element.82), channel_id=1, source_target_pairs={{1,2},{3,4},{5,6},{7,8},{9,10},{11,12},{13,14},{15,16},{17,18},{19... | collective-permute-start | bytes 36872 | tf_op jit(solution)/shard_map/ppermute | solution.py:498

commit v5 on v3

--- a/solution.py
+++ b/solution.py
@@ -9,7 +9,6 @@
 BF16 = jnp.bfloat16
 LIMIT = 16 * 1024 * 1024
 NT = (((1,), (1,)), ((), ()))
-HIGHEST = lax.Precision.HIGHEST
 
 ROWS = 128
 R = 32
@@ -293,22 +292,29 @@
         out_ref[copy] = total
 
 
+def factor_parts(factor_ref):
+    rows = factor_ref[...].reshape(-1, factor_ref.shape[2])
+    high = rows.astype(BF16)
+    return high, (rows - high.astype(F32)).astype(BF16)
+
+
 def project_kernel(coarse_ref, factor_ref, out_ref):
-    rows = factor_ref[...].reshape(-1, factor_ref.shape[2])
-    total = None
-    for z in range(coarse_ref.shape[0]):
-        columns = rows[:, z * LANES5 : (z + 1) * LANES5]
-        term = lax.dot_general(
-            coarse_ref[z], columns, NT, precision=HIGHEST, preferred_element_type=F32
-        )
-        total = term if total is None else total + term
+    coarse = jnp.concatenate([coarse_ref[z] for z in range(coarse_ref.shape[0])], axis=1)
+    parts = jnp.concatenate(split(coarse), axis=0)
+    high, low = factor_parts(factor_ref)
+    out = lax.dot_general(parts, high, NT, preferred_element_type=F32)
+    out = out + lax.dot_general(parts, low, NT, preferred_element_type=F32)
+    total = out[:R] + out[R : 2 * R] + out[2 * R :]
     for copy in range(out_ref.shape[0]):
         out_ref[copy] = total
 
 
 def solve_kernel(projected_ref, factor_ref, out_ref):
-    rows = factor_ref[...].reshape(-1, factor_ref.shape[2])
-    solved = jnp.dot(projected_ref[...], rows, precision=HIGHEST, preferred_element_type=F32)
+    parts = jnp.concatenate(split(projected_ref[...]), axis=0)
+    high, low = factor_parts(factor_ref)
+    out = jnp.dot(parts, high, preferred_element_type=F32)
+    out = out + jnp.dot(parts, low, preferred_element_type=F32)
+    solved = out[:R] + out[R : 2 * R] + out[2 * R :]
     for z in range(out_ref.shape[0]):
         out_ref[z] = solved[:, z * LANES5 : (z + 1) * LANES5]
 

time: 120 us -> 119 us (level)
  no operation moved by 1% of the time
where the time goes in v5:
time: 119 us; the launch traced here: 118 us
  starting transfers between devices  37.4 us (31%)
  blocking collectives  31.2 us (26%)
  waiting for transfers between devices  28.6 us (24%)
  Pallas kernels  17.8 us (15%)
  local copies, waits for them, and re-layouts  2.04 us (2%)
    all_to_all x1, blocking collectives, on_device(): gathered = lax.all_to_all(coarse, 'grp', 0, 0, axis_index_groups=along_z)  18.9 us
    ppermute x6, starting transfers between devices, exchange(): return (lax.ppermute(mate, 'sub', mates), lax.ppermute(off, both, offs))  16.5 us
    pallas_call x17, Pallas kernels, call(): pl.pallas_call(body, out_shape=out_shape, in_specs=[pl.BlockSpec(memory_s...  12.4 us
    all_to_all x1, blocking collectives, on_device(): lax.all_to_all(partial_projected, both, 0, 0, axis_index_groups=along_x_c...  12.3 us
    all_to_all x1, waiting for transfers between devices, on_device(): lax.all_to_all(partial_solved, 'grp', 0, 0, axis_index_groups=along_z)  7.28 us
    ppermute x3, waiting for transfers between devices, on_device(): lax.ppermute(four, 'sub', [(i, i ^ step) for i in range(subs)])  6.92 us
    all_to_all x1, waiting for transfers between devices, on_device(): shares = lax.all_to_all(partial_sums, 'sub', 0, 0)  5.98 us
    pallas_call x1, Pallas kernels, window(): pl.pallas_call(window_kernel, in_specs=[vmem] * 2 + [hbm] * 3, out_specs=...  5.41 us
  transfers between devices with their start and end apart: 16, of which 11 were waited for; matrix products, arithmetic and copies ran while one was open for 0% of the time, Pallas kernels for 10%

profile of v5, /device:TPU:32, one launch (start us, length us, event | category | flops | bytes accessed | tf_op | source)
XLA Modules:
  0.0 118.4 jit_solution(15529375186645322246)
XLA Ops:
  0.7 0.6 copy-done.13
  1.5 0.9 copy-done.1
  2.3 0.2 shard_map.167
  2.6 6.8 %collective-permute-start.1 = (f32[16,192]{1,0:T(8,128)S(1)}, f32[16,192]{1,0:T(8,128)S(1)}, u32[]{:S(2)}, u32[]{:S(2)}) collective-permute-start(f32[16,192]{1,0:T(8,128)S(1)} %get-tuple-element.45), channel_id=1, source_target_pairs={{1,2},{3,4},{5,6},{7,8},{9,10},{11,12},{13,14},{15,16},{17,18},{19... | collective-permute-start | bytes 36872 | tf_op jit(solution)/shard_map/ppermute | solution.py:488
  9.4 5.4 %shard_map.168 = (f32[6,32,128]{2,1,0:T(8,128)S(1)}, bf16[192,768]{1,0:T(8,128)(2,1)S(1)}, bf16[192,768]{1,0:T(8,128)(2,1)S(1)}, f32[8,32,1024]{2,1,0:T(8,128)}) custom-call(f32[6,32,128]{2,1,0:T(8,128)S(1)} %get-tuple-element.43.vector_ref.once_ref, s32[26,1,128]{2,1,0:T(1,128)S(1)} %reshape.164.cols_ref, f32[6,6,128]{2,1,0:T(8,128)} %diag_ref.7, ...), custom_call_target="tpu_custom_call" | custom-call | flops 1 | bytes 16777216 | tf_op jit(solution)/shard_map/pallas_call | solution.py:420
  14.9 0.6 shard_map.169
  15.6 3.9 %collective-permute-start.3 = (f32[16,192]{1,0:T(8,128)S(1)}, f32[16,192]{1,0:T(8,128)S(1)}, u32[]{:S(2)}, u32[]{:S(2)}) collective-permute-start(f32[16,192]{1,0:T(8,128)S(1)} %get-tuple-element.59), channel_id=1, source_target_pairs={{1,2},{3,4},{5,6},{7,8},{9,10},{11,12},{13,14},{15,16},{17,18},{19... | collective-permute-start | bytes 36872 | tf_op jit(solution)/shard_map/ppermute | solution.py:488
  19.5 3.6 %all-to-all-start = ((f32[8,32,1024]{2,1,0:T(8,128)}), f32[8,32,1024]{2,1,0:T(8,128)S(1)}, u32[]{:S(2)}, u32[]{:S(2)}) async-start(f32[8,32,1024]{2,1,0:T(8,128)} %get-tuple-element.70), calls=%async_computation | async-start | bytes 2097152 | tf_op jit(solution)/shard_map/all_to_all | solution.py:513
  23.2 1.7 %shard_map.170.own_ref = f32[6,32,128]{2,1,0:T(8,128)S(1)} custom-call(f32[6,32,128]{2,1,0:T(8,128)S(1)} %get-tuple-element.55.vector_ref.twice_ref, f32[6,6,128]{2,1,0:T(8,128)S(1)} %copy-done.4, f32[6,6,26,128]{3,2,1,0:T(8,128)S(1)} %bitcast.9, s32[26,1,128]{2,1,0:T(1,128)S(1)} %reshape.164.cols_ref), custom_call_target="tpu_custom_call" | custom-call | flops 1 | bytes 8388608 | tf_op jit(solution)/shard_map/pallas_call | solution.py:29
  24.9 0.1 collective-permute-done.3.off_in
  25.0 0.6 shard_map.171
  25.6 0.4 collective-permute-start.4
  26.0 0.2 shard_map.172.blocks_ref
  26.3 0.6 collective-permute-done.4
  26.9 0.2 collective-permute-start.5
  27.2 0.3 shard_map.173
  27.5 3.3 %collective-permute-done.5 = f32[32,192]{1,0:T(8,128)S(1)} collective-permute-done((f32[32,192]{1,0:T(8,128)S(1)}, f32[32,192]{1,0:T(8,128)S(1)}, u32[]{:S(2)}, u32[]{:S(2)}) %collective-permute-start.5) | collective-permute-done | bytes 24608 | tf_op jit(solution)/shard_map/ppermute | solution.py:528
  30.8 2.4 %collective-permute-start.6 = (f32[32,192]{1,0:T(8,128)S(1)}, f32[32,192]{1,0:T(8,128)S(1)}, u32[]{:S(2)}, u32[]{:S(2)}) collective-permute-start(f32[32,192]{1,0:T(8,128)S(1)} %add.100), channel_id=1, source_target_pairs={{0,4},{1,5},{2,6},{3,7},{4,0},{5,1},{6,2},{7,3},{8,12},{9,13},{10,... | collective-permute-start | bytes 73736 | tf_op jit(solution)/shard_map/ppermute | solution.py:528
  33.3 3.0 %collective-permute-done.6 = f32[32,192]{1,0:T(8,128)S(1)} collective-permute-done((f32[32,192]{1,0:T(8,128)S(1)}, f32[32,192]{1,0:T(8,128)S(1)}, u32[]{:S(2)}, u32[]{:S(2)}) %collective-permute-start.6) | collective-permute-done | bytes 24608 | tf_op jit(solution)/shard_map/ppermute | solution.py:528
  36.3 0.2 shard_map.174
  36.5 2.0 %collective-permute-start.7 = (f32[8,192]{1,0:T(8,128)S(1)}, f32[8,192]{1,0:T(8,128)S(1)}, u32[]{:S(2)}, u32[]{:S(2)}) collective-permute-start(f32[8,192]{1,0:T(8,128)S(1)} %get-tuple-element.64), channel_id=1, source_target_pairs={{0,9},{2,11},{4,13},{6,15},{8,17},{10,19},{12,21},{14,23},{16,25},... | collective-permute-start | bytes 18440 | tf_op jit(solution)/shard_map/ppermute | solution.py:491
  38.6 0.7 shard_map.175.own_ref
  39.2 2.3 %collective-permute-done.7.first_in = f32[8,192]{1,0:T(8,128)S(1)} collective-permute-done((f32[8,192]{1,0:T(8,128)S(1)}, f32[8,192]{1,0:T(8,128)S(1)}, u32[]{:S(2)}, u32[]{:S(2)}) %collective-permute-start.7) | collective-permute-done | bytes 6176 | tf_op jit(solution)/shard_map/ppermute | solution.py:491
  41.6 0.4 collective-permute-start.8
  42.1 0.1 select_n.99.place_ref
  42.2 0.6 collective-permute-done.8.second_in
  42.8 0.7 shard_map.176
  43.5 18.9 %all_to_all.25.coarse_ref = f32[8,32,128]{2,1,0:T(8,128)S(1)} all-to-all(f32[8,32,128]{2,1,0:T(8,128)S(1)} %shard_map.176), channel_id=1, replica_groups={{0,32,64,96,128,160,192,224},{8,40,72,104,136,168,200,232},{16,48,80,11..., dimensions={0} | all-to-all | bytes 262144 | tf_op jit(solution)/shard_map/all_to_all | solution.py:538
  62.4 0.5 shard_map.177
  62.9 12.3 %all_to_all.26 = f32[8,32,256]{2,1,0:T(8,128)S(1)} all-to-all(f32[8,32,256]{2,1,0:T(8,128)S(1)} %shard_map.177), channel_id=1, replica_groups={{0,1,8,9,16,17,24,25},{2,3,10,11,18,19,26,27},{4,5,12,13,20,21,28,29},{..., dimensions={0} | all-to-all | bytes 524288 | tf_op jit(solution)/shard_map/all_to_all | solution.py:542
  75.2 1.0 shard_map.178
  76.2 4.7 %all-to-all-start.3 = ((f32[8,32,128]{2,1,0:T(8,128)}), f32[8,32,128]{2,1,0:T(8,128)S(1)}, u32[]{:S(2)}, u32[]{:S(2)}) async-start(f32[8,32,128]{2,1,0:T(8,128)} %shard_map.178), calls=%async_computation.3 | async-start | bytes 262144 | tf_op jit(solution)/shard_map/all_to_all | solution.py:547
  81.0 7.3 %all-to-all-done.3.shares_ref = f32[8,32,128]{2,1,0:T(8,128)S(1)} async-done(((f32[8,32,128]{2,1,0:T(8,128)}), f32[8,32,128]{2,1,0:T(8,128)S(1)}, u32[]{:S(2)}, u32[]{:S(2)}) %all-to-all-start.3) | async-done | bytes 131104 | tf_op jit(solution)/shard_map/all_to_all | solution.py:547
  88.2 0.7 shard_map.179
  88.9 3.4 %all-to-all-start.4 = ((f32[8,32,128]{2,1,0:T(8,128)}), f32[8,32,128]{2,1,0:T(8,128)S(1)}, u32[]{:S(2)}, u32[]{:S(2)}) async-start(f32[8,32,128]{2,1,0:T(8,128)} %shard_map.179), calls=%async_computation.4 | async-start | bytes 262144 | tf_op jit(solution)/shard_map/all_to_all | solution.py:549
  92.4 6.0 %all-to-all-done.4 = f32[8,32,128]{2,1,0:T(8,128)S(1)} async-done(((f32[8,32,128]{2,1,0:T(8,128)}), f32[8,32,128]{2,1,0:T(8,128)S(1)}, u32[]{:S(2)}, u32[]{:S(2)}) %all-to-all-start.4) | async-done | bytes 131104 | tf_op jit(solution)/shard_map/all_to_all | solution.py:549
  98.4 0.4 shard_map.180
  98.8 2.0 %collective-permute-start.9 = (f32[8,192]{1,0:T(8,128)S(1)}, f32[8,192]{1,0:T(8,128)S(1)}, u32[]{:S(2)}, u32[]{:S(2)}) collective-permute-start(f32[8,192]{1,0:T(8,128)S(1)} %get-tuple-element.77), channel_id=1, source_target_pairs={{0,9},{2,11},{4,13},{6,15},{8,17},{10,19},{12,21},{14,23},{16,25},... | collective-permute-start | bytes 18440 | tf_op jit(solution)/shard_map/ppermute | solution.py:491
  100.8 0.7 shard_map.181.own_ref
  101.5 2.4 %collective-permute-done.9.first_in = f32[8,192]{1,0:T(8,128)S(1)} collective-permute-done((f32[8,192]{1,0:T(8,128)S(1)}, f32[8,192]{1,0:T(8,128)S(1)}, u32[]{:S(2)}, u32[]{:S(2)}) %collective-permute-start.9) | collective-permute-done | bytes 6176 | tf_op jit(solution)/shard_map/ppermute | solution.py:491
  103.8 1.8 %collective-permute-start.10 = (f32[8,192]{1,0:T(8,128)S(1)}, f32[8,192]{1,0:T(8,128)S(1)}, u32[]{:S(2)}, u32[]{:S(2)}) collective-permute-start(f32[8,192]{1,0:T(8,128)S(1)} %collective-permute-done.9.first_in), channel_id=1, source_target_pairs={{0,1},{1,0},{2,3},{3,2},{4,5},{5,4},{6,7},{7,6},{8,9},{9,8},{10,11... | collective-permute-start | bytes 18440 | tf_op jit(solution)/shard_map/ppermute | solution.py:496
  105.6 0.8 collective-permute-done.10.second_in
  106.4 1.3 %shard_map.182 = (f32[6,32,32]{2,1,0:T(8,128)}, f32[6,32,128]{2,1,0:T(8,128)S(1)}, f32[16,192]{1,0:T(8,128)S(1)}, f32[16,192]{1,0:T(8,128)S(1)}) custom-call(f32[6,32,32]{2,1,0:T(8,128)S(1)} %get-tuple-element.63.rhs_ref, f32[6,32,32]{2,1,0:T(8,128)S(1)} %get-tuple-element.76.vector_ref.mid_ref, f32[6,32,32]{2,1,0:T(8,128)S(1)} %shard_map.181.own_ref, ...), custom_call_target="tpu_custom_call" | custom-call | flops 1 | bytes 2097152 | tf_op jit(solution)/shard_map/pallas_call | solution.py:29
  107.7 0.3 collective-permute-start.11
  108.1 5.4 %collective-permute-start.12 = (f32[16,192]{1,0:T(8,128)S(1)}, f32[16,192]{1,0:T(8,128)S(1)}, u32[]{:S(2)}, u32[]{:S(2)}) collective-permute-start(f32[16,192]{1,0:T(8,128)S(1)} %get-tuple-element.82), channel_id=1, source_target_pairs={{1,2},{3,4},{5,6},{7,8},{9,10},{11,12},{13,14},{15,16},{17,18},{19... | collective-permute-start | bytes 36872 | tf_op jit(solution)/shard_map/ppermute | solution.py:488
  113.4 1.7 %shard_map.183.own_ref = f32[6,32,128]{2,1,0:T(8,128)S(1)} custom-call(f32[6,32,128]{2,1,0:T(8,128)S(1)} %get-tuple-element.80.vector_ref.refined_ref, f32[6,6,128]{2,1,0:T(8,128)S(1)} %copy-done.4, f32[6,6,26,128]{3,2,1,0:T(8,128)S(1)} %bitcast.10, s32[26,1,128]{2,1,0:T(1,128)S(1)} %reshape.164.cols_ref), custom_call_target="tpu_custom_call" | custom-call | flops 1 | bytes 8388608 | tf_op jit(solution)/shard_map/pallas_call | solution.py:29
  115.2 2.2 %collective-permute-done.12.off_in = f32[16,192]{1,0:T(8,128)S(1)} collective-permute-done((f32[16,192]{1,0:T(8,128)S(1)}, f32[16,192]{1,0:T(8,128)S(1)}, u32[]{:S(2)}, u32[]{:S(2)}) %collective-permute-start.12) | collective-permute-done | bytes 12320 | tf_op jit(solution)/shard_map/ppermute | solution.py:488
  117.3 1.1 shard_map.184
  (59 shorter events, 0.9 us)
Async XLA Ops:
  0.6 0.7 copy-start.13
  0.6 0.8 copy-start.5
  1.4 0.9 copy-start.1
  2.3 7.0 %copy-start.11 = (s32[26,128]{1,0:T(8,128)S(1)}, s32[26,128]{1,0:T(8,128)}, u32[]{:S(2)}) copy-start(s32[26,128]{1,0:T(8,128)} %param.20) | copy-start | bytes 39940
  2.5 12.3 %collective-permute-start = (f32[16,192]{1,0:T(8,128)S(1)}, f32[16,192]{1,0:T(8,128)S(1)}, u32[]{:S(2)}, u32[]{:S(2)}) collective-permute-start(f32[16,192]{1,0:T(8,128)S(1)} %get-tuple-element.44), channel_id=1, source_target_pairs={{0,1},{1,0},{2,3},{3,2},{4,5},{5,4},{6,7},{7,6},{8,9},{9,8},{10,11... | collective-permute-start | bytes 36872 | tf_op jit(solution)/shard_map/ppermute | solution.py:488
  2.6 12.2 %collective-permute-start.1 = (f32[16,192]{1,0:T(8,128)S(1)}, f32[16,192]{1,0:T(8,128)S(1)}, u32[]{:S(2)}, u32[]{:S(2)}) collective-permute-start(f32[16,192]{1,0:T(8,128)S(1)} %get-tuple-element.45), channel_id=1, source_target_pairs={{1,2},{3,4},{5,6},{7,8},{9,10},{11,12},{13,14},{15,16},{17,18},{19... | collective-permute-start | bytes 36872 | tf_op jit(solution)/shard_map/ppermute | solution.py:488
  9.4 5.5 %copy-start.2 = (f32[6,32,128]{2,1,0:T(8,128)S(1)}, f32[6,32,128]{2,1,0:T(8,128)}, u32[]{:S(2)}) copy-start(f32[6,32,128]{2,1,0:T(8,128)} %resid_ref.7) | copy-start | bytes 294916
  14.9 0.7 copy-start.12
  15.5 4.1 %collective-permute-start.2 = (f32[16,192]{1,0:T(8,128)S(1)}, f32[16,192]{1,0:T(8,128)S(1)}, u32[]{:S(2)}, u32[]{:S(2)}) collective-permute-start(f32[16,192]{1,0:T(8,128)S(1)} %get-tuple-element.57), channel_id=1, source_target_pairs={{0,1},{1,0},{2,3},{3,2},{4,5},{5,4},{6,7},{7,6},{8,9},{9,8},{10,11... | collective-permute-start | bytes 36872 | tf_op jit(solution)/shard_map/ppermute | solution.py:488
  15.6 7.5 %copy-start.14 = (s32[2,8]{1,0:T(2,128)S(1)}, s32[2,8]{1,0:T(2,128)}, u32[]{:S(2)}) copy-start(s32[2,8]{1,0:T(2,128)} %param.28) | copy-start | bytes 196
  15.6 7.5 %copy-start = (f32[26,6,6,128]{3,0,2,1:T(8,128)S(1)}, f32[26,6,6,128]{3,0,2,1:T(8,128)}, u32[]{:S(2)}) copy-start(f32[26,6,6,128]{3,0,2,1:T(8,128)} %param.19) | copy-start | bytes 1437700
  15.6 9.4 %collective-permute-start.3 = (f32[16,192]{1,0:T(8,128)S(1)}, f32[16,192]{1,0:T(8,128)S(1)}, u32[]{:S(2)}, u32[]{:S(2)}) collective-permute-start(f32[16,192]{1,0:T(8,128)S(1)} %get-tuple-element.59), channel_id=1, source_target_pairs={{1,2},{3,4},{5,6},{7,8},{9,10},{11,12},{13,14},{15,16},{17,18},{19... | collective-permute-start | bytes 36872 | tf_op jit(solution)/shard_map/ppermute | solution.py:488
  19.5 3.6 %copy-start.4 = (f32[6,6,128]{2,1,0:T(8,128)S(1)}, f32[6,6,128]{2,1,0:T(8,128)}, u32[]{:S(2)}) copy-start(f32[6,6,128]{2,1,0:T(8,128)} %diag_ref.7) | copy-start | bytes 55300
  19.5 23.3 %all-to-all-start = ((f32[8,32,1024]{2,1,0:T(8,128)}), f32[8,32,1024]{2,1,0:T(8,128)S(1)}, u32[]{:S(2)}, u32[]{:S(2)}) async-start(f32[8,32,1024]{2,1,0:T(8,128)} %get-tuple-element.70), calls=%async_computation | async-start | bytes 2097152 | tf_op jit(solution)/shard_map/all_to_all | solution.py:513
  23.2 1.9 %copy-start.8 = (f32[6,6,128]{2,1,0:T(8,128)S(1)}, f32[6,6,128]{2,1,0:T(8,128)}, u32[]{:S(2)}) copy-start(f32[6,6,128]{2,1,0:T(8,128)} %prolong_ref.7) | copy-start | bytes 55300
  23.2 1.9 %copy-start.10 = (s32[128]{0:T(128)S(1)}, s32[128]{0:T(128)}, u32[]{:S(2)}) copy-start(s32[128]{0:T(128)} %param.23) | copy-start | bytes 1540
  24.9 1.1 copy-start.3
  25.0 1.0 copy-start.15
  25.6 1.3 %collective-permute-start.4 = (f32[32,192]{1,0:T(8,128)S(1)}, f32[32,192]{1,0:T(8,128)S(1)}, u32[]{:S(2)}, u32[]{:S(2)}) collective-permute-start(f32[32,192]{1,0:T(8,128)S(1)} %shard_map.171), channel_id=1, source_target_pairs={{0,1},{1,0},{2,3},{3,2},{4,5},{5,4},{6,7},{7,6},{8,9},{9,8},{10,11... | collective-permute-start | bytes 73736 | tf_op jit(solution)/shard_map/ppermute | solution.py:528
  26.9 3.9 %collective-permute-start.5 = (f32[32,192]{1,0:T(8,128)S(1)}, f32[32,192]{1,0:T(8,128)S(1)}, u32[]{:S(2)}, u32[]{:S(2)}) collective-permute-start(f32[32,192]{1,0:T(8,128)S(1)} %add.99), channel_id=1, source_target_pairs={{0,2},{1,3},{2,0},{3,1},{4,6},{5,7},{6,4},{7,5},{8,10},{9,11},{10,... | collective-permute-start | bytes 73736 | tf_op jit(solution)/shard_map/ppermute | solution.py:528
  30.8 5.4 %collective-permute-start.6 = (f32[32,192]{1,0:T(8,128)S(1)}, f32[32,192]{1,0:T(8,128)S(1)}, u32[]{:S(2)}, u32[]{:S(2)}) collective-permute-start(f32[32,192]{1,0:T(8,128)S(1)} %add.100), channel_id=1, source_target_pairs={{0,4},{1,5},{2,6},{3,7},{4,0},{5,1},{6,2},{7,3},{8,12},{9,13},{10,... | collective-permute-start | bytes 73736 | tf_op jit(solution)/shard_map/ppermute | solution.py:528
  33.3 3.0 %copy-start.9 = (f32[6,6,32]{2,1,0:T(8,128)S(1)}, f32[6,6,32]{2,1,0:T(8,128)}, u32[]{:S(2)}) copy-start(f32[6,6,32]{2,1,0:T(8,128)} %smooth4_ref.1) | copy-start | bytes 13828
  36.3 2.3 %copy-start.7 = (f32[6,6,32]{2,1,0:T(8,128)S(1)}, f32[6,6,32]{2,1,0:T(8,128)}, u32[]{:S(2)}) copy-start(f32[6,6,32]{2,1,0:T(8,128)} %diag_ref.6) | copy-start | bytes 13828
  36.5 5.0 %collective-permute-start.7 = (f32[8,192]{1,0:T(8,128)S(1)}, f32[8,192]{1,0:T(8,128)S(1)}, u32[]{:S(2)}, u32[]{:S(2)}) collective-permute-start(f32[8,192]{1,0:T(8,128)S(1)} %get-tuple-element.64), channel_id=1, source_target_pairs={{0,9},{2,11},{4,13},{6,15},{8,17},{10,19},{12,21},{14,23},{16,25},... | collective-permute-start | bytes 18440 | tf_op jit(solution)/shard_map/ppermute | solution.py:491
  41.6 1.3 %collective-permute-start.8 = (f32[8,192]{1,0:T(8,128)S(1)}, f32[8,192]{1,0:T(8,128)S(1)}, u32[]{:S(2)}, u32[]{:S(2)}) collective-permute-start(f32[8,192]{1,0:T(8,128)S(1)} %collective-permute-done.7.first_in), channel_id=1, source_target_pairs={{0,1},{1,0},{2,3},{3,2},{4,5},{5,4},{6,7},{7,6},{8,9},{9,8},{10,11... | collective-permute-start | bytes 18440 | tf_op jit(solution)/shard_map/ppermute | solution.py:496
  42.1 0.8 copy-start.6
  76.2 12.0 %all-to-all-start.3 = ((f32[8,32,128]{2,1,0:T(8,128)}), f32[8,32,128]{2,1,0:T(8,128)S(1)}, u32[]{:S(2)}, u32[]{:S(2)}) async-start(f32[8,32,128]{2,1,0:T(8,128)} %shard_map.178), calls=%async_computation.3 | async-start | bytes 262144 | tf_op jit(solution)/shard_map/all_to_all | solution.py:547
  88.9 9.4 %all-to-all-start.4 = ((f32[8,32,128]{2,1,0:T(8,128)}), f32[8,32,128]{2,1,0:T(8,128)S(1)}, u32[]{:S(2)}, u32[]{:S(2)}) async-start(f32[8,32,128]{2,1,0:T(8,128)} %shard_map.179), calls=%async_computation.4 | async-start | bytes 262144 | tf_op jit(solution)/shard_map/all_to_all | solution.py:549
  98.8 5.0 %collective-permute-start.9 = (f32[8,192]{1,0:T(8,128)S(1)}, f32[8,192]{1,0:T(8,128)S(1)}, u32[]{:S(2)}, u32[]{:S(2)}) collective-permute-start(f32[8,192]{1,0:T(8,128)S(1)} %get-tuple-element.77), channel_id=1, source_target_pairs={{0,9},{2,11},{4,13},{6,15},{8,17},{10,19},{12,21},{14,23},{16,25},... | collective-permute-start | bytes 18440 | tf_op jit(solution)/shard_map/ppermute | solution.py:491
  103.8 2.6 %collective-permute-start.10 = (f32[8,192]{1,0:T(8,128)S(1)}, f32[8,192]{1,0:T(8,128)S(1)}, u32[]{:S(2)}, u32[]{:S(2)}) collective-permute-start(f32[8,192]{1,0:T(8,128)S(1)} %collective-permute-done.9.first_in), channel_id=1, source_target_pairs={{0,1},{1,0},{2,3},{3,2},{4,5},{5,4},{6,7},{7,6},{8,9},{9,8},{10,11... | collective-permute-start | bytes 18440 | tf_op jit(solution)/shard_map/ppermute | solution.py:496
  107.7 7.4 %collective-permute-start.11 = (f32[16,192]{1,0:T(8,128)S(1)}, f32[16,192]{1,0:T(8,128)S(1)}, u32[]{:S(2)}, u32[]{:S(2)}) collective-permute-start(f32[16,192]{1,0:T(8,128)S(1)} %get-tuple-element.81), channel_id=1, source_target_pairs={{0,1},{1,0},{2,3},{3,2},{4,5},{5,4},{6,7},{7,6},{8,9},{9,8},{10,11... | collective-permute-start | bytes 36872 | tf_op jit(solution)/shard_map/ppermute | solution.py:488
  108.1 9.3 %collective-permute-start.12 = (f32[16,192]{1,0:T(8,128)S(1)}, f32[16,192]{1,0:T(8,128)S(1)}, u32[]{:S(2)}, u32[]{:S(2)}) collective-permute-start(f32[16,192]{1,0:T(8,128)S(1)} %get-tuple-element.82), channel_id=1, source_target_pairs={{1,2},{3,4},{5,6},{7,8},{9,10},{11,12},{13,14},{15,16},{17,18},{19... | collective-permute-start | bytes 36872 | tf_op jit(solution)/shard_map/ppermute | solution.py:488
